TPU v7x, 128 devices: a whole 4x4x4 slice. The times are simulated.
128 devices in a mesh: fsdp: 16 (over y, x_lo, core), ctx: 8 (over z, x_hi).
Axes of the slice: x: 4 (x_hi: 2, x_lo: 2; x = x_hi * 2 + x_lo), y: 4, z: 4, core: 2. Of those that a mesh axis runs over, the one named last changes fastest.
Arguments:
- tokens: bfloat16 [16384, 768], P(('fsdp', 'ctx')), may hold values from -24 to 24
- w_qkv: bfloat16 [768, 2304], P('fsdp'), may hold values from -0.21875 to 0.21875
- w_out: bfloat16 [768, 768], P('fsdp'), may hold values from -1.75 to 1.75
- w_up: bfloat16 [768, 3072], P('fsdp'), may hold values from -0.21875 to 0.21875
- w_down: bfloat16 [3072, 768], P('fsdp'), may hold values from -0.109375 to 0.109375
- vectors: bfloat16 [8, 768], P(None, 'fsdp'), may hold values from -0.9 to 1.75
- b_up: bfloat16 [3072], P('fsdp'), may hold values from -3 to 3
- lengths: int32 [16, 3], P('fsdp'), may hold values from 1 to 512, as said below
- block_seq: int32 [16, 8], P('fsdp'), may hold values from 0 to 2, as said below
- out_grad: bfloat16 [16384, 768], P(('fsdp', 'ctx')), may hold values from -6 to 6
Outputs:
- layer_out: bfloat16 [16384, 768], P(('fsdp', 'ctx'))
- tokens_grad: float32 [16384, 768], P(('fsdp', 'ctx'))
- qkv_grad: float32 [768, 2304], P('fsdp')
- out_proj_grad: float32 [768, 768], P('fsdp')
- up_grad: float32 [768, 3072], P('fsdp')
- down_grad: float32 [3072, 768], P('fsdp')
- vectors_grad: float32 [8, 768], P(None, 'fsdp')
- up_bias_grad: float32 [3072], P('fsdp')
Inputs may be any that keep to these rules, and one draw needn't show every extreme that they name: In each group one sequence has exactly 512 tokens; sequence s of group g fills ceil(lengths[g, s] / 128) block slots. `block_seq`: every sequence of a group holds one block slot or more.
All inputs are finite; a program needn't handle non-finite values.
Results may differ from a plain program's by a relative error of at most 0.025.
Values may be sent and summed in bfloat16 or wider, within the bound.
No kernel may reach another device: no remote copies, remote signals or barrier semaphores. Data moves between devices by JAX's collectives and lax.ppermute only.
A program may use at most 128 MiB of HBM per device.

v0:
```python
import jax
import jax.numpy as jnp
from jax import lax
from jax.sharding import PartitionSpec as P

D = 768
HEADS = 12
HD = 64
BLK = 128
SPAN = 1024
NBLK = 8
SEQS = 3


epsilon = 1e-12
masked_fill = -1e30
root_half = 0.7071067811865476
inv_root_tau = 0.3989422804014327


def plain_dot(left_side, right_side):
    return jnp.dot(left_side, right_side, preferred_element_type=jnp.float32)


def left_dot(left_side, right_side):
    return lax.dot_general(
        left_side, right_side, (((0,), (0,)), ((), ())), preferred_element_type=jnp.float32
    )


def right_dot(left_side, right_side):
    return lax.dot_general(
        left_side, right_side, (((1,), (1,)), ((), ())), preferred_element_type=jnp.float32
    )


def slot_tables(length_row, seq_row):
    slot_index = jnp.arange(NBLK, dtype=jnp.int32)
    same_seq = seq_row[:, None] == seq_row[None, :]
    earlier = slot_index[None, :] < slot_index[:, None]
    block_rank = jnp.sum((same_seq & earlier).astype(jnp.int32), axis=1)
    owner_len = jnp.sum(
        jnp.where(
            seq_row[:, None] == jnp.arange(SEQS, dtype=jnp.int32)[None, :], length_row[None, :], 0
        ),
        axis=1,
    )
    block_fill = jnp.clip(owner_len - BLK * block_rank, 0, BLK)
    slot_seq = jnp.repeat(seq_row, BLK, total_repeat_length=SPAN)
    slot_fill = jnp.repeat(block_fill, BLK, total_repeat_length=SPAN)
    slot_valid = jnp.arange(SPAN, dtype=jnp.int32) % BLK < slot_fill
    return (slot_seq, slot_valid)


def norm_stats(hidden, norm_gain, norm_shift):
    centre = hidden - jnp.mean(hidden, axis=-1, keepdims=True)
    inverse = lax.rsqrt(jnp.mean(centre * centre, axis=-1, keepdims=True) + epsilon)
    normed_hat = centre * inverse
    return (normed_hat * norm_gain + norm_shift, normed_hat, inverse)


def norm_back(grad_out, norm_gain, normed_hat, inverse):
    scaled = grad_out * norm_gain
    return inverse * (
        scaled
        - jnp.mean(scaled, axis=-1, keepdims=True)
        - normed_hat * jnp.mean(scaled * normed_hat, axis=-1, keepdims=True)
    )


def split_heads(block):
    return block.reshape(block.shape[0], HEADS, HD).transpose(1, 0, 2)


def join_heads(block):
    return block.transpose(1, 0, 2).reshape(block.shape[1], HEADS * HD)


def head_scores(query_h, key_h, key_mask):
    scores = right_dot(query_h, key_h) * HD ** (-0.5)
    return jnp.where(key_mask, scores, masked_fill)


def body(tokens, w_qkv, w_out, w_up, w_down, vectors, b_up, lengths, block_seq, out_grad):
    row_count = tokens.shape[0]
    score_scale = HD ** (-0.5)
    slot_seq, slot_valid = slot_tables(lengths[0], block_seq[0])
    own_seq = lax.dynamic_slice_in_dim(slot_seq, lax.axis_index("ctx") * row_count, row_count)
    key_mask = (own_seq[:, None] == slot_seq[None, :]) & slot_valid[None, :]
    gathered = (
        lax.all_gather(w_qkv, "fsdp", axis=0, tiled=True),
        lax.all_gather(w_out, "fsdp", axis=0, tiled=True),
        lax.all_gather(w_up, "fsdp", axis=0, tiled=True),
        lax.all_gather(w_down, "fsdp", axis=0, tiled=True),
        lax.all_gather(vectors, "fsdp", axis=1, tiled=True),
        lax.all_gather(b_up, "fsdp", axis=0, tiled=True),
    )
    full_qkv, full_out, full_up, full_down = (gathered[0], gathered[1], gathered[2], gathered[3])
    vector_rows = gathered[4].astype(jnp.float32)
    up_bias = gathered[5].astype(jnp.float32)
    bias_qkv = jnp.concatenate([vector_rows[0], jnp.zeros_like(vector_rows[0]), vector_rows[1]])
    projected = (plain_dot(tokens, full_qkv) + bias_qkv).astype(jnp.bfloat16)
    keys_values = lax.all_gather(projected[:, D:], "ctx", axis=0, tiled=True)
    head_query = split_heads(projected[:, :D])
    head_key = split_heads(keys_values[:, :D])
    head_value = split_heads(keys_values[:, D:])

    def head_forward(member):
        scores = head_scores(member[0], member[1], key_mask)
        row_peak = jnp.max(scores, axis=-1, keepdims=True)
        log_total = row_peak + jnp.log(jnp.sum(jnp.exp(scores - row_peak), axis=-1, keepdims=True))
        chances = jnp.exp(scores - log_total)
        return (plain_dot(chances.astype(jnp.bfloat16), member[2]), log_total)

    head_out, log_totals = lax.map(head_forward, (head_query, head_key, head_value))
    mixture = join_heads(head_out).astype(jnp.bfloat16)
    attended = plain_dot(mixture, full_out) + vector_rows[2]
    first_norm, first_hat, first_inv = norm_stats(
        tokens.astype(jnp.float32) + attended, vector_rows[4], vector_rows[5]
    )
    first_low = first_norm.astype(jnp.bfloat16)
    up_proj = plain_dot(first_low, full_up) + up_bias
    up_erf = jax.scipy.special.erf(up_proj * root_half)
    activ_low = (0.5 * up_proj * (1.0 + up_erf)).astype(jnp.bfloat16)
    second_sum = first_norm + plain_dot(activ_low, full_down) + vector_rows[3]
    out_norm, second_hat, second_inv = norm_stats(second_sum, vector_rows[6], vector_rows[7])
    layer_out = out_norm.astype(jnp.bfloat16)
    regathered = (
        lax.all_gather(w_qkv, "fsdp", axis=0, tiled=True),
        lax.all_gather(w_out, "fsdp", axis=0, tiled=True),
        lax.all_gather(w_up, "fsdp", axis=0, tiled=True),
        lax.all_gather(w_down, "fsdp", axis=0, tiled=True),
        lax.all_gather(vectors, "fsdp", axis=1, tiled=True),
        lax.all_gather(b_up, "fsdp", axis=0, tiled=True),
    )
    full_qkv, full_out, full_up, full_down = (
        regathered[0],
        regathered[1],
        regathered[2],
        regathered[3],
    )
    out_cot = out_grad.astype(jnp.float32)
    second_cot = norm_back(out_cot, vector_rows[6], second_hat, second_inv)
    down_cot = second_cot.astype(jnp.bfloat16)
    down_grad = left_dot(activ_low, down_cot)
    up_slope = 0.5 * (1.0 + up_erf) + up_proj * jnp.exp(-0.5 * up_proj * up_proj) * inv_root_tau
    up_cot = (right_dot(down_cot, full_down) * up_slope).astype(jnp.bfloat16)
    up_grad = left_dot(first_low, up_cot)
    first_cot = second_cot + right_dot(up_cot, full_up)
    input_cot = norm_back(first_cot, vector_rows[4], first_hat, first_inv)
    attend_cot = input_cot.astype(jnp.bfloat16)
    out_proj_grad = left_dot(mixture, attend_cot)
    mixture_flat = right_dot(attend_cot, full_out).astype(jnp.bfloat16)
    mixture_cot = split_heads(mixture_flat)

    def head_backward(member):
        query_h, key_h, value_h, cot_h, log_total = member
        chances = jnp.exp(head_scores(query_h, key_h, key_mask) - log_total)
        chance_cot = right_dot(cot_h, value_h)
        score_cot = (
            chances * (chance_cot - jnp.sum(chances * chance_cot, axis=-1, keepdims=True))
        ).astype(jnp.bfloat16)
        return (
            plain_dot(score_cot, key_h) * score_scale,
            left_dot(score_cot, query_h) * score_scale,
            left_dot(chances.astype(jnp.bfloat16), cot_h),
        )

    query_cot, key_cot, value_cot = lax.map(
        head_backward, (head_query, head_key, head_value, mixture_cot, log_totals)
    )
    key_sum, value_sum = (
        lax.psum_scatter(
            join_heads(key_cot).astype(jnp.bfloat16), "ctx", scatter_dimension=0, tiled=True
        ).astype(jnp.float32),
        lax.psum_scatter(
            join_heads(value_cot).astype(jnp.bfloat16), "ctx", scatter_dimension=0, tiled=True
        ).astype(jnp.float32),
    )
    projected_cot = jnp.concatenate(
        [
            join_heads(query_cot).astype(jnp.bfloat16),
            key_sum.astype(jnp.bfloat16),
            value_sum.astype(jnp.bfloat16),
        ],
        axis=1,
    )
    qkv_grad = left_dot(tokens, projected_cot)
    tokens_grad = input_cot + right_dot(projected_cot, full_qkv)
    column_sums = jnp.sum(projected_cot.astype(jnp.float32), axis=0)
    vector_grad = jnp.stack(
        [
            column_sums[:D],
            column_sums[2 * D :],
            jnp.sum(attend_cot.astype(jnp.float32), axis=0),
            jnp.sum(down_cot.astype(jnp.float32), axis=0),
            jnp.sum(first_cot * first_hat, axis=0),
            jnp.sum(first_cot, axis=0),
            jnp.sum(out_cot * second_hat, axis=0),
            jnp.sum(out_cot, axis=0),
        ]
    )
    up_bias_grad = jnp.sum(up_cot.astype(jnp.float32), axis=0)
    pieces = (
        lax.psum_scatter(
            qkv_grad.astype(jnp.bfloat16), "fsdp", scatter_dimension=0, tiled=True
        ).astype(jnp.float32),
        lax.psum_scatter(
            out_proj_grad.astype(jnp.bfloat16), "fsdp", scatter_dimension=0, tiled=True
        ).astype(jnp.float32),
        lax.psum_scatter(
            up_grad.astype(jnp.bfloat16), "fsdp", scatter_dimension=0, tiled=True
        ).astype(jnp.float32),
        lax.psum_scatter(
            down_grad.astype(jnp.bfloat16), "fsdp", scatter_dimension=0, tiled=True
        ).astype(jnp.float32),
        lax.psum_scatter(
            vector_grad.astype(jnp.bfloat16), "fsdp", scatter_dimension=1, tiled=True
        ).astype(jnp.float32),
        lax.psum_scatter(
            up_bias_grad.astype(jnp.bfloat16), "fsdp", scatter_dimension=0, tiled=True
        ).astype(jnp.float32),
    )
    owned = (
        lax.psum(pieces[0].astype(jnp.bfloat16), "ctx").astype(jnp.float32),
        lax.psum(pieces[1].astype(jnp.bfloat16), "ctx").astype(jnp.float32),
        lax.psum(pieces[2].astype(jnp.bfloat16), "ctx").astype(jnp.float32),
        lax.psum(pieces[3].astype(jnp.bfloat16), "ctx").astype(jnp.float32),
        lax.psum(pieces[4].astype(jnp.bfloat16), "ctx").astype(jnp.float32),
        lax.psum(pieces[5].astype(jnp.bfloat16), "ctx").astype(jnp.float32),
    )
    return (layer_out, tokens_grad, owned[0], owned[1], owned[2], owned[3], owned[4], owned[5])


def solution(mesh):
    in_specs = (
        P(("fsdp", "ctx"), None),
        P("fsdp", None),
        P("fsdp", None),
        P("fsdp", None),
        P("fsdp", None),
        P(None, "fsdp"),
        P("fsdp"),
        P("fsdp", None),
        P("fsdp", None),
        P(("fsdp", "ctx"), None),
    )
    out_specs = (
        P(("fsdp", "ctx"), None),
        P(("fsdp", "ctx"), None),
        P("fsdp", None),
        P("fsdp", None),
        P("fsdp", None),
        P("fsdp", None),
        P(None, "fsdp"),
        P("fsdp"),
    )
    return jax.shard_map(body, mesh=mesh, in_specs=in_specs, out_specs=out_specs, check_vma=False)
```

profile of v0, /device:TPU:0, one launch (start us, length us, event | category | flops | bytes accessed | tf_op | source)
XLA Modules:
  0.0 931.4 jit_solution(14360061080526676157)
XLA Ops:
  7.9 20.3 %all-gather = bf16[16,48,8]{1,2,0:T(8,128)(2,1)S(1)} all-gather(bf16[1,48,8]{1,2,0:T(8,128)(2,1)} %bitcast.243), channel_id=1, replica_groups=mesh['fsdp'=16,'ctx'=8] {'fsdp'}, dimensions={0}, use_global_device_ids=true | all-gather | bytes 13056 | tf_op jit(solution)/shard_map/all_gather | solution.py:95
  29.0 19.7 %all-gather.7.cloned.1.call-done = bf16[768,2304]{1,0:T(8,128)(2,1)} async-done(((bf16[48,2304]{1,0:T(8,128)(2,1)}), bf16[768,2304]{1,0:T(8,128)(2,1)}) %all-gather.7.cloned.1.call-update) | async-done | bytes 3538960 | tf_op jit(solution)/shard_map/all_gather | solution.py:91
  48.7 2.8 fusion.47
  57.5 29.6 %all-reduce = bf16[3072]{0:T(1024)(128)(2,1)S(1)} all-reduce(bf16[3072]{0:T(1024)(128)(2,1)S(1)} %dynamic-update-slice.4), channel_id=1, replica_groups=mesh['fsdp'=16,'ctx'=8] {'fsdp'}, use_global_device_ids=true, to_apply=%add | all-reduce | flops 3072 | bytes 12288
  87.7 5.1 select_select_fusion
  93.5 5.6 fusion.62
  100.1 15.5 %all-gather.9.cloned.1.call-done = bf16[1024,1536]{1,0:T(8,128)(2,1)} async-done(((bf16[128,1536]{1,0:T(8,128)(2,1)}), bf16[1024,1536]{1,0:T(8,128)(2,1)}) %all-gather.9.cloned.1.call-update) | async-done | bytes 3145744 | tf_op jit(solution)/shard_map/all_gather | solution.py:103
  115.6 2.1 fusion.86
  117.7 1.6 copy.51
  119.4 4.1 copy.54
  123.5 1.6 copy.52
  125.1 3.1 copy.55
  128.2 28.5 %while.30 = (s32[]{:T(128)}, bf16[12,128,64]{1,2,0:T(8,128)(2,1)S(1)}, f32[12,128,1]{1,2,0:T(1,128)}, bf16[12,128,64]{2,1,0:T(8,128)(2,1)}, bf16[12,1024,64]{2,1...) while((s32[]{:T(128)}, ...), condition=%wide.region_5.7_spmd.clone, body=%wide.region_2.0_spmd.clone.sunk | while | flops 34733952 | bytes 2175077 | solution.py:115
  156.8 1.6 copy-done.1
  158.4 1.7 fusion.91
  160.3 27.5 %all-gather.13.cloned.1.call-done = bf16[768,3072]{1,0:T(8,128)(2,1)} async-done(((bf16[48,3072]{1,0:T(8,128)(2,1)}), bf16[768,3072]{1,0:T(8,128)(2,1)}) %all-gather.13.cloned.1.call-update) | async-done | bytes 4718608 | tf_op jit(solution)/shard_map/all_gather | solution.py:93
  187.8 3.2 convolution_add_fusion.1
  191.1 37.2 %all-gather.15.cloned.1.call-done = bf16[3072,768]{1,0:T(8,128)(2,1)} async-done(((bf16[192,768]{1,0:T(8,128)(2,1)}), bf16[3072,768]{1,0:T(8,128)(2,1)}) %all-gather.15.cloned.1.call-update) | async-done | bytes 4718608 | tf_op jit(solution)/shard_map/all_gather | solution.py:94
  228.3 3.5 fusion.92
  232.0 1.5 fusion.60
  234.3 2.3 fusion.93
  236.6 2.4 multiply_reduce_fusion.1
  239.0 1.5 convert_reduce_fusion.1
  241.3 84.4 %while.31 = (s32[]{:T(128)}, bf16[12,128,64]{1,2,0:T(8,128)(2,1)S(1)}, bf16[12,1024,64]{1,2,0:T(8,128)(2,1)}, bf16[12,1024,64]{1,2,0:T(8,128)(2,1)}, bf16[12,128...) while((s32[]{:T(128)}, ...), condition=%wide.region_16.18_spmd.clone, body=%wide.region_14.17_spmd.clone.sunk | while | flops 85401472 | bytes 5387393 | solution.py:169
  243.2 1.4 multiply_reduce_fusion.7
  244.6 1.6 fusion.140
  250.2 1.4 multiply_reduce_fusion.7
  251.7 1.6 fusion.140
  257.2 1.4 multiply_reduce_fusion.7
  258.7 1.6 fusion.140
  264.2 1.4 multiply_reduce_fusion.7
  265.7 1.6 fusion.140
  272.8 1.6 fusion.140
  278.3 1.4 multiply_reduce_fusion.7
  279.8 1.6 fusion.140
  286.8 1.6 fusion.140
  293.9 1.6 fusion.140
  300.9 1.6 fusion.140
  307.9 1.6 fusion.140
  314.9 1.6 fusion.140
  322.0 1.6 fusion.140
  325.7 2.7 copy.62
  328.6 2.6 copy.64
  331.3 70.6 %reduce-scatter.22.cloned.1.call-done = bf16[128,768]{1,0:T(8,128)(2,1)} async-done(((bf16[1024,768]{1,0:T(8,128)(2,1)}), bf16[128,768]{1,0:T(8,128)(2,1)}) %reduce-scatter.22.cloned.1.call-update) | async-done | bytes 196624
  402.9 75.1 %reduce-scatter.24.cloned.1.call-done = bf16[128,768]{1,0:T(8,128)(2,1)} async-done(((bf16[1024,768]{1,0:T(8,128)(2,1)}), bf16[128,768]{1,0:T(8,128)(2,1)}) %reduce-scatter.24.cloned.1.call-update) | async-done | bytes 196624
  479.1 2.8 fusion.45
  481.9 5.8 copy.66
  487.8 2.5 convolution_convert_fusion.3
  490.4 3.6 convolution_convert_fusion.1
  494.1 3.6 convolution_convert_fusion
  498.6 1.5 stack.40
  503.1 1.4 fusion.81
  507.4 47.0 %reduce-scatter.26.cloned.1.call-done = bf16[48,2304]{1,0:T(8,128)(2,1)} async-done(((bf16[768,2304]{1,0:T(8,128)(2,1)}), bf16[48,2304]{1,0:T(8,128)(2,1)}) %reduce-scatter.26.cloned.1.call-update) | async-done | bytes 221200
  554.4 2.0 copy.67
  556.4 61.4 %reduce-scatter.16.cloned.1.call-done = bf16[48,768]{1,0:T(8,128)(2,1)} async-done(((bf16[768,768]{1,0:T(8,128)(2,1)}), bf16[48,768]{1,0:T(8,128)(2,1)}) %reduce-scatter.16.cloned.1.call-update) | async-done | bytes 73744 | tf_op jit(solution)/shard_map/reduce_scatter | solution.py:208
  617.7 71.4 %reduce-scatter.18.cloned.1.call-done = bf16[48,3072]{1,0:T(8,128)(2,1)} async-done(((bf16[768,3072]{1,0:T(8,128)(2,1)}), bf16[48,3072]{1,0:T(8,128)(2,1)}) %reduce-scatter.18.cloned.1.call-update) | async-done | bytes 294928 | tf_op jit(solution)/shard_map/reduce_scatter | solution.py:211
  689.2 72.4 %reduce-scatter.20.cloned.1.call-done = bf16[192,768]{1,0:T(8,128)(2,1)} async-done(((bf16[3072,768]{1,0:T(8,128)(2,1)}), bf16[192,768]{1,0:T(8,128)(2,1)}) %reduce-scatter.20.cloned.1.call-update) | async-done | bytes 294928 | tf_op jit(solution)/shard_map/reduce_scatter | solution.py:214
  762.2 29.4 %all-reduce.1 = bf16[3072]{0:T(1024)(128)(2,1)S(1)} all-reduce(bf16[3072]{0:T(1024)(128)(2,1)S(1)} %copy-done.26), channel_id=9, replica_groups=mesh['fsdp'=16,'ctx'=8] {'fsdp'}, use_global_device_ids=true, to_apply=%region_37.39.clone | all-reduce | flops 3072 | bytes 12288
  791.8 3.3 convolution_add_fusion.3
  795.1 28.1 %reduce-scatter.28.cloned.1.call-done = bf16[48,8]{1,0:T(8,128)(2,1)} async-done(((bf16[768,8]{1,0:T(8,128)(2,1)}), bf16[48,8]{1,0:T(8,128)(2,1)}) %reduce-scatter.28.cloned.1.call-update) | async-done | bytes 784
  823.9 23.9 %all-reduce.2 = (bf16[8,48]{1,0:T(8,128)(2,1)S(1)}, bf16[192]{0:T(256)(128)(2,1)S(1)}) all-reduce(bf16[8,48]{1,0:T(8,128)(2,1)S(1)} %copy.69, bf16[192]{0:T(256)(128)(2,1)S(1)} %dynamic-slice.11), channel_id=1, replica_groups=mesh['fsdp'=16,'ctx'=8] {'ctx'}, use_global_device_ids=true, to_apply=%region_35.37 | all-reduce | flops 576 | bytes 2304 | tf_op jit(solution)/shard_map/psum | solution.py:229
  849.0 70.5 %all-reduce.6.cloned.1.call-done = (bf16[48,2304]{0,1:T(8,128)(2,1)}, bf16[48,768]{1,0:T(8,128)(2,1)}, bf16[48,3072]{1,0:T(8,128)(2,1)}, bf16[192,768]{1,0:T(8,128)(2,1)}) async-done(((bf16[48,2304]{0,1:T(8,128)(2,1)}, bf16[48,768]{1,0:T(8,128)(2,1)}, bf16[48,3072]{1,0:T(8,128)(2,1)}, bf16[192,768]{1,0:T(8,128)(2,1)}), (bf16[48,2304]{0,1:T(8,128)(2,1)}, bf16[48,768]{1,0:T(8,128)(2,1)}, ...) | async-done | bytes 884752 | tf_op jit(solution)/shard_map/psum | solution.py:225
  919.5 1.9 convert_element_type.176
  921.4 1.8 convert_element_type.178
  (265 shorter events, 110.0 us)
Async XLA Ops:
  7.2 41.6 %all-gather.7.cloned.1.call-start = ((), (), s32[]{:S(2)}) async-start(), calls=%async_computation.7 | async-start | bytes 3760128 | tf_op jit(solution)/shard_map/all_gather | solution.py:91
  7.9 107.7 %all-gather.9.cloned.1.call-start = ((), (), s32[]{:S(2)}) async-start(), calls=%async_computation.8 | async-start | bytes 3538944 | tf_op jit(solution)/shard_map/all_gather | solution.py:103
  51.5 2.8 copy-start.16
  51.5 3.7 copy-start.28
  51.5 4.4 copy-start.27
  51.6 5.7 copy-start.29
  52.4 104.4 %all-gather.11.cloned.1.call-start = ((), (), s32[]{:S(2)}) async-start(), calls=%async_computation.9 | async-start | bytes 1253376 | tf_op jit(solution)/shard_map/all_gather | solution.py:92
  53.1 134.7 %all-gather.13.cloned.1.call-start = ((), (), s32[]{:S(2)}) async-start(), calls=%async_computation.10 | async-start | bytes 5013504 | tf_op jit(solution)/shard_map/all_gather | solution.py:93
  53.7 174.6 %all-gather.15.cloned.1.call-start = ((), (), s32[]{:S(2)}) async-start(), calls=%async_computation.11 | async-start | bytes 5013504 | tf_op jit(solution)/shard_map/all_gather | solution.py:94
  54.3 347.6 %reduce-scatter.22.cloned.1.call-start = ((), (), s32[]{:S(2)}) async-start(), calls=%async_computation.15 | async-start | bytes 1769472
  128.2 30.1 %copy-start.9 = (bf16[128,768]{1,0:T(8,128)(2,1)S(1)}, bf16[128,768]{1,0:T(8,128)(2,1)}, u32[]{:S(2)}) copy-start(bf16[128,768]{1,0:T(8,128)(2,1)} %param.20) | copy-start | bytes 589828
  156.7 1.6 copy-start.1
  156.7 34.3 %copy-start.10 = (bf16[12,128,64]{1,2,0:T(8,128)(2,1)}, bf16[12,128,64]{1,2,0:T(8,128)(2,1)S(1)}, u32[]{:S(2)}) copy-start(bf16[12,128,64]{1,2,0:T(8,128)(2,1)S(1)} %get-tuple-element.121) | copy-start | bytes 589828
  158.4 29.5 %copy-start.14 = (f32[3072]{0:T(1024)S(1)}, f32[3072]{0:T(1024)}, u32[]{:S(2)}) copy-start(f32[3072]{0:T(1024)} %convert_element_type.153) | copy-start | bytes 36868
  160.1 76.5 %copy-start.17 = (f32[128]{0:T(128)}, f32[128]{0:T(128)S(1)}, u32[]{:S(2)}) copy-start(f32[128]{0:T(128)S(1)} %broadcast_multiply_fusion.5) | copy-start | bytes 1540
  160.3 76.3 %copy-start.19 = (f32[128]{0:T(128)}, f32[128]{0:T(128)S(1)}, u32[]{:S(2)}) copy-start(f32[128]{0:T(128)S(1)} %add_rsqrt_fusion.1) | copy-start | bytes 1540
  187.8 40.4 %copy-start.22 = (f32[768]{0:T(1024)S(1)}, f32[768]{0:T(1024)}, u32[]{:S(2)}) copy-start(f32[768]{0:T(1024)} %get-tuple-element.282) | copy-start | bytes 9220
  228.3 6.0 slice-start.2
  228.3 3.7 copy-start.11
  228.3 3.7 copy-start.21
  228.3 6.0 slice-start.3
  233.5 3.2 slice-start
  234.3 2.3 slice-start.1
  236.6 2.4 copy-start.7
  239.0 1.5 copy-start.3
  239.0 2.3 copy-start.15
  240.5 247.3 %copy-start.2 = (f32[128,768]{1,0:T(8,128)}, f32[128,768]{1,0:T(8,128)S(1)}, u32[]{:S(2)}) copy-start(f32[128,768]{1,0:T(8,128)S(1)} %get-tuple-element.341) | copy-start | bytes 1179652
  325.7 153.4 %copy-start.6 = (bf16[12,128,64]{1,2,0:T(8,128)(2,1)}, bf16[12,128,64]{1,2,0:T(8,128)(2,1)S(1)}, u32[]{:S(2)}) copy-start(bf16[12,128,64]{1,2,0:T(8,128)(2,1)S(1)} %get-tuple-element.123) | copy-start | bytes 589828
  328.4 149.6 %reduce-scatter.24.cloned.1.call-start = ((), (), s32[]{:S(2)}) async-start(), calls=%async_computation.16 | async-start | bytes 1769472
  331.2 223.1 %reduce-scatter.26.cloned.1.call-start = ((), (), s32[]{:S(2)}) async-start(), calls=%async_computation.17 | async-start | bytes 3760128
  402.9 79.0 %copy-start.4 = (bf16[128,768]{0,1:T(8,128)(2,1)}, bf16[128,768]{0,1:T(8,128)(2,1)S(1)}, u32[]{:S(2)}) copy-start(bf16[128,768]{0,1:T(8,128)(2,1)S(1)} %copy.63) | copy-start | bytes 589828
  479.1 2.8 copy-start.5
  487.7 2.6 copy-start.8
  487.8 2.6 copy-start.18
  487.8 2.6 copy-start.20
  487.8 130.0 %reduce-scatter.16.cloned.1.call-start = ((), (), s32[]{:S(2)}) async-start(), calls=%async_computation.12 | async-start | bytes 1253376 | tf_op jit(solution)/shard_map/reduce_scatter | solution.py:208
  490.3 198.8 %reduce-scatter.18.cloned.1.call-start = ((), (), s32[]{:S(2)}) async-start(), calls=%async_computation.13 | async-start | bytes 5013504 | tf_op jit(solution)/shard_map/reduce_scatter | solution.py:211
  494.1 267.5 %reduce-scatter.20.cloned.1.call-start = ((), (), s32[]{:S(2)}) async-start(), calls=%async_computation.14 | async-start | bytes 5013504 | tf_op jit(solution)/shard_map/reduce_scatter | solution.py:214
  497.7 3.6 copy-start.25
  497.7 4.2 copy-start.24
  497.7 4.8 copy-start.23
  497.7 294.0 %copy-start = (bf16[768,2304]{1,0:T(8,128)(2,1)S(1)}, bf16[768,2304]{1,0:T(8,128)(2,1)}, u32[]{:S(2)}) copy-start(bf16[768,2304]{1,0:T(8,128)(2,1)} %all-gather.7.cloned.1.call-done) | copy-start | bytes 10616836
  497.8 325.4 %reduce-scatter.28.cloned.1.call-start = ((), (), s32[]{:S(2)}) async-start(), calls=%async_computation.18 | async-start | bytes 208896
  507.3 254.9 %copy-start.26 = (bf16[3072]{0:T(1024)(128)(2,1)S(1)}, bf16[3072]{0:T(1024)(128)(2,1)}, u32[]{:S(2)}) copy-start(bf16[3072]{0:T(1024)(128)(2,1)} %get-tuple-element.375) | copy-start | bytes 18436
  507.3 412.2 %all-reduce.6.cloned.1.call-start = ((), (), s32[]{:S(2)}) async-start(), calls=%async_computation.19 | async-start | bytes 2506752 | tf_op jit(solution)/shard_map/psum | solution.py:225
  919.5 3.7 copy-start.12
  919.5 4.7 copy-start.13
Sparse Core Ops, SparseCore 0:
  9.7 38.9 all-gather.6
  52.5 63.1 all-gather.8
  117.4 30.5 all-gather.10
  149.5 38.3 all-gather.12
  189.4 38.8 all-gather.14
  328.5 73.2 reduce-scatter.21
  406.0 71.9 reduce-scatter.23
  487.9 66.4 reduce-scatter.25
  556.8 60.9 reduce-scatter.15
  620.0 69.1 reduce-scatter.17
  691.6 69.9 reduce-scatter.19
  763.8 59.2 reduce-scatter.27
  826.7 92.7 all-reduce.5
where the time goes:
time: 935 us; the launch traced here: 931 us
  waiting for transfers between devices  599 us (64%)
  matrix products  126 us (13%)
  blocking collectives  103 us (11%)
  local copies, waits for them, and re-layouts  53.1 us (6%)
  other arithmetic  33.3 us (4%)
  between operations  15.6 us (2%)
    unnamed x17, waiting for transfers between devices  223 us
    reduce_scatter x1, waiting for transfers between devices, body(): lax.psum_scatter(down_grad.astype(jnp.bfloat16), 'fsdp', scatter_dimensio...  72.4 us
    reduce_scatter x1, waiting for transfers between devices, body(): lax.psum_scatter(up_grad.astype(jnp.bfloat16), 'fsdp', scatter_dimension=...  71.4 us
    psum x1, waiting for transfers between devices, body(): lax.psum(pieces[0].astype(jnp.bfloat16), 'ctx').astype(jnp.float32)  70.5 us
    reduce_scatter x1, waiting for transfers between devices, body(): lax.psum_scatter(out_proj_grad.astype(jnp.bfloat16), 'fsdp', scatter_dime...  61.4 us
    unnamed x2, blocking collectives  59 us
    dot_general x40, matrix products, right_dot(): lax.dot_general(left_side, right_side, (((1,), (1,)), ((), ())), preferre...  54.7 us
    dot_general x28, matrix products, left_dot(): lax.dot_general(left_side, right_side, (((0,), (0,)), ((), ())), preferre...  42.1 us
  transfers between devices with their start and end apart: 13, of which 12 were waited for; matrix products, arithmetic and copies ran while one was open for 10% of the time, Pallas kernels for 0%

commit v1 on v0

v1 whole, which is shorter than its diff:
```python
import jax
import jax.numpy as jnp
from jax import lax
from jax.experimental import pallas as pl
from jax.experimental.pallas import tpu as pltpu
from jax.sharding import PartitionSpec as P

D = 768
HD = 64
BLK = 128
NBLK = 8
SEQS = 3
SLOTS = 4
LOCAL = 3
WIDE = LOCAL * HD
FF = 3072
HALF = FF // 2
F = 16

epsilon = 1e-12
masked_fill = -1e30
root_half = 0.7071067811865476
inv_root_tau = 0.3989422804014327

bf16 = jnp.bfloat16
f32 = jnp.float32

VM = pl.BlockSpec(memory_space=pltpu.VMEM)
SM = pl.BlockSpec(memory_space=pltpu.SMEM)


def params():
    return pltpu.CompilerParams(vmem_limit_bytes=56 * 1024 * 1024)


def nn(a, b):
    return lax.dot_general(a, b, (((1,), (0,)), ((), ())), preferred_element_type=f32)


def nt(a, b):
    return lax.dot_general(a, b, (((1,), (1,)), ((), ())), preferred_element_type=f32)


def tn(a, b):
    return lax.dot_general(a, b, (((0,), (0,)), ((), ())), preferred_element_type=f32)


def call(kernel, name, out_shape, in_specs, scratch=(), flops=0, nbytes=0):
    return pl.pallas_call(
        kernel,
        out_shape=out_shape,
        in_specs=in_specs,
        out_specs=jax.tree.map(lambda _: VM, out_shape),
        scratch_shapes=list(scratch),
        compiler_params=params(),
        cost_estimate=pl.CostEstimate(flops=flops, bytes_accessed=nbytes, transcendentals=0),
        name=name,
    )


def shape(dims, dtype=f32):
    return jax.ShapeDtypeStruct(dims, dtype)


def slot_table(meta, table):
    xh = meta[0]
    for i in range(4):
        own = meta[4 + 2 * i + xh]
        for k in range(SLOTS):
            table[SLOTS * i + k] = 0
        count = jnp.int32(0)
        for b in range(NBLK):
            same = meta[4 + b] == own

            @pl.when(same)
            def _(i=i, b=b, count=count):
                table[SLOTS * i + jnp.minimum(count, SLOTS - 1)] = b

            count = count + same.astype(jnp.int32)


def attend_kernel(meta, x, w, bias, chances, query, keys, values, mixture, table):
    slot_table(meta, table)
    xh = meta[0]
    xs = x[...].reshape(NBLK * BLK, D)
    key_all = nn(xs, w[:, WIDE : 2 * WIDE]).astype(bf16)
    value_all = (nn(xs, w[:, 2 * WIDE : 3 * WIDE]) + bias[1:2, :]).astype(bf16)
    for h in range(LOCAL):
        keys[h] = key_all[:, HD * h : HD * h + HD]
        values[h] = value_all[:, HD * h : HD * h + HD]
    xq = jnp.concatenate([x[2 * i + xh] for i in range(4)], axis=0)
    q_all = (nn(xq, w[:, :WIDE]) + bias[0:1, :]).astype(bf16) * bf16(HD**-0.5)
    for h in range(LOCAL):
        query[h] = q_all[:, HD * h : HD * h + HD]
    lane = lax.broadcasted_iota(jnp.int32, (1, BLK), 1)
    for i in range(4):
        length = meta[1 + meta[4 + 2 * i + xh]]
        blank = jnp.concatenate(
            [jnp.where(lane < length - BLK * k, 0.0, masked_fill) for k in range(SLOTS)], axis=1
        )
        picks = [pl.ds(pl.multiple_of(table[SLOTS * i + k] * BLK, BLK), BLK) for k in range(SLOTS)]
        outs = []
        for h in range(LOCAL):
            key_h = jnp.concatenate([keys[h, p, :] for p in picks], axis=0)
            value_h = jnp.concatenate([values[h, p, :] for p in picks], axis=0)
            scores = nt(query[h, BLK * i : BLK * i + BLK, :], key_h) + blank
            peak = jnp.max(scores, axis=-1, keepdims=True)
            raised = jnp.exp(scores - peak)
            share = (raised * (1.0 / jnp.sum(raised, axis=-1, keepdims=True))).astype(bf16)
            chances[i, h] = share
            outs.append(nn(share, value_h))
        mixture[i] = jnp.concatenate(outs, axis=1).astype(bf16)


def attend(meta, x_all, w_heads, bias):
    return call(
        attend_kernel,
        "attend",
        (
            shape((4, LOCAL, BLK, SLOTS * BLK), bf16),
            shape((LOCAL, 4 * BLK, HD), bf16),
            shape((LOCAL, NBLK * BLK, HD), bf16),
            shape((LOCAL, NBLK * BLK, HD), bf16),
            shape((4, BLK, WIDE), bf16),
        ),
        [SM, VM, VM, VM],
        [pltpu.SMEM((4 * SLOTS,), jnp.int32)],
        flops=2 * 10**9,
        nbytes=6 * 10**6,
    )(meta, x_all, w_heads, bias)


def attend_back_kernel(
    meta, x, w, cot, chances, query, keys, values, grad_w, partial, sums, table, key_acc, value_acc
):
    slot_table(meta, table)
    xh = meta[0]
    key_acc[...] = jnp.zeros_like(key_acc)
    value_acc[...] = jnp.zeros_like(value_acc)
    query_cots = []
    for i in range(4):
        picks = [pl.ds(pl.multiple_of(table[SLOTS * i + k] * BLK, BLK), BLK) for k in range(SLOTS)]
        parts = []
        cot_i = cot[i]
        for h in range(LOCAL):
            key_h = jnp.concatenate([keys[h, p, :] for p in picks], axis=0)
            value_h = jnp.concatenate([values[h, p, :] for p in picks], axis=0)
            cot_h = cot_i[:, HD * h : HD * h + HD]
            share_low = chances[i, h]
            share = share_low.astype(f32)
            chance_cot = nt(cot_h, value_h)
            inner = jnp.sum(share * chance_cot, axis=-1, keepdims=True)
            score_cot = (share * (chance_cot - inner)).astype(bf16)
            parts.append(nn(score_cot, key_h))
            key_part = tn(score_cot, query[h, BLK * i : BLK * i + BLK, :])
            value_part = tn(share_low, cot_h)
            for k, p in enumerate(picks):
                key_acc[h, p, :] += key_part[BLK * k : BLK * k + BLK]
                value_acc[h, p, :] += value_part[BLK * k : BLK * k + BLK]
        query_cots.append((jnp.concatenate(parts, axis=1) * HD**-0.5).astype(bf16))
    query_cot = jnp.concatenate(query_cots, axis=0)
    key_cot = jnp.concatenate([key_acc[h] for h in range(LOCAL)], axis=1).astype(bf16)
    value_cot = jnp.concatenate([value_acc[h] for h in range(LOCAL)], axis=1).astype(bf16)
    xs = x[...].reshape(NBLK * BLK, D)
    xq = jnp.concatenate([x[2 * i + xh] for i in range(4)], axis=0)
    grad_w[:, :WIDE] = tn(xq, query_cot).astype(bf16)
    grad_w[:, WIDE : 2 * WIDE] = tn(xs, key_cot).astype(bf16)
    grad_w[:, 2 * WIDE : 3 * WIDE] = tn(xs, value_cot).astype(bf16)
    sums[0:1] = jnp.sum(query_cot.astype(f32), axis=0, keepdims=True)
    sums[1:2] = jnp.sum(value_cot.astype(f32), axis=0, keepdims=True)
    key_value = nt(key_cot, w[:, WIDE : 2 * WIDE]) + nt(value_cot, w[:, 2 * WIDE : 3 * WIDE])
    query_part = nt(query_cot, w[:, :WIDE])
    for i in range(4):
        row = BLK * 2 * i
        both = [key_value[row : row + BLK], key_value[row + BLK : row + 2 * BLK]]
        mine = query_part[BLK * i : BLK * i + BLK]
        partial[2 * i] = (both[0] + jnp.where(xh == 0, mine, 0.0)).astype(bf16)
        partial[2 * i + 1] = (both[1] + jnp.where(xh == 1, mine, 0.0)).astype(bf16)


def attend_back(meta, x_all, w_heads, cot, kept):
    return call(
        attend_back_kernel,
        "attend_back",
        (shape((D, LOCAL * WIDE), bf16), shape((NBLK, BLK, D), bf16), shape((2, WIDE))),
        [SM] + [VM] * 7,
        [
            pltpu.SMEM((4 * SLOTS,), jnp.int32),
            pltpu.VMEM((LOCAL, NBLK * BLK, HD), f32),
            pltpu.VMEM((LOCAL, NBLK * BLK, HD), f32),
        ],
        flops=5 * 10**9,
        nbytes=10**7,
    )(meta, x_all, w_heads, cot, *kept)


def centred(hidden):
    centre = hidden - jnp.mean(hidden, axis=-1, keepdims=True)
    inverse = lax.rsqrt(jnp.mean(centre * centre, axis=-1, keepdims=True) + epsilon)
    return centre * inverse, inverse


def norm_back(scaled, hat, inverse):
    return inverse * (
        scaled
        - jnp.mean(scaled, axis=-1, keepdims=True)
        - hat * jnp.mean(scaled * hat, axis=-1, keepdims=True)
    )


def first_kernel(mixture, weights, vectors, tokens, norm, low, hat, inverse):
    w_out = weights[:, 192:240, :].reshape(D, D)
    total = nn(mixture[0], w_out[:WIDE])
    for z in range(1, 4):
        total += nn(mixture[z], w_out[WIDE * z : WIDE * z + WIDE])
    first_hat, first_inv = centred(tokens[...].astype(f32) + (total + vectors[2:3]))
    first_norm = first_hat * vectors[4:5] + vectors[5:6]
    norm[...] = first_norm
    low[...] = first_norm.astype(bf16)
    hat[...] = first_hat
    inverse[...] = first_inv


def feed_kernel(mine, other, weights, b_up, activ, slope, keep, send):
    rows = jnp.concatenate([mine[...], other[...]], axis=0)
    total = None
    for j in range(2):
        w_up = weights[:, 96 + 48 * j : 144 + 48 * j, :].reshape(D, D)
        up = nn(rows, w_up) + b_up[:, D * j : D * j + D]
        erf = lax.erf(up * root_half)
        low = (0.5 * up * (1.0 + erf)).astype(bf16)
        activ[:, D * j : D * j + D] = low
        slope[:, D * j : D * j + D] = (
            0.5 * (1.0 + erf) + up * jnp.exp(-0.5 * up * up) * inv_root_tau
        ).astype(bf16)
        w_down = weights[8 * j : 8 * j + 8, 0:96, :].reshape(D, D)
        part = nn(low, w_down)
        total = part if total is None else total + part
    keep[...] = total[:BLK]
    send[...] = total[BLK:].astype(bf16)


def second_kernel(norm, keep, came, vectors, out_grad, layer_out, cot, low, sums):
    second_sum = norm[...] + (keep[...] + came[...].astype(f32)) + vectors[3:4]
    second_hat, second_inv = centred(second_sum)
    layer_out[...] = (second_hat * vectors[6:7] + vectors[7:8]).astype(bf16)
    out_cot = out_grad[...].astype(f32)
    second_cot = norm_back(out_cot * vectors[6:7], second_hat, second_inv)
    cot[...] = second_cot
    down_cot = second_cot.astype(bf16)
    low[...] = down_cot
    sums[0:1] = jnp.sum(down_cot.astype(f32), axis=0, keepdims=True)
    sums[1:2] = jnp.sum(out_cot * second_hat, axis=0, keepdims=True)
    sums[2:3] = jnp.sum(out_cot, axis=0, keepdims=True)


def feed_back_kernel(mine, other, weights, slope, up_cot, keep, send, sums):
    rows = jnp.concatenate([mine[...], other[...]], axis=0)
    total = None
    for j in range(2):
        w_down = weights[8 * j : 8 * j + 8, 0:96, :].reshape(D, D)
        w_up = weights[:, 96 + 48 * j : 144 + 48 * j, :].reshape(D, D)
        low = (nt(rows, w_down) * slope[:, D * j : D * j + D].astype(f32)).astype(bf16)
        up_cot[:, D * j : D * j + D] = low
        sums[:, D * j : D * j + D] = jnp.sum(low.astype(f32), axis=0, keepdims=True)
        part = nt(low, w_up)
        total = part if total is None else total + part
    keep[...] = total[:BLK]
    send[...] = total[BLK:].astype(bf16)


def feed_grad_kernel(mine, other, low_mine, low_other, activ, up_cot, grads):
    down_cot = jnp.concatenate([mine[...], other[...]], axis=0)
    first_low = jnp.concatenate([low_mine[...], low_other[...]], axis=0)
    for j in range(2):
        down = tn(activ[:, D * j : D * j + D], down_cot).astype(bf16)
        grads[8 * j : 8 * j + 8, 0:96, :] = down.reshape(8, 96, D)
        up = tn(first_low, up_cot[:, D * j : D * j + D]).astype(bf16)
        grads[:, 96 + 48 * j : 144 + 48 * j, :] = up.reshape(F, 48, D)


def first_back_kernel(
    cot, keep, came, vectors, hat, inverse, weights, mixture, input_cot, back, grad_out, sums
):
    first_cot = cot[...] + (keep[...] + came[...].astype(f32))
    first_hat = hat[...]
    total = norm_back(first_cot * vectors[4:5], first_hat, inverse[...])
    input_cot[...] = total
    attend_cot = total.astype(bf16)
    sums[0:1] = jnp.sum(attend_cot.astype(f32), axis=0, keepdims=True)
    sums[1:2] = jnp.sum(first_cot * first_hat, axis=0, keepdims=True)
    sums[2:3] = jnp.sum(first_cot, axis=0, keepdims=True)
    w_out = weights[:, 192:240, :].reshape(D, D)
    for z in range(4):
        back[z] = nt(attend_cot, w_out[WIDE * z : WIDE * z + WIDE]).astype(bf16)
        grad_out[4 * z : 4 * z + 4] = (
            tn(mixture[z], attend_cot).astype(bf16).reshape(4, 48, D)
        )


CHIPS = [[i for i in range(F) if i % 2 == k] for k in range(2)]
ZS = [[0, 2, 4, 6], [1, 3, 5, 7]]
HALVES = [[0, 1, 4, 5], [2, 3, 6, 7]]


def swap(x, axis, size, bit):
    return lax.ppermute(x, axis, [(i, i ^ bit) for i in range(size)])


def a2a(x, axis, groups=None):
    return lax.all_to_all(x, axis, 0, 0, tiled=True, axis_index_groups=groups)


def spread(x, axis, n, groups=None):
    return a2a(jnp.broadcast_to(x[None], (n,) + x.shape), axis, groups)


def body(tokens, w_qkv, w_out, w_up, w_down, vectors, b_up, lengths, block_seq, out_grad):
    place = lax.axis_index("ctx")
    z, xh, half = place // 2, place % 2, (place // 2) % 2
    core = lax.axis_index("fsdp") % 2

    def pick(x, index, axis):
        return lax.dynamic_index_in_dim(x, index, axis, keepdims=False)

    feed_own = jnp.concatenate(
        [
            pick(w_down.reshape(2, 96, D), half, 0),
            pick(w_up.reshape(48, F, 2, 96), half, 2).reshape(48, 2, D).transpose(1, 0, 2).reshape(96, D),
            w_out,
        ],
        axis=0,
    )
    feed_w = lax.all_gather(feed_own, "fsdp", axis=0, tiled=False)
    heads_own = jnp.concatenate(
        [
            pick(w_qkv.reshape(48, 3, 4, WIDE), z, 2).reshape(48, 3 * WIDE),
            vectors.T,
            b_up.reshape(48, 4),
            jnp.zeros((48, 180), bf16),
        ],
        axis=1,
    )
    heads_mine = spread(heads_own, "fsdp", 8, CHIPS)
    heads_other = swap(heads_mine, "fsdp", F, 1)
    heads_w = jnp.where(
        core == 0,
        jnp.concatenate([heads_mine, heads_other], axis=1),
        jnp.concatenate([heads_other, heads_mine], axis=1),
    ).reshape(D, D)
    x_all = spread(tokens, "ctx", NBLK)

    rows = heads_w[:, 576:584].T.astype(f32)
    up_bias = pick(heads_w[:, 584:588].reshape(F, 2, 96), half, 1).reshape(1, HALF).astype(f32)
    head_bias = pick(rows[0:2].reshape(2, 4, WIDE), z, 1)
    meta = jnp.concatenate([xh[None], lengths[0], block_seq[0]]).astype(jnp.int32)

    *kept, mixture_part = attend(meta, x_all, heads_w, head_bias)
    mixture = a2a(mixture_part, "ctx", ZS)
    first_norm, first_low, first_hat, first_inv = call(
        first_kernel,
        "first",
        (shape((BLK, D)), shape((BLK, D), bf16), shape((BLK, D)), shape((BLK, 1))),
        [VM] * 4,
        flops=2 * BLK * D * D,
        nbytes=8 * 10**6,
    )(mixture, feed_w, rows, tokens)
    low_other = swap(first_low, "ctx", NBLK, 2)
    activ, slope, keep, send = call(
        feed_kernel,
        "feed",
        (shape((2 * BLK, HALF), bf16), shape((2 * BLK, HALF), bf16), shape((BLK, D)), shape((BLK, D), bf16)),
        [VM] * 4,
        flops=8 * BLK * D * HALF,
        nbytes=8 * 10**6,
    )(first_low, low_other, feed_w, up_bias)
    came = swap(send, "ctx", NBLK, 2)
    layer_out, second_cot, down_cot, second_sums = call(
        second_kernel,
        "second",
        (shape((BLK, D), bf16), shape((BLK, D)), shape((BLK, D), bf16), shape((3, D))),
        [VM] * 5,
        flops=10**7,
        nbytes=2 * 10**6,
    )(first_norm, keep, came, rows, out_grad)
    down_other = swap(down_cot, "ctx", NBLK, 2)
    up_cot, keep, send, up_sums = call(
        feed_back_kernel,
        "feed_back",
        (shape((2 * BLK, HALF), bf16), shape((BLK, D)), shape((BLK, D), bf16), shape((1, HALF))),
        [VM] * 4,
        flops=8 * BLK * D * HALF,
        nbytes=8 * 10**6,
    )(down_cot, down_other, feed_w, slope)
    came = swap(send, "ctx", NBLK, 2)
    feed_grads = call(
        feed_grad_kernel,
        "feed_grad",
        shape((F, 192, D), bf16),
        [VM] * 6,
        flops=8 * BLK * D * HALF,
        nbytes=8 * 10**6,
    )(down_cot, down_other, first_low, low_other, activ, up_cot)
    input_cot, back, out_grads, first_sums = call(
        first_back_kernel,
        "first_back",
        (shape((BLK, D)), shape((4, BLK, WIDE), bf16), shape((F, 48, D), bf16), shape((3, D))),
        [VM] * 8,
        flops=4 * BLK * D * D,
        nbytes=8 * 10**6,
    )(second_cot, keep, came, rows, first_hat, first_inv, feed_w, mixture)
    grads = jnp.concatenate([feed_grads, out_grads], axis=1)
    feed_sum = lax.psum_scatter(grads.reshape(F * 240, D), "fsdp", scatter_dimension=0, tiled=True)
    cot = a2a(back, "ctx", ZS)
    head_grads, partial, head_sums = attend_back(meta, x_all, heads_w, cot, kept)

    tokens_grad = input_cot + jnp.sum(a2a(partial, "ctx").astype(f32), axis=0)

    slot = (lax.broadcasted_iota(jnp.int32, (1, D), 1) // WIDE) == z
    head_rows = jnp.where(slot, jnp.tile(head_sums, (1, 4)), 0.0)
    vector_part = jnp.concatenate([head_rows, first_sums[0:1], second_sums[0:1], first_sums[1:3], second_sums[1:3]])
    extras = jnp.concatenate([vector_part.T, up_sums.reshape(D, 2), jnp.zeros((D, 182), f32)], axis=1)
    heads_grad = jnp.concatenate([head_grads, extras.astype(bf16)], axis=1).reshape(8, 2, 48, D)
    mine = pick(heads_grad, core, 1)
    other = swap(pick(heads_grad, 1 - core, 1), "fsdp", F, 1)
    pair = (mine.astype(f32) + other.astype(f32)).astype(bf16)
    heads_sum = jnp.sum(a2a(pair, "fsdp", CHIPS).astype(f32), axis=0).astype(bf16)

    padded = jnp.concatenate([feed_sum, jnp.zeros((16, D), bf16)], axis=0)
    quarter = jnp.sum(a2a(padded.reshape(4, 64, D), "ctx", HALVES).astype(f32), axis=0).astype(bf16)
    every = spread(jnp.concatenate([quarter, heads_sum], axis=0), "ctx", NBLK).astype(f32)

    halves = every[:, :64].reshape(2, 2, 2, 64, D).transpose(1, 0, 2, 3, 4).reshape(2, 256, D)
    down_grad = halves[:, :96].reshape(192, D)
    up_grad = jnp.stack(
        [jnp.concatenate([halves[h, 96:144], halves[h, 144:192]], axis=1).reshape(48, F, 96) for h in range(2)],
        axis=2,
    ).reshape(48, FF)
    out_proj_grad = halves[0, 192:240] + halves[1, 192:240]
    heads = every[:, 64:].reshape(4, 2, 48, 4, WIDE)
    by_z = heads[:, 0] + heads[:, 1]
    qkv_grad = by_z[:, :, :3].transpose(1, 2, 0, 3).reshape(48, 3 * D)
    extra = every[:, 64:, 576:586]
    vectors_grad = jnp.sum(extra[:, :, :8], axis=0).T
    ups = extra[:, :, 8:].reshape(2, 2, 2, 48, 2)
    up_bias_grad = jnp.sum(ups, axis=(0, 2)).reshape(192)
    return (layer_out, tokens_grad, qkv_grad, out_proj_grad, up_grad, down_grad, vectors_grad, up_bias_grad)


def solution(mesh):
    by_token = P(("fsdp", "ctx"), None)
    by_row = P("fsdp", None)
    in_specs = (
        by_token, by_row, by_row, by_row, by_row, P(None, "fsdp"), P("fsdp"), by_row, by_row, by_token,
    )
    out_specs = (by_token, by_token, by_row, by_row, by_row, by_row, P(None, "fsdp"), P("fsdp"))
    return jax.shard_map(body, mesh=mesh, in_specs=in_specs, out_specs=out_specs, check_vma=False)
```

time: 935 us -> 316 us (0.34)
  waiting for transfers between devices: 599 us -> 140 us
  matrix products: 126 us -> 0 us
  blocking collectives: 103 us -> 35.2 us
  Pallas kernels: 0 us -> 48.8 us
  starting transfers between devices: 0.71 us -> 29.8 us
  other arithmetic: 33.3 us -> 11.5 us
  local copies, waits for them, and re-layouts: 53.1 us -> 32.1 us
    unnamed x17 -> x2, waiting for transfers between devices: 223 us -> 0.03 us
    reduce_scatter x3 -> x1, waiting for transfers between devices: 205 us -> 45.7 us  [body(): lax.psum_scatter(grads.reshape(F * 240, D), 'fsdp', scatter_dimension=0,...]
    dot_general x96 -> x0, matrix products: 126 us -> none  [the longest x40 54.7 us: right_dot(): lax.dot_general(left_side, right_side, (((1,), (1,)), ((), ())), preferre...]
    all_gather x5 -> x1, waiting for transfers between devices: 100 us -> 0.01 us  [body(): feed_w = lax.all_gather(feed_own, 'fsdp', axis=0, tiled=False)]
    all_to_all x0 -> x6, waiting for transfers between devices: none -> 76.4 us  [a2a(): return lax.all_to_all(x, axis, 0, 0, tiled=True, axis_index_groups=groups)]
    psum x1 -> x0, waiting for transfers between devices: 70.5 us -> none  [body(): lax.psum(pieces[0].astype(jnp.bfloat16), 'ctx').astype(jnp.float32)]
    unnamed x2 -> x0, blocking collectives: 59 us -> none
    pallas_call x0 -> x8, Pallas kernels: none -> 48.8 us  [the longest x1 11.2 us: attend_back(): call(attend_back_kernel, 'attend_back', (shape((D, LOCAL * WIDE), bf16),...]
  transfers between devices with their start and end apart: 13 -> 14, of which waited for: 12 -> 11; matrix products, arithmetic and copies ran while one was open for 10% -> 6% of each run, Pallas kernels for 0% -> 8%
where the time goes in v1:
time: 316 us; the launch traced here: 312 us
  waiting for transfers between devices  140 us (44%)
  Pallas kernels  48.8 us (15%)
  blocking collectives  35.2 us (11%)
  local copies, waits for them, and re-layouts  32.1 us (10%)
  starting transfers between devices  29.8 us (9%)
  between operations  14.7 us (5%)
  other arithmetic  11.5 us (4%)
    all_to_all x6, waiting for transfers between devices, a2a(): return lax.all_to_all(x, axis, 0, 0, tiled=True, axis_index_groups=groups)  76.4 us
    reduce_scatter x1, waiting for transfers between devices, body(): lax.psum_scatter(grads.reshape(F * 240, D), 'fsdp', scatter_dimension=0,...  45.7 us
    all_to_all x2, blocking collectives, a2a(): return lax.all_to_all(x, axis, 0, 0, tiled=True, axis_index_groups=groups)  35.2 us
    all_to_all x6, starting transfers between devices, a2a(): return lax.all_to_all(x, axis, 0, 0, tiled=True, axis_index_groups=groups)  27.3 us
    ppermute x6, waiting for transfers between devices, swap(): return lax.ppermute(x, axis, [(i, i ^ bit) for i in range(size)])  17.4 us
    pallas_call x1, Pallas kernels, attend_back(): call(attend_back_kernel, 'attend_back', (shape((D, LOCAL * WIDE), bf16),...  11.2 us
    pallas_call x1, Pallas kernels, attend(): call(attend_kernel, 'attend', (shape((4, LOCAL, BLK, SLOTS * BLK), bf16),...  9.02 us
  transfers between devices with their start and end apart: 14, of which 11 were waited for; matrix products, arithmetic and copies ran while one was open for 6% of the time, Pallas kernels for 8%

profile of v1, /device:TPU:0, one launch (start us, length us, event | category | flops | bytes accessed | tf_op | source)
XLA Modules:
  0.0 311.6 jit_solution(18381030551663848937)
XLA Ops:
  7.3 1.4 reshape.152
  8.7 1.2 dynamic-slice_reduce_fusion
  10.4 0.8 pad_maximum_fusion.1
  12.6 19.1 %all_to_all.40 = bf16[8,48,768]{2,1,0:T(8,128)(2,1)S(1)} all-to-all(bf16[8,48,768]{2,1,0:T(8,128)(2,1)S(1)} %broadcast_in_dim.43), channel_id=1, replica_groups={{0,16,32,48,64,80,96,112},{8,24,40,56,72,88,104,120},{1,17,33,49,65,81,..., dimensions={0} | all-to-all | bytes 1179648 | tf_op jit(solution)/shard_map/all_to_all | solution.py:311
  31.7 1.2 broadcast_in_dim.41
  33.0 8.8 %all-to-all-start = ((bf16[8,128,768]{2,1,0:T(8,128)(2,1)}), bf16[8,128,768]{2,1,0:T(8,128)(2,1)}, u32[]{:S(2)}, u32[]{:S(2)}) async-start(bf16[8,128,768]{2,1,0:T(8,128)(2,1)} %broadcast_in_dim.41), calls=%async_computation | async-start | bytes 3145728 | tf_op jit(solution)/shard_map/all_to_all | solution.py:311
  42.3 1.4 collective-permute-done
  44.3 0.8 copy.66
  45.1 30.7 %all-to-all-done.x = bf16[8,128,768]{2,1,0:T(8,128)(2,1)} async-done(((bf16[8,128,768]{2,1,0:T(8,128)(2,1)}), bf16[8,128,768]{2,1,0:T(8,128)(2,1)}, u32[]{:S(2)}, u32[]{:S(2)}) %all-to-all-start) | async-done | bytes 1572896 | tf_op jit(solution)/shard_map/all_to_all | solution.py:311
  75.8 9.0 %attend.1 = (bf16[4,3,128,512]{3,2,1,0:T(8,128)(2,1)}, bf16[3,512,64]{2,1,0:T(8,128)(2,1)}, bf16[3,1024,64]{2,1,0:T(8,128)(2,1)}, bf16[3,1024,64]{2,1,0:T(8,128)(2,1)}, bf16[4,128,192]{2,1,0:T(8,128)(2,1)}) custom-call(s32[12]{0:T(128)} %pad_add_fusion.meta, bf16[8,128,768]{2,1,0:T(8,128)(2,1)} %all-to-all-done.x, bf16[768,768]{1,0:T(8,128)(2,1)} %bitcast.50, ...), custom_call_target="tpu_custom_call" | custom-call | flops 2000000000 | bytes 6000000 | tf_op jit(solution)/shard_map/attend/pallas_call | solution.py:116
  84.8 1.8 copy.67
  86.6 3.4 %all-to-all-start.2 = ((bf16[4,128,192]{1,2,0:T(8,128)(2,1)}), bf16[4,128,192]{1,2,0:T(8,128)(2,1)S(1)}, u32[]{:S(2)}, u32[]{:S(2)}) async-start(bf16[4,128,192]{1,2,0:T(8,128)(2,1)} %copy.67), calls=%async_computation.2 | async-start | bytes 393216 | tf_op jit(solution)/shard_map/all_to_all | solution.py:311
  90.0 0.7 copy.71.vectors
  90.8 5.5 %all-to-all-done.2 = bf16[4,128,192]{1,2,0:T(8,128)(2,1)S(1)} async-done(((bf16[4,128,192]{1,2,0:T(8,128)(2,1)}), bf16[4,128,192]{1,2,0:T(8,128)(2,1)S(1)}, u32[]{:S(2)}, u32[]{:S(2)}) %all-to-all-start.2) | async-done | bytes 196640 | tf_op jit(solution)/shard_map/all_to_all | solution.py:311
  96.3 0.8 copy.70.mixture
  97.1 4.3 %first.1 = (f32[128,768]{1,0:T(8,128)}, bf16[128,768]{1,0:T(8,128)(2,1)}, f32[128,768]{1,0:T(8,128)}, f32[128,1]{1,0:T(8,128)}) custom-call(bf16[4,128,192]{2,1,0:T(8,128)(2,1)} %copy.70.mixture, bf16[16,240,768]{2,1,0:T(8,128)(2,1)} %bitcast.39, f32[8,768]{1,0:T(8,128)} %copy.71.vectors, bf16[128,768]{1,0:T(8,128)(2,1)} %tokens.1), custom_call_target="tpu_custom_call" | custom-call | flops 150994944 | bytes 8000000 | tf_op jit(solution)/shard_map/first/pallas_call | solution.py:360
  101.4 0.6 collective-permute-start.1
  101.9 1.0 slice.93
  103.2 0.7 reshape.168.b_up
  103.9 3.4 %collective-permute-done.1.other.low_other = bf16[128,768]{1,0:T(8,128)(2,1)S(1)} collective-permute-done((bf16[128,768]{1,0:T(8,128)(2,1)}, bf16[128,768]{1,0:T(8,128)(2,1)S(1)}, u32[]{:S(2)}, u32[]{:S(2)}) %collective-permute-start.1) | collective-permute-done | bytes 196640 | tf_op jit(solution)/shard_map/ppermute | solution.py:307
  107.3 0.7 copy-done.5
  107.9 5.5 %feed.1 = (bf16[256,1536]{1,0:T(8,128)(2,1)}, bf16[256,1536]{1,0:T(8,128)(2,1)}, f32[128,768]{1,0:T(8,128)}, bf16[128,768]{1,0:T(8,128)(2,1)}) custom-call(bf16[128,768]{1,0:T(8,128)(2,1)} %get-tuple-element.38.mine.low_mine, bf16[128,768]{1,0:T(8,128)(2,1)} %copy-done.5, bf16[16,240,768]{2,1,0:T(8,128)(2,1)} %bitcast.40, f32[1,1536]{1,0:T(1,128)} %reshape.168.b_up), custom_call_target="tpu_custom_call" | custom-call | flops 1207959552 | bytes 8000000 | tf_op jit(solution)/shard_map/feed/pallas_call | solution.py:369
  113.4 0.6 collective-permute-start.2
  114.0 5.3 %collective-permute-done.2.came = bf16[128,768]{1,0:T(8,128)(2,1)S(1)} collective-permute-done((bf16[128,768]{1,0:T(8,128)(2,1)}, bf16[128,768]{1,0:T(8,128)(2,1)S(1)}, u32[]{:S(2)}, u32[]{:S(2)}) %collective-permute-start.2) | collective-permute-done | bytes 196640 | tf_op jit(solution)/shard_map/ppermute | solution.py:307
  119.3 0.7 copy-done.12
  120.0 2.4 second.1
  122.4 0.6 collective-permute-start.3
  123.0 5.3 %collective-permute-done.3.other = bf16[128,768]{1,0:T(8,128)(2,1)S(1)} collective-permute-done((bf16[128,768]{1,0:T(8,128)(2,1)}, bf16[128,768]{1,0:T(8,128)(2,1)S(1)}, u32[]{:S(2)}, u32[]{:S(2)}) %collective-permute-start.3) | collective-permute-done | bytes 196640 | tf_op jit(solution)/shard_map/ppermute | solution.py:307
  128.3 0.7 copy-done.4
  129.0 5.6 %feed_back.1 = (bf16[256,1536]{1,0:T(8,128)(2,1)}, f32[128,768]{1,0:T(8,128)}, bf16[128,768]{1,0:T(8,128)(2,1)}, f32[1,1536]{1,0:T(1,128)}) custom-call(bf16[128,768]{1,0:T(8,128)(2,1)} %get-tuple-element.43.mine, bf16[128,768]{1,0:T(8,128)(2,1)} %copy-done.4, bf16[16,240,768]{2,1,0:T(8,128)(2,1)} %bitcast.41, bf16[256,1536]{1,0:T(8,128)(2,1)} %get-tuple-element.44.slope), custom_call_target="tpu_custom_call" | custom-call | flops 1207959552 | bytes 8000000 | tf_op jit(solution)/shard_map/feed_back/pallas_call | solution.py:387
  135.1 5.4 %feed_grad.1 = bf16[16,192,768]{2,1,0:T(8,128)(2,1)} custom-call(bf16[128,768]{1,0:T(8,128)(2,1)} %get-tuple-element.43.mine, bf16[128,768]{1,0:T(8,128)(2,1)} %copy-done.4, bf16[128,768]{1,0:T(8,128)(2,1)} %get-tuple-element.38.mine.low_mine, bf16[128,768]{1,0:T(8,128)(2,1)} %copy-done.5, bf16[256,1536]{1,0:T(8,128)(2,1)} %get-tuple-element.56.activ, ...), custom_call_target="tpu_custom_call" | custom-call | flops 1207959552 | bytes 8000000 | tf_op jit(solution)/shard_map/feed_grad/pallas_call | solution.py:396
  140.5 0.7 copy-done.13
  141.2 5.4 %first_back.1 = (f32[128,768]{1,0:T(8,128)}, bf16[4,128,192]{2,1,0:T(8,128)(2,1)}, bf16[16,48,768]{2,1,0:T(8,128)(2,1)}, f32[3,768]{1,0:T(4,128)}) custom-call(f32[128,768]{1,0:T(8,128)} %get-tuple-element.42.cot, f32[128,768]{1,0:T(8,128)} %get-tuple-element.45.keep, bf16[128,768]{1,0:T(8,128)(2,1)} %copy-done.13, f32[8,768]{1,0:T(8,128)} %copy.71.vectors, ...), custom_call_target="tpu_custom_call" | custom-call | flops 301989888 | bytes 8000000 | tf_op jit(solution)/shard_map/first_back/pallas_call | solution.py:404
  146.6 4.2 %pad_maximum_fusion = bf16[16,240,768]{2,1,0:T(8,128)(2,1)} fusion(bf16[16,48,768]{2,1,0:T(8,128)(2,1)} %get-tuple-element.58, bf16[16,192,768]{2,1,0:T(8,128)(2,1)S(1)} %copy-done.2), kind=kLoop, calls=%fused_computation | loop fusion | flops 11796480 | bytes 11796480 | tf_op jit(solution)/shard_map/concatenate | solution.py:412
  150.9 0.9 copy-done.10
  151.8 0.8 copy.75
  152.6 3.4 %all-to-all-start.3 = ((bf16[4,128,192]{1,2,0:T(8,128)(2,1)}), bf16[4,128,192]{1,2,0:T(8,128)(2,1)S(1)}, u32[]{:S(2)}, u32[]{:S(2)}) async-start(bf16[4,128,192]{1,2,0:T(8,128)(2,1)} %copy.75), calls=%async_computation.3 | async-start | bytes 393216 | tf_op jit(solution)/shard_map/all_to_all | solution.py:311
  156.6 5.7 %all-to-all-done.3 = bf16[4,128,192]{1,2,0:T(8,128)(2,1)S(1)} async-done(((bf16[4,128,192]{1,2,0:T(8,128)(2,1)}), bf16[4,128,192]{1,2,0:T(8,128)(2,1)S(1)}, u32[]{:S(2)}, u32[]{:S(2)}) %all-to-all-start.3) | async-done | bytes 196640 | tf_op jit(solution)/shard_map/all_to_all | solution.py:311
  162.3 0.8 copy.76.cot
  163.1 11.2 %attend_back.1 = (bf16[768,576]{1,0:T(8,128)(2,1)}, bf16[8,128,768]{2,1,0:T(8,128)(2,1)}, f32[2,192]{1,0:T(2,128)}) custom-call(s32[12]{0:T(128)} %pad_add_fusion.meta, bf16[8,128,768]{2,1,0:T(8,128)(2,1)} %all-to-all-done.x, bf16[768,768]{1,0:T(8,128)(2,1)} %bitcast.52, bf16[4,128,192]{2,1,0:T(8,128)(2,1)} %copy.76.cot, ...), custom_call_target="tpu_custom_call" | custom-call | flops 5000000000 | bytes 10000000 | tf_op jit(solution)/shard_map/attend_back/pallas_call | solution.py:182
  174.3 0.7 tile.4
  175.3 1.7 maximum_maximum_fusion
  177.2 2.0 collective-permute-done.5
  179.1 1.0 fusion
  180.1 4.5 %all-to-all-start.6 = ((bf16[8,48,768]{2,1,0:T(8,128)(2,1)}), bf16[8,48,768]{2,1,0:T(8,128)(2,1)S(1)}, u32[]{:S(2)}, u32[]{:S(2)}) async-start(bf16[8,48,768]{2,1,0:T(8,128)(2,1)} %fusion), calls=%async_computation.7 | async-start | bytes 1179648 | tf_op jit(solution)/shard_map/all_to_all | solution.py:311
  184.6 45.7 %reduce-scatter.2.cloned.1.call-done = bf16[240,768]{1,0:T(8,128)(2,1)} async-done(((bf16[3840,768]{1,0:T(8,128)(2,1)}), bf16[240,768]{1,0:T(8,128)(2,1)}) %reduce-scatter.2.cloned.1.call-update) | async-done | bytes 368656 | tf_op jit(solution)/shard_map/reduce_scatter | solution.py:413
  230.3 1.0 concatenate.56
  231.3 16.1 %all_to_all.41 = bf16[4,64,768]{2,1,0:T(8,128)(2,1)S(1)} all-to-all(bf16[4,64,768]{2,1,0:T(8,128)(2,1)S(1)} %bitcast.54), channel_id=1, replica_groups={{0,1,4,5},{2,3,6,7},{8,9,12,13},{10,11,14,15},{16,17,20,21},{18,19,22,2..., dimensions={0} | all-to-all | bytes 786432 | tf_op jit(solution)/shard_map/all_to_all | solution.py:311
  247.4 3.6 %all-to-all-start.4 = ((bf16[8,128,768]{2,1,0:T(8,128)(2,1)}), bf16[8,128,768]{2,1,0:T(8,128)(2,1)S(1)}, u32[]{:S(2)}, u32[]{:S(2)}) async-start(bf16[8,128,768]{2,1,0:T(8,128)(2,1)} %get-tuple-element.55), calls=%async_computation.4 | async-start | bytes 3145728 | tf_op jit(solution)/shard_map/all_to_all | solution.py:311
  251.2 19.4 %all-to-all-done.4 = bf16[8,128,768]{2,1,0:T(8,128)(2,1)S(1)} async-done(((bf16[8,128,768]{2,1,0:T(8,128)(2,1)}), bf16[8,128,768]{2,1,0:T(8,128)(2,1)S(1)}, u32[]{:S(2)}, u32[]{:S(2)}) %all-to-all-start.4) | async-done | bytes 1572896 | tf_op jit(solution)/shard_map/all_to_all | solution.py:311
  270.5 1.2 broadcast_in_dim.47
  271.7 3.8 %all-to-all-start.7 = ((bf16[8,112,768]{2,1,0:T(8,128)(2,1)}), bf16[8,112,768]{2,1,0:T(8,128)(2,1)S(1)}, u32[]{:S(2)}, u32[]{:S(2)}) async-start(bf16[8,112,768]{2,1,0:T(8,128)(2,1)} %broadcast_in_dim.47), calls=%async_computation.8 | async-start | bytes 2752512 | tf_op jit(solution)/shard_map/all_to_all | solution.py:311
  275.8 0.8 copy-done.9
  276.5 0.8 add.66
  277.3 15.2 %all-to-all-done.7 = bf16[8,112,768]{2,1,0:T(8,128)(2,1)S(1)} async-done(((bf16[8,112,768]{2,1,0:T(8,128)(2,1)}), bf16[8,112,768]{2,1,0:T(8,128)(2,1)S(1)}, u32[]{:S(2)}, u32[]{:S(2)}) %all-to-all-start.7) | async-done | bytes 1376288 | tf_op jit(solution)/shard_map/all_to_all | solution.py:311
  292.8 0.8 fusion.7
  293.6 0.9 slice.109
  294.4 1.1 slice.98
  295.5 2.4 reshape.160
  298.7 1.1 reshape.161
  300.4 0.6 copy.80
  301.0 1.9 reshape.164
  303.3 0.7 copy.81
  304.1 0.7 reshape.167
  (100 shorter events, 7.1 us)
Async XLA Ops:
  7.2 3.2 %copy-start = (bf16[192,768]{1,0:T(8,128)(2,1)S(1)}, bf16[192,768]{1,0:T(8,128)(2,1)}, u32[]{:S(2)}) copy-start(bf16[192,768]{1,0:T(8,128)(2,1)} %param.14) | copy-start | bytes 884740
  7.2 3.2 %copy-start.14 = (bf16[48,768]{1,0:T(8,128)(2,1)S(1)}, bf16[48,768]{1,0:T(8,128)(2,1)}, u32[]{:S(2)}) copy-start(bf16[48,768]{1,0:T(8,128)(2,1)} %param.12) | copy-start | bytes 221188
  7.2 89.9 %all-gather.3.cloned.1.call-start = ((), (), s32[]{:S(2)}) async-start(), calls=%async_computation.10 | async-start | bytes 6266880 | tf_op jit(solution)/shard_map/all_gather | solution.py:334
  7.3 3.9 %copy-start.19 = (bf16[192]{0:T(256)(128)(2,1)S(1)}, bf16[192]{0:T(256)(128)(2,1)}, u32[]{:S(2)}) copy-start(bf16[192]{0:T(256)(128)(2,1)} %param.16) | copy-start | bytes 1156
  7.3 4.0 %copy-start.18 = (bf16[8,48]{1,0:T(8,128)(2,1)S(1)}, bf16[8,48]{1,0:T(8,128)(2,1)}, u32[]{:S(2)}) copy-start(bf16[8,48]{1,0:T(8,128)(2,1)} %param.15) | copy-start | bytes 2308
  7.3 4.1 %copy-start.11 = (bf16[48,2304]{1,0:T(8,128)(2,1)S(1)}, bf16[48,2304]{1,0:T(8,128)(2,1)}, u32[]{:S(2)}) copy-start(bf16[48,2304]{1,0:T(8,128)(2,1)} %param.11) | copy-start | bytes 663556
  11.2 20.5 %copy-start.6 = (bf16[128,768]{1,0:T(8,128)(2,1)S(1)}, bf16[128,768]{1,0:T(8,128)(2,1)}, u32[]{:S(2)}) copy-start(bf16[128,768]{1,0:T(8,128)(2,1)} %tokens.1) | copy-start | bytes 589828
  32.9 8.8 %copy-start.20 = (s32[1,8]{1,0:T(1,128)S(1)}, s32[1,8]{1,0:T(1,128)}, u32[]{:S(2)}) copy-start(s32[1,8]{1,0:T(1,128)} %param.18) | copy-start | bytes 100
  32.9 8.8 %copy-start.21 = (s32[1,3]{1,0:T(1,128)S(1)}, s32[1,3]{1,0:T(1,128)}, u32[]{:S(2)}) copy-start(s32[1,3]{1,0:T(1,128)} %param.17) | copy-start | bytes 40
  33.0 42.9 %all-to-all-start = ((bf16[8,128,768]{2,1,0:T(8,128)(2,1)}), bf16[8,128,768]{2,1,0:T(8,128)(2,1)}, u32[]{:S(2)}, u32[]{:S(2)}) async-start(bf16[8,128,768]{2,1,0:T(8,128)(2,1)} %broadcast_in_dim.41), calls=%async_computation | async-start | bytes 3145728 | tf_op jit(solution)/shard_map/all_to_all | solution.py:311
  41.7 2.0 collective-permute-start
  44.2 31.6 %copy-start.3 = (bf16[8,96,768]{2,1,0:T(8,128)(2,1)}, bf16[8,96,768]{2,1,0:T(8,128)(2,1)S(1)}, u32[]{:S(2)}) copy-start(bf16[8,96,768]{2,1,0:T(8,128)(2,1)S(1)} %maximum_select_fusion) | copy-start | bytes 3538948
  86.6 9.7 %all-to-all-start.2 = ((bf16[4,128,192]{1,2,0:T(8,128)(2,1)}), bf16[4,128,192]{1,2,0:T(8,128)(2,1)S(1)}, u32[]{:S(2)}, u32[]{:S(2)}) async-start(bf16[4,128,192]{1,2,0:T(8,128)(2,1)} %copy.67), calls=%async_computation.2 | async-start | bytes 393216 | tf_op jit(solution)/shard_map/all_to_all | solution.py:311
  90.0 140.3 %reduce-scatter.2.cloned.1.call-start = ((), (), s32[]{:S(2)}) async-start(), calls=%async_computation.9 | async-start | bytes 6266880 | tf_op jit(solution)/shard_map/reduce_scatter | solution.py:413
  101.4 5.9 %collective-permute-start.1 = (bf16[128,768]{1,0:T(8,128)(2,1)}, bf16[128,768]{1,0:T(8,128)(2,1)S(1)}, u32[]{:S(2)}, u32[]{:S(2)}) collective-permute-start(bf16[128,768]{1,0:T(8,128)(2,1)} %get-tuple-element.38.mine.low_mine), channel_id=1, source_target_pairs={{0,2},{1,3},{2,0},{3,1},{4,6},{5,7},{6,4},{7,5},{8,10},{9,11},{10,... | collective-permute-start | bytes 589832 | tf_op jit(solution)/shard_map/ppermute | solution.py:307
  107.3 0.7 copy-start.5
  113.4 5.9 %collective-permute-start.2 = (bf16[128,768]{1,0:T(8,128)(2,1)}, bf16[128,768]{1,0:T(8,128)(2,1)S(1)}, u32[]{:S(2)}, u32[]{:S(2)}) collective-permute-start(bf16[128,768]{1,0:T(8,128)(2,1)} %get-tuple-element.40), channel_id=1, source_target_pairs={{0,2},{1,3},{2,0},{3,1},{4,6},{5,7},{6,4},{7,5},{8,10},{9,11},{10,... | collective-permute-start | bytes 589832 | tf_op jit(solution)/shard_map/ppermute | solution.py:307
  119.3 0.7 copy-start.12
  122.4 5.9 %collective-permute-start.3 = (bf16[128,768]{1,0:T(8,128)(2,1)}, bf16[128,768]{1,0:T(8,128)(2,1)S(1)}, u32[]{:S(2)}, u32[]{:S(2)}) collective-permute-start(bf16[128,768]{1,0:T(8,128)(2,1)} %get-tuple-element.43.mine), channel_id=1, source_target_pairs={{0,2},{1,3},{2,0},{3,1},{4,6},{5,7},{6,4},{7,5},{8,10},{9,11},{10,... | collective-permute-start | bytes 589832 | tf_op jit(solution)/shard_map/ppermute | solution.py:307
  128.3 0.7 copy-start.4
  134.6 5.9 %collective-permute-start.4 = (bf16[128,768]{1,0:T(8,128)(2,1)}, bf16[128,768]{1,0:T(8,128)(2,1)S(1)}, u32[]{:S(2)}, u32[]{:S(2)}) collective-permute-start(bf16[128,768]{1,0:T(8,128)(2,1)} %get-tuple-element.46), channel_id=1, source_target_pairs={{0,2},{1,3},{2,0},{3,1},{4,6},{5,7},{6,4},{7,5},{8,10},{9,11},{10,... | collective-permute-start | bytes 589832 | tf_op jit(solution)/shard_map/ppermute | solution.py:307
  140.5 0.7 copy-start.13
  141.2 5.4 %copy-start.2 = (bf16[16,192,768]{2,1,0:T(8,128)(2,1)S(1)}, bf16[16,192,768]{2,1,0:T(8,128)(2,1)}, u32[]{:S(2)}) copy-start(bf16[16,192,768]{2,1,0:T(8,128)(2,1)} %feed_grad.1) | copy-start | bytes 14155780
  150.9 0.9 copy-start.10
  150.9 5.2 %copy-start.15 = (f32[3,768]{1,0:T(4,128)S(1)}, f32[3,768]{1,0:T(4,128)}, u32[]{:S(2)}) copy-start(f32[3,768]{1,0:T(4,128)} %get-tuple-element.62) | copy-start | bytes 27652
  150.9 5.3 %copy-start.17 = (f32[1,1536]{1,0:T(1,128)S(1)}, f32[1,1536]{1,0:T(1,128)}, u32[]{:S(2)}) copy-start(f32[1,1536]{1,0:T(1,128)} %get-tuple-element.63) | copy-start | bytes 18436
  150.9 5.7 %copy-start.16 = (f32[3,768]{1,0:T(4,128)S(1)}, f32[3,768]{1,0:T(4,128)}, u32[]{:S(2)}) copy-start(f32[3,768]{1,0:T(4,128)} %get-tuple-element.61) | copy-start | bytes 27652
  152.6 9.7 %all-to-all-start.3 = ((bf16[4,128,192]{1,2,0:T(8,128)(2,1)}), bf16[4,128,192]{1,2,0:T(8,128)(2,1)S(1)}, u32[]{:S(2)}, u32[]{:S(2)}) async-start(bf16[4,128,192]{1,2,0:T(8,128)(2,1)} %copy.75), calls=%async_computation.3 | async-start | bytes 393216 | tf_op jit(solution)/shard_map/all_to_all | solution.py:311
  177.0 2.1 collective-permute-start.5
  180.1 51.2 %all-to-all-start.6 = ((bf16[8,48,768]{2,1,0:T(8,128)(2,1)}), bf16[8,48,768]{2,1,0:T(8,128)(2,1)S(1)}, u32[]{:S(2)}, u32[]{:S(2)}) async-start(bf16[8,48,768]{2,1,0:T(8,128)(2,1)} %fusion), calls=%async_computation.7 | async-start | bytes 1179648 | tf_op jit(solution)/shard_map/all_to_all | solution.py:311
  247.4 23.1 %all-to-all-start.4 = ((bf16[8,128,768]{2,1,0:T(8,128)(2,1)}), bf16[8,128,768]{2,1,0:T(8,128)(2,1)S(1)}, u32[]{:S(2)}, u32[]{:S(2)}) async-start(bf16[8,128,768]{2,1,0:T(8,128)(2,1)} %get-tuple-element.55), calls=%async_computation.4 | async-start | bytes 3145728 | tf_op jit(solution)/shard_map/all_to_all | solution.py:311
  271.7 20.8 %all-to-all-start.7 = ((bf16[8,112,768]{2,1,0:T(8,128)(2,1)}), bf16[8,112,768]{2,1,0:T(8,128)(2,1)S(1)}, u32[]{:S(2)}, u32[]{:S(2)}) async-start(bf16[8,112,768]{2,1,0:T(8,128)(2,1)} %broadcast_in_dim.47), calls=%async_computation.8 | async-start | bytes 2752512 | tf_op jit(solution)/shard_map/all_to_all | solution.py:311
  275.5 1.0 copy-start.9
  298.3 1.5 copy-start.8
  298.3 1.7 copy-start.7
  301.0 3.8 %copy-start.1 = (bf16[192,768]{1,0:T(8,128)(2,1)S(1)}, bf16[192,768]{1,0:T(8,128)(2,1)}, u32[]{:S(2)}) copy-start(bf16[192,768]{1,0:T(8,128)(2,1)} %param.14) | copy-start | bytes 884740
Sparse Core Ops, SparseCore 0:
  11.3 59.5 all-gather.2
  151.0 79.2 reduce-scatter.1

commit v2 on v1

v2 whole, which is shorter than its diff:
```python
import jax
import jax.numpy as jnp
from jax import lax
from jax.experimental import pallas as pl
from jax.experimental.pallas import tpu as pltpu
from jax.sharding import PartitionSpec as P

D = 768
HD = 64
BLK = 128
NBLK = 8
SEQS = 3
SLOTS = 4
LOCAL = 3
WIDE = LOCAL * HD
FF = 3072
HALF = FF // 2
F = 16

epsilon = 1e-12
masked_fill = -1e30
root_half = 0.7071067811865476
inv_root_tau = 0.3989422804014327

bf16 = jnp.bfloat16
f32 = jnp.float32

VM = pl.BlockSpec(memory_space=pltpu.VMEM)
SM = pl.BlockSpec(memory_space=pltpu.SMEM)
HB = pl.BlockSpec(memory_space=pltpu.HBM)
EXTRA = 640


def params(mib):
    return pltpu.CompilerParams(vmem_limit_bytes=mib * 1024 * 1024)


def nn(a, b):
    return lax.dot_general(a, b, (((1,), (0,)), ((), ())), preferred_element_type=f32)


def nt(a, b):
    return lax.dot_general(a, b, (((1,), (1,)), ((), ())), preferred_element_type=f32)


def tn(a, b):
    return lax.dot_general(a, b, (((0,), (0,)), ((), ())), preferred_element_type=f32)


def call(kernel, name, out_shape, in_specs, scratch=(), flops=0, nbytes=0, out_specs=None, mib=16):
    return pl.pallas_call(
        kernel,
        out_shape=out_shape,
        in_specs=in_specs,
        out_specs=jax.tree.map(lambda _: VM, out_shape) if out_specs is None else out_specs,
        scratch_shapes=list(scratch),
        compiler_params=params(mib),
        cost_estimate=pl.CostEstimate(flops=flops, bytes_accessed=nbytes, transcendentals=0),
        name=name,
    )


def shape(dims, dtype=f32):
    return jax.ShapeDtypeStruct(dims, dtype)


def places():
    place = lax.axis_index("ctx")
    return lax.rem(place, 2), lax.div(place, 2), lax.rem(lax.axis_index("fsdp"), 2)


def begin(sems, first, *pairs):
    copies = [pltpu.make_async_copy(a, b, sems.at[first + k]) for k, (a, b) in enumerate(pairs)]
    for copy in copies:
        copy.start()
    return copies


def finish(copies):
    for copy in copies:
        copy.wait()


def dma(n):
    return pltpu.SemaphoreType.DMA((n,))


def head_rows(w_mine, w_other, weights, row):
    core = places()[2]
    return (
        (w_mine.at[:, pl.ds(row, 48)], weights.at[:, core]),
        (w_other.at[:, pl.ds(row, 48)], weights.at[:, 1 - core]),
    )


def token_rows(tokens, other, pairs, x):
    xh, zed, _ = places()
    moves = [(tokens, x.at[2 * zed + xh]), (other, x.at[2 * zed + 1 - xh])]
    for k, pair in enumerate(pairs):
        z = zed ^ (k + 1)
        moves += [(pair.at[0], x.at[2 * z + xh]), (pair.at[1], x.at[2 * z + 1 - xh])]
    return moves


def slot_table(block_seq, table):
    xh, _, _ = places()
    for i in range(4):
        own = block_seq[0, 2 * i + xh]
        for k in range(SLOTS):
            table[SLOTS * i + k] = 0
        count = jnp.int32(0)
        for b in range(NBLK):
            same = block_seq[0, b] == own

            @pl.when(same)
            def _(i=i, b=b, count=count):
                table[SLOTS * i + jnp.minimum(count, SLOTS - 1)] = b

            count = count + same.astype(jnp.int32)


def attend_kernel(lengths, block_seq, tokens, other, pair1, pair2, pair3, w_mine, w_other, rows, *refs):
    kept_out, sends, refs = refs[:4], refs[4:8], refs[8:]
    x, own, weights, chances, query, keys, values, mixture, table, sems = refs
    loads = begin(sems, 0, *token_rows(tokens, other, (pair1, pair2, pair3), x))
    loads += begin(sems, 13, (tokens, own.at[places()[1]]))
    loads += begin(
        sems, 14, *((pair.at[0], own.at[places()[1] ^ (k + 1)]) for k, pair in enumerate((pair1, pair2, pair3)))
    )
    loads += begin(sems, 8, *head_rows(w_mine, w_other, weights, 0))
    slot_table(block_seq, table)
    xh, zed, core = places()
    finish(loads)
    w = weights[...].reshape(D, D)
    rows[...] = jnp.transpose(w[:, EXTRA:].astype(f32))[:16]
    bias = jnp.zeros((2, WIDE), f32)
    for z in range(4):
        bias = jnp.where(zed == z, rows[0:2, WIDE * z : WIDE * z + WIDE], bias)
    xs = x[...].reshape(NBLK * BLK, D)
    key_all = nn(xs, w[:, WIDE : 2 * WIDE]).astype(bf16)
    value_all = (nn(xs, w[:, 2 * WIDE : 3 * WIDE]) + bias[1:2, :]).astype(bf16)
    for h in range(LOCAL):
        keys[h] = key_all[:, HD * h : HD * h + HD]
        values[h] = value_all[:, HD * h : HD * h + HD]
    q_all = (nn(own[...].reshape(4 * BLK, D), w[:, :WIDE]) + bias[0:1, :]).astype(bf16) * bf16(HD**-0.5)
    for h in range(LOCAL):
        query[h] = q_all[:, HD * h : HD * h + HD]
    stores = begin(sems, 10, *zip((query, keys, values), kept_out[1:]))
    lane = lax.broadcasted_iota(jnp.int32, (1, BLK), 1)
    for i in range(4):
        length = lengths[0, block_seq[0, 2 * i + xh]]
        blank = jnp.concatenate(
            [jnp.where(lane < length - BLK * k, 0.0, masked_fill) for k in range(SLOTS)], axis=1
        )
        picks = [pl.ds(pl.multiple_of(table[SLOTS * i + k] * BLK, BLK), BLK) for k in range(SLOTS)]
        outs = []
        for h in range(LOCAL):
            key_h = jnp.concatenate([keys[h, p, :] for p in picks], axis=0)
            value_h = jnp.concatenate([values[h, p, :] for p in picks], axis=0)
            scores = nt(query[h, BLK * i : BLK * i + BLK, :], key_h) + blank
            peak = jnp.max(scores, axis=-1, keepdims=True)
            raised = jnp.exp(scores - peak)
            share = (raised * (1.0 / jnp.sum(raised, axis=-1, keepdims=True))).astype(bf16)
            chances[i, h] = share
            outs.append(nn(share, value_h))
        mixture[zed ^ i] = jnp.concatenate(outs, axis=1).astype(bf16)
    stores += begin(sems, 0, *((mixture.at[k], out) for k, out in enumerate(sends)), (chances, kept_out[0]))
    finish(stores)


KEPT = (
    shape((4, LOCAL, BLK, SLOTS * BLK), bf16),
    shape((LOCAL, 4 * BLK, HD), bf16),
    shape((LOCAL, NBLK * BLK, HD), bf16),
    shape((LOCAL, NBLK * BLK, HD), bf16),
)
KEPT_VMEM = [pltpu.VMEM(one.shape, one.dtype) for one in KEPT]


def attend(lengths, block_seq, blocks, w_mine, w_other):
    return call(
        attend_kernel,
        "attend",
        (shape((16, D)),) + KEPT + (shape((BLK, WIDE), bf16),) * 4,
        [SM, SM] + [HB] * 7,
        [pltpu.VMEM((NBLK, BLK, D), bf16), pltpu.VMEM((4, BLK, D), bf16), pltpu.VMEM((8, 2, 48, D), bf16)]
        + KEPT_VMEM
        + [pltpu.VMEM((4, BLK, WIDE), bf16), pltpu.SMEM((4 * SLOTS,), jnp.int32), dma(17)],
        mib=56,
        flops=2 * 10**9,
        nbytes=6 * 10**6,
        out_specs=(VM,) + (HB,) * 8,
    )(lengths, block_seq, *blocks, w_mine, w_other)


def attend_back_kernel(block_seq, w_mine, w_other, *refs):
    cots, kept, refs = refs[:4], refs[4:8], refs[8:]
    query_out, key_out, value_out, part0, part1, part2, part3, weights, chances, query, keys, values = refs[:12]
    table, key_acc, value_acc, cot, partial, sems = refs[12:]
    xh, zed, core = places()
    loads = begin(sems, 0, *((one, cot.at[zed ^ k]) for k, one in enumerate(cots)))
    loads += begin(sems, 4, *zip(kept, (chances, query, keys, values)))
    late = begin(sems, 8, *head_rows(w_mine, w_other, weights, 0))
    slot_table(block_seq, table)
    key_acc[...] = jnp.zeros_like(key_acc)
    value_acc[...] = jnp.zeros_like(value_acc)
    finish(loads)
    query_cots = []
    for i in range(4):
        picks = [pl.ds(pl.multiple_of(table[SLOTS * i + k] * BLK, BLK), BLK) for k in range(SLOTS)]
        parts = []
        cot_i = cot[i]
        for h in range(LOCAL):
            key_h = jnp.concatenate([keys[h, p, :] for p in picks], axis=0)
            value_h = jnp.concatenate([values[h, p, :] for p in picks], axis=0)
            cot_h = cot_i[:, HD * h : HD * h + HD]
            share_low = chances[i, h]
            share = share_low.astype(f32)
            chance_cot = nt(cot_h, value_h)
            inner = jnp.sum(share * chance_cot, axis=-1, keepdims=True)
            score_cot = (share * (chance_cot - inner)).astype(bf16)
            parts.append(nn(score_cot, key_h))
            key_part = tn(score_cot, query[h, BLK * i : BLK * i + BLK, :])
            value_part = tn(share_low, cot_h)
            for k, p in enumerate(picks):
                key_acc[h, p, :] += key_part[BLK * k : BLK * k + BLK]
                value_acc[h, p, :] += value_part[BLK * k : BLK * k + BLK]
        query_cots.append((jnp.concatenate(parts, axis=1) * HD**-0.5).astype(bf16))
    query_cot = jnp.concatenate(query_cots, axis=0)
    key_cot = jnp.concatenate([key_acc[h] for h in range(LOCAL)], axis=1).astype(bf16)
    value_cot = jnp.concatenate([value_acc[h] for h in range(LOCAL)], axis=1).astype(bf16)
    query_out[...] = query_cot
    key_out[...] = key_cot
    value_out[...] = value_cot
    finish(late)
    w = weights[...].reshape(D, D)
    key_value = nt(key_cot, w[:, WIDE : 2 * WIDE]) + nt(value_cot, w[:, 2 * WIDE : 3 * WIDE])
    query_part = nt(query_cot, w[:, :WIDE])
    for i in range(4):
        row = BLK * 2 * i
        mine_q = query_part[BLK * i : BLK * i + BLK]
        partial[zed ^ i, 0] = (
            jnp.where(xh == 0, key_value[row : row + BLK], key_value[row + BLK : row + 2 * BLK]) + mine_q
        ).astype(bf16)
        partial[zed ^ i, 1] = jnp.where(
            xh == 0, key_value[row + BLK : row + 2 * BLK], key_value[row : row + BLK]
        ).astype(bf16)
    stores = begin(sems, 0, *((partial.at[k], out) for k, out in enumerate((part0, part1, part2, part3))))
    finish(stores)


def attend_back(block_seq, w_mine, w_other, cots, kept):
    return call(
        attend_back_kernel,
        "attend_back",
        (shape((4 * BLK, WIDE), bf16), shape((NBLK * BLK, WIDE), bf16), shape((NBLK * BLK, WIDE), bf16))
        + (shape((2, BLK, D), bf16),) * 4,
        [SM] + [HB] * 10,
        [pltpu.VMEM((8, 2, 48, D), bf16)]
        + KEPT_VMEM
        + [
            pltpu.SMEM((4 * SLOTS,), jnp.int32),
            pltpu.VMEM((LOCAL, NBLK * BLK, HD), f32),
            pltpu.VMEM((LOCAL, NBLK * BLK, HD), f32),
            pltpu.VMEM((4, BLK, WIDE), bf16),
            pltpu.VMEM((4, 2, BLK, D), bf16),
            dma(10),
        ],
        mib=56,
        flops=4 * 10**9,
        nbytes=8 * 10**6,
        out_specs=(VM,) * 3 + (HB,) * 4,
    )(block_seq, w_mine, w_other, *cots, *kept)


def head_grad_kernel(
    tokens, other, pair1, pair2, pair3, query, keys, values, first_sums, second_sums, up_sums,
    mine, send, x, packed, sems,
):
    loads = begin(sems, 0, *token_rows(tokens, other, (pair1, pair2, pair3), x))
    xh, zed, core = places()
    query_cot, key_cot, value_cot = query[...], keys[...], values[...]
    finish(loads)
    xs = x[...].reshape(NBLK * BLK, D)
    xq = jnp.concatenate([x[2 * i + xh] for i in range(4)], axis=0)
    grads = jnp.concatenate(
        [tn(xq, query_cot), tn(xs, key_cot), tn(xs, value_cot), jnp.zeros((D, EXTRA - 3 * WIDE), f32)], axis=1
    ).astype(bf16)
    lane = lax.broadcasted_iota(jnp.int32, (2, D), 1)
    edge = zed * WIDE
    inside = (lane >= edge) & (lane < edge + WIDE)
    own = jnp.concatenate(
        [
            jnp.sum(query_cot.astype(f32), axis=0, keepdims=True),
            jnp.sum(value_cot.astype(f32), axis=0, keepdims=True),
        ],
        axis=0,
    )
    own = jnp.where(inside, jnp.concatenate([own] * 4, axis=1), 0.0)
    vec = jnp.concatenate(
        [first_sums[0:1], second_sums[0:1], first_sums[1:3], second_sums[1:3], up_sums[...]], axis=0
    )
    extra = jnp.concatenate([own, vec, jnp.zeros((118, D), f32)], axis=0)
    extra = jnp.transpose(extra).astype(bf16)
    for f in range(F):
        slot = core if f % 2 == 0 else 1 - core
        packed[slot, f // 2, :, :EXTRA] = grads[48 * f : 48 * f + 48]
        packed[slot, f // 2, :, EXTRA:] = extra[48 * f : 48 * f + 48]
    stores = begin(sems, 0, (packed.at[1], send), (packed.at[0], mine))
    finish(stores)


def head_grad(blocks, cots, sums):
    half = shape((8, 48, D), bf16)
    return call(
        head_grad_kernel,
        "head_grad",
        (half, half),
        [HB] * 5 + [VM] * 6,
        [pltpu.VMEM((NBLK, BLK, D), bf16), pltpu.VMEM((2, 8, 48, D), bf16), dma(8)],
        mib=56,
        flops=2 * 10**9,
        nbytes=4 * 10**6,
        out_specs=(HB, HB),
    )(*blocks, *cots, *sums)


def centred(hidden):
    centre = hidden - jnp.mean(hidden, axis=-1, keepdims=True)
    inverse = lax.rsqrt(jnp.mean(centre * centre, axis=-1, keepdims=True) + epsilon)
    return centre * inverse, inverse


def norm_back(scaled, hat, inverse):
    return inverse * (
        scaled
        - jnp.mean(scaled, axis=-1, keepdims=True)
        - hat * jnp.mean(scaled * hat, axis=-1, keepdims=True)
    )


def pack_kernel(vectors, b_up, w_qkv, w_out, w_up, w_down, heads, feed, heads_own, feed_own, qkv, up, sems):
    xh, zed, core = places()
    half = lax.rem(zed, 2)
    start = pl.multiple_of(96 * half, 32)
    loads = begin(
        sems,
        0,
        (w_qkv, qkv),
        (w_up, up),
        (w_out, heads_own.at[pl.ds(48, 48)]),
        (w_down.at[pl.ds(start, 96)], feed_own.at[pl.ds(0, 96)]),
    )
    bias = b_up[...].astype(f32)
    small = jnp.concatenate([vectors[...].astype(f32)] + [bias[:, 48 * e : 48 * e + 48] for e in range(4)], axis=0)
    small = jnp.concatenate([small, jnp.zeros((12, 80), f32)], axis=1)
    small = jnp.concatenate([small, jnp.zeros((116, 128), f32)], axis=0)
    heads_own[0:48, EXTRA:] = jnp.transpose(small)[:48].astype(bf16)
    heads_own[0:48, 3 * WIDE : EXTRA] = jnp.zeros((48, EXTRA - 3 * WIDE), bf16)
    loads[0].wait()
    for z in range(4):

        @pl.when(zed == z)
        def _(z=z):
            heads_own[0:48, : 3 * WIDE] = jnp.concatenate(
                [qkv[:, D * t + WIDE * z : D * t + WIDE * z + WIDE] for t in range(3)], axis=1
            )

    loads[2].wait()
    stores = begin(sems, 4, *((heads_own, heads.at[k]) for k in range(8)))
    loads[1].wait()
    for h in range(2):

        @pl.when(half == h)
        def _(h=h):
            for e in range(2):
                first = 96 * h + 48 * e
                feed_own[96 + 48 * e : 144 + 48 * e, :] = jnp.concatenate(
                    [up[:, 192 * f + first : 192 * f + first + 48] for f in range(F)], axis=1
                )

    loads[3].wait()
    stores += begin(sems, 12, *((feed_own, feed.at[k]) for k in range(8)))
    finish(stores)


def first_kernel(mix0, mix1, mix2, mix3, w_mine, w_other, vectors, tokens, low, norm, hat, *scratch):
    weights, mixes, norm_own, hat_own, sems = scratch
    xh, zed, core = places()
    loads = begin(sems, 0, *((mix, mixes.at[k]) for k, mix in enumerate((mix0, mix1, mix2, mix3))))
    loads += begin(sems, 4, *head_rows(w_mine, w_other, weights, 48))
    total = tokens[...].astype(f32) + vectors[2:3]
    finish(loads)
    for k in range(4):
        total += nn(mixes[k], weights[pl.ds(2 * (zed ^ k), 2)].reshape(WIDE, D))
    first_hat, first_inv = centred(total)
    first_norm = first_hat * vectors[4:5] + vectors[5:6]
    low[...] = first_norm.astype(bf16)
    norm_own[...] = first_norm
    hat_own[:, :D] = first_hat
    hat_own[:, D:] = jnp.broadcast_to(first_inv, (BLK, 128))
    finish(begin(sems, 0, (norm_own, norm), (hat_own, hat)))


def load_feed(w_mine, w_other, weights, sems, order):
    core = places()[2]
    loads = {}
    for k in order:
        rows = pl.ds(48 * k, 48)
        loads[k] = begin(
            sems,
            2 * k,
            (w_mine.at[:, rows], weights.at[k, :, core]),
            (w_other.at[:, rows], weights.at[k, :, 1 - core]),
        )
    return loads


def feed_kernel(mine, other, w_mine, w_other, vectors, activ, slope, keep, send, weights, sems):
    loads = load_feed(w_mine, w_other, weights, sems, (2, 0, 3, 1))
    rows = jnp.concatenate([mine[...], other[...]], axis=0)
    b_up = jnp.where(lax.rem(places()[1], 2) == 0, vectors[8:10], vectors[10:12])
    total = None
    for e in range(2):
        finish(loads[2 + e])
        up = nn(rows, weights[2 + e].reshape(D, D)) + b_up[e : e + 1, :]
        erf = lax.erf(up * root_half)
        low = (0.5 * up * (1.0 + erf)).astype(bf16)
        activ[:, D * e : D * e + D] = low
        slope[:, D * e : D * e + D] = (
            0.5 * (1.0 + erf) + up * jnp.exp(-0.5 * up * up) * inv_root_tau
        ).astype(bf16)
        finish(loads[e])
        part = nn(low, weights[e].reshape(D, D))
        total = part if total is None else total + part
    keep[...] = total[:BLK]
    send[...] = total[BLK:].astype(bf16)


def second_kernel(norm, keep, came, vectors, out_grad, layer_out, cot, low, sums):
    second_sum = norm[...] + (keep[...] + came[...].astype(f32)) + vectors[3:4]
    second_hat, second_inv = centred(second_sum)
    layer_out[...] = (second_hat * vectors[6:7] + vectors[7:8]).astype(bf16)
    out_cot = out_grad[...].astype(f32)
    second_cot = norm_back(out_cot * vectors[6:7], second_hat, second_inv)
    cot[...] = second_cot
    down_cot = second_cot.astype(bf16)
    low[...] = down_cot
    sums[0:1] = jnp.sum(down_cot.astype(f32), axis=0, keepdims=True)
    sums[1:2] = jnp.sum(out_cot * second_hat, axis=0, keepdims=True)
    sums[2:3] = jnp.sum(out_cot, axis=0, keepdims=True)


def feed_back_kernel(mine, other, w_mine, w_other, slope, up_cot, keep, send, sums, weights, sems):
    loads = load_feed(w_mine, w_other, weights, sems, (0, 2, 1, 3))
    rows = jnp.concatenate([mine[...], other[...]], axis=0)
    total = None
    for e in range(2):
        finish(loads[e] + loads[2 + e])
        w_down = weights[e].reshape(D, D)
        w_up = weights[2 + e].reshape(D, D)
        low = (nt(rows, w_down) * slope[:, D * e : D * e + D].astype(f32)).astype(bf16)
        up_cot[:, D * e : D * e + D] = low
        sums[e : e + 1, :] = jnp.sum(low.astype(f32), axis=0, keepdims=True)
        part = nt(low, w_up)
        total = part if total is None else total + part
    keep[...] = total[:BLK]
    send[...] = total[BLK:].astype(bf16)


def feed_grad_kernel(mine, other, low_mine, low_other, activ, up_cot, keep, send, packed, sems):
    xh, zed, core = places()
    down_cot = jnp.concatenate([mine[...], other[...]], axis=0)
    first_low = jnp.concatenate([low_mine[...], low_other[...]], axis=0)
    for e in range(2):
        down = tn(activ[:, D * e : D * e + D], down_cot).astype(bf16)
        up = tn(first_low, up_cot[:, D * e : D * e + D]).astype(bf16)
        for f in range(F):
            slot = core if f % 2 == 0 else 1 - core
            packed[slot, f // 2, 48 * e : 48 * e + 48, :] = down[48 * f : 48 * f + 48]
            packed[slot, f // 2, 96 + 48 * e : 144 + 48 * e, :] = up[48 * f : 48 * f + 48]
    finish(begin(sems, 0, (packed.at[1], send), (packed.at[0], keep)))


def first_back_kernel(
    cot, keep, came, vectors, hat, w_mine, w_other, mix0, mix1, mix2, mix3,
    input_cot, grad_keep, grad_send, back0, back1, back2, back3, sums,
    weights, mixes, hats, total_own, back, packed, sems,
):
    xh, zed, core = places()
    load_hat = begin(sems, 0, (hat, hats))
    loads = begin(sems, 1, *head_rows(w_mine, w_other, weights, 48))
    late = begin(sems, 3, *((mix, mixes.at[k]) for k, mix in enumerate((mix0, mix1, mix2, mix3))))
    first_cot = cot[...] + (keep[...] + came[...].astype(f32))
    finish(load_hat)
    first_hat = hats[:, :D]
    total = norm_back(first_cot * vectors[4:5], first_hat, hats[:, D : D + 1])
    total_own[...] = total
    attend_cot = total.astype(bf16)
    finish(loads)
    stores = begin(sems, 7, (total_own, input_cot))
    for k, out in enumerate((back0, back1, back2, back3)):
        back[k] = nt(attend_cot, weights[pl.ds(2 * (zed ^ k), 2)].reshape(WIDE, D)).astype(bf16)
        stores += begin(sems, 8 + k, (back.at[k], out))
    finish(late)
    for k in range(4):
        grads = tn(mixes[k], attend_cot).astype(bf16)
        for j in range(4):
            slot = core if j % 2 == 0 else 1 - core
            packed[slot, 2 * (zed ^ k) + j // 2] = grads[48 * j : 48 * j + 48]
    stores += begin(sems, 12, (packed.at[1], grad_send), (packed.at[0], grad_keep))
    sums[0:1] = jnp.sum(attend_cot.astype(f32), axis=0, keepdims=True)
    sums[1:2] = jnp.sum(first_cot * first_hat, axis=0, keepdims=True)
    sums[2:3] = jnp.sum(first_cot, axis=0, keepdims=True)
    finish(stores)


def pair_kernel(feed_keep, feed_came, out_keep, out_came, pair):
    pair[:, 0:192, :] = (feed_keep[...].astype(f32) + feed_came[...].astype(f32)).astype(bf16)
    pair[:, 192:240, :] = (out_keep[...].astype(f32) + out_came[...].astype(f32)).astype(bf16)


def feed_sum_kernel(parts, out0, out1, out2, out3, slots, sems):
    xh, zed, core = places()
    member = 2 * lax.div(zed, 2) + xh
    for m in range(4):
        rows = 64 if m < 3 else 48
        total = parts[0, 64 * m : 64 * m + rows, :].astype(f32)
        for chip in range(1, 8):
            total += parts[chip, 64 * m : 64 * m + rows, :].astype(f32)
        slots[member ^ m, 0:rows, :] = total.astype(bf16)
        if rows < 64:
            slots[member ^ m, rows:64, :] = jnp.zeros((64 - rows, D), bf16)
    finish(begin(sems, 0, *((slots.at[k], out) for k, out in enumerate((out0, out1, out2, out3)))))


def last_sum_kernel(heads, part0, part1, part2, part3, copies, total, sems):
    quarter = part0[...].astype(f32)
    for part in (part1, part2, part3):
        quarter += part[...].astype(f32)
    total[0:64, :] = quarter.astype(bf16)
    whole = heads[0].astype(f32)
    for chip in range(1, 8):
        whole += heads[chip].astype(f32)
    total[64:112, :] = whole.astype(bf16)
    finish(begin(sems, 0, *((total, copies.at[k]) for k in range(NBLK))))


def unpack_kernel(every, qkv, out, up, down, vectors, bias):
    ups = []
    for h in range(2):
        quarters = [every[4 * (m // 2) + 2 * h + m % 2, 0:64, :].astype(f32) for m in range(4)]
        whole = jnp.concatenate(quarters, axis=0)
        down[96 * h : 96 * h + 96, :] = whole[0:96]
        ups.append([whole[96:144], whole[144:192]])
        out[...] = whole[192:240] if h == 0 else out[...] + whole[192:240]
    up[...] = jnp.concatenate(
        [ups[h][e][:, 48 * f : 48 * f + 48] for f in range(F) for h in range(2) for e in range(2)], axis=1
    )
    heads = [every[2 * z, 64:112, :].astype(f32) + every[2 * z + 1, 64:112, :].astype(f32) for z in range(4)]
    for t in range(3):
        qkv[:, D * t : D * t + D] = jnp.concatenate(
            [heads[z][:, WIDE * t : WIDE * t + WIDE] for z in range(4)], axis=1
        )
    both = [heads[h][:, EXTRA:] + heads[2 + h][:, EXTRA:] for h in range(2)]
    small = [jnp.transpose(jnp.concatenate([one, jnp.zeros((80, 128), f32)], axis=0)) for one in both]
    vectors[...] = (small[0] + small[1])[0:8, 0:48]
    bias[...] = jnp.concatenate([small[0][8:10], small[1][8:10]], axis=0)[:, 0:48]


CHIPS = [[i for i in range(F) if i % 2 == k] for k in range(2)]


def swap(x, axis, size, bit):
    return lax.ppermute(x, axis, [(i, i ^ bit) for i in range(size)])


def a2a(x, axis, groups=None):
    return lax.all_to_all(x, axis, 0, 0, tiled=True, axis_index_groups=groups)


def body(tokens, w_qkv, w_out, w_up, w_down, vectors, b_up, lengths, block_seq, out_grad):
    after = lax.optimization_barrier

    token_other = swap(tokens, "ctx", NBLK, 1)
    token_other, vectors = after((token_other, vectors))
    pair = jnp.stack([tokens, token_other])
    pairs = [swap(pair, "ctx", NBLK, 2 * k) for k in (1, 2, 3)]
    heads_out, feed_out = call(
        pack_kernel,
        "pack",
        (shape((8, 96, D), bf16), shape((8, 192, D), bf16)),
        [VM, VM] + [HB] * 4,
        [
            pltpu.VMEM((96, D), bf16),
            pltpu.VMEM((192, D), bf16),
            pltpu.VMEM((48, 3 * D), bf16),
            pltpu.VMEM((48, FF), bf16),
            dma(20),
        ],
        mib=56,
        flops=10**6,
        nbytes=5 * 10**6,
        out_specs=(HB, HB),
    )(vectors, b_up.reshape(1, 192), w_qkv, w_out, w_up, w_down)
    w1_mine = a2a(heads_out, "fsdp", CHIPS)
    w1_mine, feed_out, *pairs = after((w1_mine, feed_out, *pairs))
    w2_mine = a2a(feed_out, "fsdp", CHIPS)
    w1_other = swap(w1_mine, "fsdp", F, 1)

    blocks = [tokens, token_other, *pairs]
    rows, *kept, mix0, mix1, mix2, mix3 = attend(lengths, block_seq, blocks, w1_mine, w1_other)
    mixes = [mix0] + [swap(mix, "ctx", NBLK, 2 * (k + 1)) for k, mix in enumerate((mix1, mix2, mix3))]
    first_low, first_norm, first_hat = call(
        first_kernel,
        "first",
        (shape((BLK, D), bf16), shape((BLK, D)), shape((BLK, D + 128))),
        [HB] * 6 + [VM, VM],
        [
            pltpu.VMEM((8, 2, 48, D), bf16),
            pltpu.VMEM((4, BLK, WIDE), bf16),
            pltpu.VMEM((BLK, D), f32),
            pltpu.VMEM((BLK, D + 128), f32),
            dma(6),
        ],
        flops=2 * BLK * D * D,
        nbytes=4 * 10**6,
        out_specs=(VM, HB, HB),
    )(*mixes, w1_mine, w1_other, rows, tokens)
    low_other = swap(first_low, "ctx", NBLK, 2)
    w2_mine, first_norm = after((w2_mine, first_norm))
    w2_other = swap(w2_mine, "fsdp", F, 1)
    loaded = [pltpu.VMEM((4, 8, 2, 48, D), bf16), dma(8)]
    activ, slope, keep, send = call(
        feed_kernel,
        "feed",
        (shape((2 * BLK, HALF), bf16), shape((2 * BLK, HALF), bf16), shape((BLK, D)), shape((BLK, D), bf16)),
        [VM, VM, HB, HB, VM],
        loaded,
        flops=8 * BLK * D * HALF,
        nbytes=8 * 10**6,
    )(first_low, low_other, w2_mine, w2_other, rows)
    came = swap(send, "ctx", NBLK, 2)
    layer_out, second_cot, down_cot, second_sums = call(
        second_kernel,
        "second",
        (shape((BLK, D), bf16), shape((BLK, D)), shape((BLK, D), bf16), shape((3, D))),
        [VM] * 5,
        flops=10**7,
        nbytes=2 * 10**6,
    )(first_norm, keep, came, rows, out_grad)
    down_other = swap(down_cot, "ctx", NBLK, 2)
    up_cot, keep, send, up_sums = call(
        feed_back_kernel,
        "feed_back",
        (shape((2 * BLK, HALF), bf16), shape((BLK, D)), shape((BLK, D), bf16), shape((2, D))),
        [VM, VM, HB, HB, VM],
        loaded,
        flops=8 * BLK * D * HALF,
        nbytes=8 * 10**6,
    )(down_cot, down_other, w2_mine, w2_other, slope)
    came = swap(send, "ctx", NBLK, 2)
    feed_part = shape((8, 192, D), bf16)
    feed_keep, feed_send = call(
        feed_grad_kernel,
        "feed_grad",
        (feed_part, feed_part),
        [VM] * 6,
        [pltpu.VMEM((2, 8, 192, D), bf16), dma(2)],
        mib=20,
        flops=8 * BLK * D * HALF,
        nbytes=8 * 10**6,
        out_specs=(HB, HB),
    )(down_cot, down_other, first_low, low_other, activ, up_cot)
    feed_send, came = after((feed_send, came))
    feed_came = swap(feed_send, "fsdp", F, 1)
    out_part = shape((8, 48, D), bf16)
    back_part = shape((BLK, WIDE), bf16)
    input_cot, out_keep, out_send, back0, back1, back2, back3, first_sums = call(
        first_back_kernel,
        "first_back",
        (shape((BLK, D)), out_part, out_part, back_part, back_part, back_part, back_part, shape((3, D))),
        [VM] * 4 + [HB] * 7,
        [
            pltpu.VMEM((8, 2, 48, D), bf16),
            pltpu.VMEM((4, BLK, WIDE), bf16),
            pltpu.VMEM((BLK, D + 128), f32),
            pltpu.VMEM((BLK, D), f32),
            pltpu.VMEM((4, BLK, WIDE), bf16),
            pltpu.VMEM((2, 8, 48, D), bf16),
            dma(14),
        ],
        flops=4 * BLK * D * D,
        nbytes=4 * 10**6,
        out_specs=(HB,) * 7 + (VM,),
    )(second_cot, keep, came, rows, first_hat, w1_mine, w1_other, *mixes)
    feed_came, back1 = after((feed_came, back1))
    cots = [back0] + [swap(back, "ctx", NBLK, 2 * (k + 1)) for k, back in enumerate((back1, back2, back3))]
    out_came = swap(out_send, "fsdp", F, 1)

    def add(one, two):
        return (one.astype(f32) + two.astype(f32)).astype(bf16)

    feed_pair = call(pair_kernel, "pair", shape((8, 240, D), bf16), [VM] * 4, mib=56, flops=10**6, nbytes=9 * 10**6)(
        feed_keep, feed_came, out_keep, out_came
    )
    feed_parts = a2a(feed_pair, "fsdp", CHIPS)
    *head_cots, part0, part1, part2, part3 = attend_back(block_seq, w1_mine, w1_other, cots, kept)
    partials = (part0, part1, part2, part3)
    head_keep, head_send = head_grad(blocks, head_cots, (first_sums, second_sums, up_sums))
    head_came = swap(head_send, "fsdp", F, 1)
    token_parts = [swap(partials[k], "ctx", NBLK, 2 * k) for k in (1, 2, 3)]
    head_pair, *token_parts = after((add(head_keep, head_came), *token_parts))
    head_parts = a2a(head_pair, "fsdp", CHIPS)

    part0, part1, part2, part3 = call(
        feed_sum_kernel,
        "feed_sum",
        (shape((64, D), bf16),) * 4,
        [VM],
        [pltpu.VMEM((4, 64, D), bf16), dma(4)],
        mib=56,
        flops=10**6,
        nbytes=3 * 10**6,
        out_specs=(HB,) * 4,
    )(feed_parts)
    parts = [part0] + [swap(part, "ctx", NBLK, bit) for part, bit in ((part1, 1), (part2, 4), (part3, 5))]
    copies = call(
        last_sum_kernel,
        "last_sum",
        shape((NBLK, 112, D), bf16),
        [VM] * 5,
        [pltpu.VMEM((112, D), bf16), dma(NBLK)],
        mib=56,
        flops=10**6,
        nbytes=4 * 10**6,
        out_specs=HB,
    )(head_parts, *parts)
    by_z = partials[0].astype(f32)
    for part in token_parts:
        by_z += part.astype(f32)
    by_z = by_z.astype(bf16)
    tokens_grad = input_cot + by_z[0].astype(f32) + swap(by_z[1], "ctx", NBLK, 1).astype(f32)
    every = a2a(copies, "ctx")
    qkv_grad, out_grad_w, up_grad, down_grad, vectors_grad, bias_grad = call(
        unpack_kernel,
        "unpack",
        (shape((48, 3 * D)), shape((48, D)), shape((48, FF)), shape((192, D)), shape((8, 48)), shape((4, 48))),
        [VM],
        flops=10**6,
        nbytes=4 * 10**6,
    )(every)
    return (layer_out, tokens_grad, qkv_grad, out_grad_w, up_grad, down_grad, vectors_grad, bias_grad.reshape(192))


def solution(mesh):
    by_token = P(("fsdp", "ctx"), None)
    by_row = P("fsdp", None)
    in_specs = (
        by_token, by_row, by_row, by_row, by_row, P(None, "fsdp"), P("fsdp"), by_row, by_row, by_token,
    )
    out_specs = (by_token, by_token, by_row, by_row, by_row, by_row, P(None, "fsdp"), P("fsdp"))
    return jax.shard_map(body, mesh=mesh, in_specs=in_specs, out_specs=out_specs, check_vma=False)
```

time: 316 us -> 233 us (0.74)
  waiting for transfers between devices: 140 us -> 92.8 us
  blocking collectives: 35.2 us -> 0 us
  starting transfers between devices: 29.8 us -> 61.4 us
  local copies, waits for them, and re-layouts: 32.1 us -> 15.5 us
  between operations: 14.7 us -> 0.96 us
  Pallas kernels: 48.8 us -> 56.6 us
  other arithmetic: 11.5 us -> 4.16 us
    all_to_all x6 -> x5, waiting for transfers between devices: 76.4 us -> 1.45 us  [a2a(): return lax.all_to_all(x, axis, 0, 0, tiled=True, axis_index_groups=groups)]
    ppermute x6 -> x26, waiting for transfers between devices: 17.4 us -> 91.3 us  [swap(): return lax.ppermute(x, axis, [(i, i ^ bit) for i in range(size)])]
    reduce_scatter x1 -> x0, waiting for transfers between devices: 45.7 us -> none  [body(): lax.psum_scatter(grads.reshape(F * 240, D), 'fsdp', scatter_dimension=0,...]
    all_to_all x2 -> x0, blocking collectives: 35.2 us -> none  [a2a(): return lax.all_to_all(x, axis, 0, 0, tiled=True, axis_index_groups=groups)]
    ppermute x6 -> x26, starting transfers between devices: 2.36 us -> 33.8 us  [swap(): return lax.ppermute(x, axis, [(i, i ^ bit) for i in range(size)])]
    pallas_call x5 -> x11, Pallas kernels: 35.3 us -> 50.1 us  [the longest x1 11.3 us: attend_back(): call(attend_back_kernel, 'attend_back', (shape((4 * BLK, WIDE), bf16), sh...]
    unnamed x46 -> x86, local copies, waits for them, and re-layouts: 5.25 us -> 13.6 us
    concatenate x6 -> x0, other arithmetic: 7.33 us -> none  [the longest x1 4.21 us: body(): grads = jnp.concatenate([feed_grads, out_grads], axis=1)]
  transfers between devices with their start and end apart: 14 -> 31, of which waited for: 11 -> 21; matrix products, arithmetic and copies ran while one was open for 6% -> 2% of each run, Pallas kernels for 8% -> 16%
where the time goes in v2:
time: 233 us; the launch traced here: 231 us
  waiting for transfers between devices  92.8 us (40%)
  starting transfers between devices  61.4 us (26%)
  Pallas kernels  56.6 us (24%)
  local copies, waits for them, and re-layouts  15.5 us (7%)
  other arithmetic  4.16 us (2%)
    ppermute x26, waiting for transfers between devices, swap(): return lax.ppermute(x, axis, [(i, i ^ bit) for i in range(size)])  91.3 us
    ppermute x26, starting transfers between devices, swap(): return lax.ppermute(x, axis, [(i, i ^ bit) for i in range(size)])  33.8 us
    all_to_all x5, starting transfers between devices, a2a(): return lax.all_to_all(x, axis, 0, 0, tiled=True, axis_index_groups=groups)  27.6 us
    unnamed x86, local copies, waits for them, and re-layouts  13.6 us
    pallas_call x1, Pallas kernels, attend_back(): call(attend_back_kernel, 'attend_back', (shape((4 * BLK, WIDE), bf16), sh...  11.3 us
    pallas_call x1, Pallas kernels, attend(): call(attend_kernel, 'attend', (shape((16, D)),) + KEPT + (shape((BLK, WID...  10.7 us
    pallas_call x1, Pallas kernels, head_grad(): call(head_grad_kernel, 'head_grad', (half, half), [HB] * 5 + [VM] * 6, [p...  5.29 us
    pallas_call x1, Pallas kernels, body(): call(pair_kernel, 'pair', shape((8, 240, D), bf16), [VM] * 4, mib=56, flo...  4.9 us
  transfers between devices with their start and end apart: 31, of which 21 were waited for; matrix products, arithmetic and copies ran while one was open for 2% of the time, Pallas kernels for 16%

profile of v2, /device:TPU:0, one launch (start us, length us, event | category | flops | bytes accessed | tf_op | source)
XLA Modules:
  0.0 231.3 jit_solution(8430748431414041576)
XLA Ops:
  0.6 3.2 %collective-permute-start = (bf16[128,768]{1,0:T(8,128)(2,1)}, bf16[128,768]{1,0:T(8,128)(2,1)S(1)}, u32[]{:S(2)}, u32[]{:S(2)}) collective-permute-start(bf16[128,768]{1,0:T(8,128)(2,1)} %tokens.5), channel_id=1, source_target_pairs={{0,1},{1,0},{2,3},{3,2},{4,5},{5,4},{6,7},{7,6},{8,9},{9,8},{10,11... | collective-permute-start | bytes 589832 | tf_op jit(solution)/shard_map/ppermute | solution.py:575
  3.8 1.2 reshape.24.b_up
  5.0 3.9 %collective-permute-done.other = bf16[128,768]{1,0:T(8,128)(2,1)S(1)} collective-permute-done((bf16[128,768]{1,0:T(8,128)(2,1)}, bf16[128,768]{1,0:T(8,128)(2,1)S(1)}, u32[]{:S(2)}, u32[]{:S(2)}) %collective-permute-start) | collective-permute-done | bytes 196640 | tf_op jit(solution)/shard_map/ppermute | solution.py:575
  8.9 3.8 %pack.1 = (bf16[8,96,768]{2,1,0:T(8,128)(2,1)}, bf16[8,192,768]{2,1,0:T(8,128)(2,1)}) custom-call(bf16[8,48]{1,0:T(8,128)(2,1)} %vectors, bf16[1,192]{1,0:T(2,128)(2,1)} %reshape.24.b_up, bf16[48,2304]{1,0:T(8,128)(2,1)} %w_qkv.1, bf16[48,768]{1,0:T(8,128)(2,1)} %w_out.1, bf16[48,3072]{1,0:T(8,128)(2,1)} %w_up.1, bf16[192,768]{1,0:T(8,128)(2,1)} %w_down.1), custom_call_target="tpu_custom_call" | custom-call | flops 1000000 | bytes 5000000 | tf_op jit(solution)/shard_map/pack/pallas_call | solution.py:589
  12.7 5.6 %all-to-all-start = ((bf16[8,96,768]{2,1,0:T(8,128)(2,1)}), bf16[8,96,768]{2,1,0:T(8,128)(2,1)S(1)}, u32[]{:S(2)}, u32[]{:S(2)}) async-start(bf16[8,96,768]{2,1,0:T(8,128)(2,1)} %get-tuple-element.81), calls=%async_computation | async-start | bytes 2359296 | tf_op jit(solution)/shard_map/all_to_all | solution.py:579
  18.4 4.1 %collective-permute-start.3 = (bf16[2,128,768]{2,1,0:T(8,128)(2,1)S(1)}, bf16[2,128,768]{2,1,0:T(8,128)(2,1)S(1)}, u32[]{:S(2)}, u32[]{:S(2)}) collective-permute-start(bf16[2,128,768]{2,1,0:T(8,128)(2,1)S(1)} %pad_maximum_fusion), channel_id=1, source_target_pairs={{0,6},{1,7},{2,4},{3,5},{4,2},{5,3},{6,0},{7,1},{8,14},{9,15},{10,... | collective-permute-start | bytes 1179656 | tf_op jit(solution)/shard_map/ppermute | solution.py:575
  22.5 0.9 collective-permute-start.1
  23.5 15.4 %collective-permute-done.3.pair3 = bf16[2,128,768]{2,1,0:T(8,128)(2,1)S(1)} collective-permute-done((bf16[2,128,768]{2,1,0:T(8,128)(2,1)S(1)}, bf16[2,128,768]{2,1,0:T(8,128)(2,1)S(1)}, u32[]{:S(2)}, u32[]{:S(2)}) %collective-permute-start.3) | collective-permute-done | bytes 393248 | tf_op jit(solution)/shard_map/ppermute | solution.py:575
  38.9 0.7 collective-permute-done.1.pair1
  40.4 5.4 %all-to-all-start.1 = ((bf16[8,192,768]{2,1,0:T(8,128)(2,1)}), bf16[8,192,768]{2,1,0:T(8,128)(2,1)S(1)}, u32[]{:S(2)}, u32[]{:S(2)}) async-start(bf16[8,192,768]{2,1,0:T(8,128)(2,1)} %get-tuple-element.84), calls=%async_computation.1 | async-start | bytes 4718592 | tf_op jit(solution)/shard_map/all_to_all | solution.py:579
  45.9 2.8 %collective-permute-done.4.w_other = bf16[8,96,768]{2,1,0:T(8,128)(2,1)S(1)} collective-permute-done((bf16[8,96,768]{2,1,0:T(8,128)(2,1)S(1)}, bf16[8,96,768]{2,1,0:T(8,128)(2,1)S(1)}, u32[]{:S(2)}, u32[]{:S(2)}) %collective-permute-start.4) | collective-permute-done | bytes 1179680 | tf_op jit(solution)/shard_map/ppermute | solution.py:575
  48.7 1.1 copy-done.3
  49.8 10.7 %attend.1 = (f32[16,768]{1,0:T(8,128)}, bf16[4,3,128,512]{3,2,1,0:T(8,128)(2,1)}, bf16[3,512,64]{2,1,0:T(8,128)(2,1)}, bf16[3,1024,64]{2,1,0:T(8,128)(2,1)}, bf1...) custom-call(s32[1,3]{1,0:T(1,128)} %lengths.1, ...), custom_call_target="tpu_custom_call" | custom-call | flops 2000000000 | bytes 6000000 | tf_op jit(solution)/shard_map/attend/pallas_call | solution.py:181
  60.6 1.2 collective-permute-start.5
  61.7 3.3 %collective-permute-start.6 = (bf16[128,192]{1,0:T(8,128)(2,1)}, bf16[128,192]{1,0:T(8,128)(2,1)S(1)}, u32[]{:S(2)}, u32[]{:S(2)}) collective-permute-start(bf16[128,192]{1,0:T(8,128)(2,1)} %get-tuple-element.91), channel_id=1, source_target_pairs={{0,4},{1,5},{2,6},{3,7},{4,0},{5,1},{6,2},{7,3},{8,12},{9,13},{10,... | collective-permute-start | bytes 147464 | tf_op jit(solution)/shard_map/ppermute | solution.py:575
  65.3 3.4 %collective-permute-done.6.mix2 = bf16[128,192]{1,0:T(8,128)(2,1)S(1)} collective-permute-done((bf16[128,192]{1,0:T(8,128)(2,1)}, bf16[128,192]{1,0:T(8,128)(2,1)S(1)}, u32[]{:S(2)}, u32[]{:S(2)}) %collective-permute-start.6) | collective-permute-done | bytes 49184 | tf_op jit(solution)/shard_map/ppermute | solution.py:575
  68.7 2.0 collective-permute-done.7.mix3
  70.7 1.3 copy-done.1
  71.9 1.3 copy-done.4
  73.2 0.8 copy-done.7
  74.0 0.8 copy-done.12
  74.8 1.5 first.1
  76.4 0.7 copy-done.14
  77.1 7.5 %collective-permute-done.8.other.low_other = bf16[128,768]{1,0:T(8,128)(2,1)S(1)} collective-permute-done((bf16[128,768]{1,0:T(8,128)(2,1)}, bf16[128,768]{1,0:T(8,128)(2,1)S(1)}, u32[]{:S(2)}, u32[]{:S(2)}) %collective-permute-start.8) | collective-permute-done | bytes 196640 | tf_op jit(solution)/shard_map/ppermute | solution.py:575
  84.6 0.9 copy-done.15
  85.5 3.0 %feed.1 = (bf16[256,1536]{1,0:T(8,128)(2,1)S(1)}, bf16[256,1536]{1,0:T(8,128)(2,1)S(1)}, f32[128,768]{1,0:T(8,128)S(1)}, bf16[128,768]{1,0:T(8,128)(2,1)S(1)}) custom-call(bf16[128,768]{1,0:T(8,128)(2,1)S(1)} %copy-done.15, bf16[128,768]{1,0:T(8,128)(2,1)S(1)} %collective-permute-done.8.other.low_other, bf16[8,192,768]{2,1,0:T(8,128)(2,1)S(1)} %all-to-all-done.1.w_mine, ...), custom_call_target="tpu_custom_call" | custom-call | flops 1207959552 | bytes 8000000 | tf_op jit(solution)/shard_map/feed/pallas_call | solution.py:634
  88.9 6.2 %collective-permute-done.10.came = bf16[128,768]{1,0:T(8,128)(2,1)S(1)} collective-permute-done((bf16[128,768]{1,0:T(8,128)(2,1)S(1)}, bf16[128,768]{1,0:T(8,128)(2,1)S(1)}, u32[]{:S(2)}, u32[]{:S(2)}) %collective-permute-start.10) | collective-permute-done | bytes 196640 | tf_op jit(solution)/shard_map/ppermute | solution.py:575
  95.1 1.0 second.1
  96.6 5.2 %collective-permute-done.11.other = bf16[128,768]{1,0:T(8,128)(2,1)S(1)} collective-permute-done((bf16[128,768]{1,0:T(8,128)(2,1)S(1)}, bf16[128,768]{1,0:T(8,128)(2,1)S(1)}, u32[]{:S(2)}, u32[]{:S(2)}) %collective-permute-start.11) | collective-permute-done | bytes 196640 | tf_op jit(solution)/shard_map/ppermute | solution.py:575
  101.8 2.5 %feed_back.1 = (bf16[256,1536]{1,0:T(8,128)(2,1)S(1)}, f32[128,768]{1,0:T(8,128)S(1)}, bf16[128,768]{1,0:T(8,128)(2,1)S(1)}, f32[2,768]{1,0:T(2,128)S(1)}) custom-call(bf16[128,768]{1,0:T(8,128)(2,1)S(1)} %get-tuple-element.102.mine, bf16[128,768]{1,0:T(8,128)(2,1)S(1)} %collective-permute-done.11.other, bf16[8,192,768]{2,1,0:T(8,128)(2,1)S(1)} %all-to-all-done.1.w_mine, ...), custom_call_target="tpu_custom_call" | custom-call | flops 1207959552 | bytes 8000000 | tf_op jit(solution)/shard_map/feed_back/pallas_call | solution.py:653
  104.9 0.7 collective-permute-start.12
  105.6 1.8 feed_grad.1
  107.4 3.2 %collective-permute-done.12.came = bf16[128,768]{1,0:T(8,128)(2,1)S(1)} collective-permute-done((bf16[128,768]{1,0:T(8,128)(2,1)S(1)}, bf16[128,768]{1,0:T(8,128)(2,1)S(1)}, u32[]{:S(2)}, u32[]{:S(2)}) %collective-permute-start.12) | collective-permute-done | bytes 196640 | tf_op jit(solution)/shard_map/ppermute | solution.py:575
  110.6 3.7 %first_back.1 = (f32[128,768]{1,0:T(8,128)S(1)}, bf16[8,48,768]{2,1,0:T(8,128)(2,1)S(1)}, bf16[8,48,768]{2,1,0:T(8,128)(2,1)S(1)}, bf16[128,192]{1,0:T(8,128)(2,...) custom-call(f32[128,768]{1,0:T(8,128)S(1)} %get-tuple-element.101.co, ...), custom_call_target="tpu_custom_call" | custom-call | flops 301989888 | bytes 4000000 | tf_op jit(solution)/shard_map/first_back/pallas_call | solution.py:679
  114.4 0.8 copy-done.11
  118.2 1.6 collective-permute-done.22.out_came
  119.8 0.8 copy-done.28
  120.6 4.9 %pair.1 = bf16[8,240,768]{2,1,0:T(8,128)(2,1)} custom-call(bf16[8,192,768]{2,1,0:T(8,128)(2,1)} %copy-done.6, bf16[8,192,768]{2,1,0:T(8,128)(2,1)} %copy-done.27, bf16[8,48,768]{2,1,0:T(8,128)(2,1)} %copy-done.11, bf16[8,48,768]{2,1,0:T(8,128)(2,1)} %copy-done.28), custom_call_target="tpu_custom_call" | custom-call | flops 1000000 | bytes 9000000 | tf_op jit(solution)/shard_map/pair/pallas_call | solution.py:704
  125.5 5.8 %all-to-all-start.3 = ((bf16[8,240,768]{2,1,0:T(8,128)(2,1)}), bf16[8,240,768]{2,1,0:T(8,128)(2,1)}, u32[]{:S(2)}, u32[]{:S(2)}) async-start(bf16[8,240,768]{2,1,0:T(8,128)(2,1)} %pair.1), calls=%async_computation.3 | async-start | bytes 5898240 | tf_op jit(solution)/shard_map/all_to_all | solution.py:579
  131.8 2.9 %collective-permute-start.16 = (bf16[128,192]{1,0:T(8,128)(2,1)S(1)}, bf16[128,192]{1,0:T(8,128)(2,1)S(1)}, u32[]{:S(2)}, u32[]{:S(2)}) collective-permute-start(bf16[128,192]{1,0:T(8,128)(2,1)S(1)} %copy-done.20), channel_id=1, source_target_pairs={{0,6},{1,7},{2,4},{3,5},{4,2},{5,3},{6,0},{7,1},{8,14},{9,15},{10,... | collective-permute-start | bytes 147464 | tf_op jit(solution)/shard_map/ppermute | solution.py:575
  134.8 2.8 %collective-permute-done.15.refs_2_ = bf16[128,192]{1,0:T(8,128)(2,1)S(1)} collective-permute-done((bf16[128,192]{1,0:T(8,128)(2,1)S(1)}, bf16[128,192]{1,0:T(8,128)(2,1)S(1)}, u32[]{:S(2)}, u32[]{:S(2)}) %collective-permute-start.15) | collective-permute-done | bytes 49184 | tf_op jit(solution)/shard_map/ppermute | solution.py:575
  138.2 0.7 collective-permute-done.14.refs_1_
  139.6 11.3 %attend_back.1 = (bf16[512,192]{1,0:T(8,128)(2,1)}, bf16[1024,192]{1,0:T(8,128)(2,1)}, bf16[1024,192]{1,0:T(8,128)(2,1)}, bf16[2,128,768]{2,1,0:T(8,128)(2,1)}, ...) custom-call(s32[1,8]{1,0:T(1,128)} %block_seq.3, ...), custom_call_target="tpu_custom_call" | custom-call | flops 4000000000 | bytes 8000000 | tf_op jit(solution)/shard_map/attend_back/pallas_call | solution.py:253
  151.0 5.3 %head_grad.1 = (bf16[8,48,768]{2,1,0:T(8,128)(2,1)}, bf16[8,48,768]{2,1,0:T(8,128)(2,1)}) custom-call(bf16[128,768]{1,0:T(8,128)(2,1)} %tokens.5, bf16[128,768]{1,0:T(8,128)(2,1)} %copy-done.30, bf16[2,128,768]{2,1,0:T(8,128)(2,1)} %copy-done.36, bf16[2,128,768]{2,1,0:T(8,128)(2,1)} %copy-done.35, bf16[2,128,768]{2,1,0:T(8,128)(2,1)} %copy-done.34, ...), custom_call_target="tpu_custom_call" | custom-call | flops 2000000000 | bytes 4000000 | tf_op jit(solution)/shard_map/head_grad/pallas_call | solution.py:315
  156.6 2.5 %collective-permute-start.19 = (bf16[2,128,768]{2,1,0:T(8,128)(2,1)S(1)}, bf16[2,128,768]{2,1,0:T(8,128)(2,1)}, u32[]{:S(2)}, u32[]{:S(2)}) collective-permute-start(bf16[2,128,768]{2,1,0:T(8,128)(2,1)S(1)} %copy-done.38), channel_id=1, source_target_pairs={{0,4},{1,5},{2,6},{3,7},{4,0},{5,1},{6,2},{7,3},{8,12},{9,13},{10,... | collective-permute-start | bytes 1179656 | tf_op jit(solution)/shard_map/ppermute | solution.py:575
  159.2 2.0 collective-permute-start.20
  161.2 2.0 add_convert_fusion
  163.2 5.2 %collective-permute-done.18 = bf16[2,128,768]{2,1,0:T(8,128)(2,1)S(1)} collective-permute-done((bf16[2,128,768]{2,1,0:T(8,128)(2,1)S(1)}, bf16[2,128,768]{2,1,0:T(8,128)(2,1)S(1)}, u32[]{:S(2)}, u32[]{:S(2)}) %collective-permute-start.18) | collective-permute-done | bytes 393248 | tf_op jit(solution)/shard_map/ppermute | solution.py:575
  168.4 8.8 %collective-permute-done.19 = bf16[2,128,768]{2,1,0:T(8,128)(2,1)} collective-permute-done((bf16[2,128,768]{2,1,0:T(8,128)(2,1)S(1)}, bf16[2,128,768]{2,1,0:T(8,128)(2,1)}, u32[]{:S(2)}, u32[]{:S(2)}) %collective-permute-start.19) | collective-permute-done | bytes 393248 | tf_op jit(solution)/shard_map/ppermute | solution.py:575
  177.2 2.6 %collective-permute-done.20 = bf16[2,128,768]{2,1,0:T(8,128)(2,1)} collective-permute-done((bf16[2,128,768]{2,1,0:T(8,128)(2,1)S(1)}, bf16[2,128,768]{2,1,0:T(8,128)(2,1)}, u32[]{:S(2)}, u32[]{:S(2)}) %collective-permute-start.20) | collective-permute-done | bytes 393248 | tf_op jit(solution)/shard_map/ppermute | solution.py:575
  179.8 5.6 %all-to-all-start.2 = ((bf16[8,48,768]{2,1,0:T(8,128)(2,1)}), bf16[8,48,768]{2,1,0:T(8,128)(2,1)S(1)}, u32[]{:S(2)}, u32[]{:S(2)}) async-start(bf16[8,48,768]{2,1,0:T(8,128)(2,1)} %add_convert_fusion), calls=%async_computation.2 | async-start | bytes 1179648 | tf_op jit(solution)/shard_map/all_to_all | solution.py:579
  185.4 3.0 %feed_sum.1 = (bf16[64,768]{1,0:T(8,128)(2,1)}, bf16[64,768]{1,0:T(8,128)(2,1)}, bf16[64,768]{1,0:T(8,128)(2,1)}, bf16[64,768]{1,0:T(8,128)(2,1)}) custom-call(bf16[8,240,768]{2,1,0:T(8,128)(2,1)} %all-to-all-done.3.parts), custom_call_target="tpu_custom_call" | custom-call | flops 1000000 | bytes 3000000 | tf_op jit(solution)/shard_map/feed_sum/pallas_call | solution.py:716
  188.4 2.8 %collective-permute-start.23 = (bf16[64,768]{1,0:T(8,128)(2,1)}, bf16[64,768]{1,0:T(8,128)(2,1)S(1)}, u32[]{:S(2)}, u32[]{:S(2)}) collective-permute-start(bf16[64,768]{1,0:T(8,128)(2,1)} %get-tuple-element.143), channel_id=1, source_target_pairs={{0,1},{1,0},{2,3},{3,2},{4,5},{5,4},{6,7},{7,6},{8,9},{9,8},{10,11... | collective-permute-start | bytes 294920 | tf_op jit(solution)/shard_map/ppermute | solution.py:575
  191.2 3.8 %collective-permute-start.25 = (bf16[64,768]{1,0:T(8,128)(2,1)}, bf16[64,768]{1,0:T(8,128)(2,1)S(1)}, u32[]{:S(2)}, u32[]{:S(2)}) collective-permute-start(bf16[64,768]{1,0:T(8,128)(2,1)} %get-tuple-element.145), channel_id=1, source_target_pairs={{0,5},{1,4},{2,7},{3,6},{4,1},{5,0},{6,3},{7,2},{8,13},{9,12},{10,... | collective-permute-start | bytes 294920 | tf_op jit(solution)/shard_map/ppermute | solution.py:575
  195.0 1.4 all-to-all-done.2.heads
  196.4 2.0 collective-permute-done.24.part2
  198.5 1.5 collective-permute-done.25.part3
  200.6 2.5 %last_sum.1 = bf16[8,112,768]{2,1,0:T(8,128)(2,1)} custom-call(bf16[8,48,768]{2,1,0:T(8,128)(2,1)} %copy-done.26, bf16[64,768]{1,0:T(8,128)(2,1)} %get-tuple-element.142.part0, bf16[64,768]{1,0:T(8,128)(2,1)} %copy-done.31, bf16[64,768]{1,0:T(8,128)(2,1)} %copy-done.32, bf16[64,768]{1,0:T(8,128)(2,1)} %copy-done.33), custom_call_target="tpu_custom_call" | custom-call | flops 1000000 | bytes 4000000 | tf_op jit(solution)/shard_map/last_sum/pallas_call | solution.py:728
  203.1 5.2 %all-to-all-start.4 = ((bf16[8,112,768]{2,1,0:T(8,128)(2,1)}), bf16[8,112,768]{2,1,0:T(8,128)(2,1)S(1)}, u32[]{:S(2)}, u32[]{:S(2)}) async-start(bf16[8,112,768]{2,1,0:T(8,128)(2,1)} %last_sum.1), calls=%async_computation.4 | async-start | bytes 2752512 | tf_op jit(solution)/shard_map/all_to_all | solution.py:579
  208.3 1.3 add_convert_fusion.1
  209.6 3.6 %collective-permute-start.21 = (bf16[128,768]{1,0:T(8,128)(2,1)S(1)}, bf16[128,768]{1,0:T(8,128)(2,1)S(1)}, u32[]{:S(2)}, u32[]{:S(2)}) collective-permute-start(bf16[128,768]{1,0:T(8,128)(2,1)S(1)} %slice_bitcast_fusion), channel_id=1, source_target_pairs={{0,1},{1,0},{2,3},{3,2},{4,5},{5,4},{6,7},{7,6},{8,9},{9,8},{10,11... | collective-permute-start | bytes 589832 | tf_op jit(solution)/shard_map/ppermute | solution.py:575
  213.2 15.1 %collective-permute-done.21 = bf16[128,768]{1,0:T(8,128)(2,1)S(1)} collective-permute-done((bf16[128,768]{1,0:T(8,128)(2,1)S(1)}, bf16[128,768]{1,0:T(8,128)(2,1)S(1)}, u32[]{:S(2)}, u32[]{:S(2)}) %collective-permute-start.21) | collective-permute-done | bytes 196640 | tf_op jit(solution)/shard_map/ppermute | solution.py:575
  228.4 0.8 fusion
  229.2 1.5 unpack.1
  (105 shorter events, 9.3 us)
Async XLA Ops:
  0.6 8.3 %collective-permute-start = (bf16[128,768]{1,0:T(8,128)(2,1)}, bf16[128,768]{1,0:T(8,128)(2,1)S(1)}, u32[]{:S(2)}, u32[]{:S(2)}) collective-permute-start(bf16[128,768]{1,0:T(8,128)(2,1)} %tokens.5), channel_id=1, source_target_pairs={{0,1},{1,0},{2,3},{3,2},{4,5},{5,4},{6,7},{7,6},{8,9},{9,8},{10,11... | collective-permute-start | bytes 589832 | tf_op jit(solution)/shard_map/ppermute | solution.py:575
  5.0 13.3 %copy-start.9 = (bf16[128,768]{1,0:T(8,128)(2,1)S(1)}, bf16[128,768]{1,0:T(8,128)(2,1)}, u32[]{:S(2)}) copy-start(bf16[128,768]{1,0:T(8,128)(2,1)} %tokens.5) | copy-start | bytes 589828
  8.9 9.4 %copy-start.30 = (bf16[128,768]{1,0:T(8,128)(2,1)}, bf16[128,768]{1,0:T(8,128)(2,1)S(1)}, u32[]{:S(2)}) copy-start(bf16[128,768]{1,0:T(8,128)(2,1)S(1)} %collective-permute-done.other) | copy-start | bytes 589828
  12.7 26.9 %all-to-all-start = ((bf16[8,96,768]{2,1,0:T(8,128)(2,1)}), bf16[8,96,768]{2,1,0:T(8,128)(2,1)S(1)}, u32[]{:S(2)}, u32[]{:S(2)}) async-start(bf16[8,96,768]{2,1,0:T(8,128)(2,1)} %get-tuple-element.81), calls=%async_computation | async-start | bytes 2359296 | tf_op jit(solution)/shard_map/all_to_all | solution.py:579
  18.4 20.5 %collective-permute-start.3 = (bf16[2,128,768]{2,1,0:T(8,128)(2,1)S(1)}, bf16[2,128,768]{2,1,0:T(8,128)(2,1)S(1)}, u32[]{:S(2)}, u32[]{:S(2)}) collective-permute-start(bf16[2,128,768]{2,1,0:T(8,128)(2,1)S(1)} %pad_maximum_fusion), channel_id=1, source_target_pairs={{0,6},{1,7},{2,4},{3,5},{4,2},{5,3},{6,0},{7,1},{8,14},{9,15},{10,... | collective-permute-start | bytes 1179656 | tf_op jit(solution)/shard_map/ppermute | solution.py:575
  22.5 16.4 %collective-permute-start.2 = (bf16[2,128,768]{2,1,0:T(8,128)(2,1)S(1)}, bf16[2,128,768]{2,1,0:T(8,128)(2,1)S(1)}, u32[]{:S(2)}, u32[]{:S(2)}) collective-permute-start(bf16[2,128,768]{2,1,0:T(8,128)(2,1)S(1)} %pad_maximum_fusion), channel_id=1, source_target_pairs={{0,4},{1,5},{2,6},{3,7},{4,0},{5,1},{6,2},{7,3},{8,12},{9,13},{10,... | collective-permute-start | bytes 1179656 | tf_op jit(solution)/shard_map/ppermute | solution.py:575
  22.5 17.1 %collective-permute-start.1 = (bf16[2,128,768]{2,1,0:T(8,128)(2,1)S(1)}, bf16[2,128,768]{2,1,0:T(8,128)(2,1)S(1)}, u32[]{:S(2)}, u32[]{:S(2)}) collective-permute-start(bf16[2,128,768]{2,1,0:T(8,128)(2,1)S(1)} %pad_maximum_fusion), channel_id=1, source_target_pairs={{0,2},{1,3},{2,0},{3,1},{4,6},{5,7},{6,4},{7,5},{8,10},{9,11},{10,... | collective-permute-start | bytes 1179656 | tf_op jit(solution)/shard_map/ppermute | solution.py:575
  38.9 0.8 copy-start.34
  38.9 0.9 copy-start.35
  39.6 9.1 %copy-start = (bf16[8,96,768]{2,1,0:T(8,128)(2,1)}, bf16[8,96,768]{2,1,0:T(8,128)(2,1)S(1)}, u32[]{:S(2)}) copy-start(bf16[8,96,768]{2,1,0:T(8,128)(2,1)S(1)} %all-to-all-done.w_mine) | copy-start | bytes 3538948
  40.4 36.7 %all-to-all-start.1 = ((bf16[8,192,768]{2,1,0:T(8,128)(2,1)}), bf16[8,192,768]{2,1,0:T(8,128)(2,1)S(1)}, u32[]{:S(2)}, u32[]{:S(2)}) async-start(bf16[8,192,768]{2,1,0:T(8,128)(2,1)} %get-tuple-element.84), calls=%async_computation.1 | async-start | bytes 4718592 | tf_op jit(solution)/shard_map/all_to_all | solution.py:579
  45.8 24.9 %copy-start.10 = (bf16[128,768]{1,0:T(8,128)(2,1)S(1)}, bf16[128,768]{1,0:T(8,128)(2,1)}, u32[]{:S(2)}) copy-start(bf16[128,768]{1,0:T(8,128)(2,1)} %tokens.5) | copy-start | bytes 589828
  45.8 2.9 %collective-permute-start.4 = (bf16[8,96,768]{2,1,0:T(8,128)(2,1)S(1)}, bf16[8,96,768]{2,1,0:T(8,128)(2,1)S(1)}, u32[]{:S(2)}, u32[]{:S(2)}) collective-permute-start(bf16[8,96,768]{2,1,0:T(8,128)(2,1)S(1)} %all-to-all-done.w_mine), channel_id=1, source_target_pairs={{0,8},{8,0},{16,24},{24,16},{32,40},{40,32},{48,56},{56,48},{64,72... | collective-permute-start | bytes 3538952 | tf_op jit(solution)/shard_map/ppermute | solution.py:575
  48.7 1.1 copy-start.3
  60.6 4.8 %collective-permute-start.5 = (bf16[128,192]{1,0:T(8,128)(2,1)}, bf16[128,192]{1,0:T(8,128)(2,1)S(1)}, u32[]{:S(2)}, u32[]{:S(2)}) collective-permute-start(bf16[128,192]{1,0:T(8,128)(2,1)} %get-tuple-element.90), channel_id=1, source_target_pairs={{0,2},{1,3},{2,0},{3,1},{4,6},{5,7},{6,4},{7,5},{8,10},{9,11},{10,... | collective-permute-start | bytes 147464 | tf_op jit(solution)/shard_map/ppermute | solution.py:575
  61.7 7.0 %collective-permute-start.6 = (bf16[128,192]{1,0:T(8,128)(2,1)}, bf16[128,192]{1,0:T(8,128)(2,1)S(1)}, u32[]{:S(2)}, u32[]{:S(2)}) collective-permute-start(bf16[128,192]{1,0:T(8,128)(2,1)} %get-tuple-element.91), channel_id=1, source_target_pairs={{0,4},{1,5},{2,6},{3,7},{4,0},{5,1},{6,2},{7,3},{8,12},{9,13},{10,... | collective-permute-start | bytes 147464 | tf_op jit(solution)/shard_map/ppermute | solution.py:575
  65.0 5.7 %collective-permute-start.7 = (bf16[128,192]{1,0:T(8,128)(2,1)}, bf16[128,192]{1,0:T(8,128)(2,1)S(1)}, u32[]{:S(2)}, u32[]{:S(2)}) collective-permute-start(bf16[128,192]{1,0:T(8,128)(2,1)} %get-tuple-element.92), channel_id=1, source_target_pairs={{0,6},{1,7},{2,4},{3,5},{4,2},{5,3},{6,0},{7,1},{8,14},{9,15},{10,... | collective-permute-start | bytes 147464 | tf_op jit(solution)/shard_map/ppermute | solution.py:575
  70.7 1.3 copy-start.1
  71.9 1.3 copy-start.4
  73.2 0.8 copy-start.7
  74.0 0.8 copy-start.12
  74.8 9.8 %copy-start.8 = (f32[16,768]{1,0:T(8,128)S(1)}, f32[16,768]{1,0:T(8,128)}, u32[]{:S(2)}) copy-start(f32[16,768]{1,0:T(8,128)} %get-tuple-element.93.vectors) | copy-start | bytes 147460
  77.1 7.5 %collective-permute-start.9 = (bf16[8,192,768]{2,1,0:T(8,128)(2,1)S(1)}, bf16[8,192,768]{2,1,0:T(8,128)(2,1)S(1)}, u32[]{:S(2)}, u32[]{:S(2)}) collective-permute-start(bf16[8,192,768]{2,1,0:T(8,128)(2,1)S(1)} %all-to-all-done.1.w_mine), channel_id=1, source_target_pairs={{0,8},{8,0},{16,24},{24,16},{32,40},{40,32},{48,56},{56,48},{64,72... | collective-permute-start | bytes 7077896 | tf_op jit(solution)/shard_map/ppermute | solution.py:575
  77.1 7.5 %collective-permute-start.8 = (bf16[128,768]{1,0:T(8,128)(2,1)}, bf16[128,768]{1,0:T(8,128)(2,1)S(1)}, u32[]{:S(2)}, u32[]{:S(2)}) collective-permute-start(bf16[128,768]{1,0:T(8,128)(2,1)} %copy-done.14), channel_id=1, source_target_pairs={{0,2},{1,3},{2,0},{3,1},{4,6},{5,7},{6,4},{7,5},{8,10},{9,11},{10,... | collective-permute-start | bytes 589832 | tf_op jit(solution)/shard_map/ppermute | solution.py:575
  84.6 0.9 copy-start.15
  85.5 9.6 %copy-start.17 = (bf16[128,768]{1,0:T(8,128)(2,1)S(1)}, bf16[128,768]{1,0:T(8,128)(2,1)}, u32[]{:S(2)}) copy-start(bf16[128,768]{1,0:T(8,128)(2,1)} %out_grad.1) | copy-start | bytes 589828
  88.5 6.6 %collective-permute-start.10 = (bf16[128,768]{1,0:T(8,128)(2,1)S(1)}, bf16[128,768]{1,0:T(8,128)(2,1)S(1)}, u32[]{:S(2)}, u32[]{:S(2)}) collective-permute-start(bf16[128,768]{1,0:T(8,128)(2,1)S(1)} %get-tuple-element.99), channel_id=1, source_target_pairs={{0,2},{1,3},{2,0},{3,1},{4,6},{5,7},{6,4},{7,5},{8,10},{9,11},{10,... | collective-permute-start | bytes 589832 | tf_op jit(solution)/shard_map/ppermute | solution.py:575
  96.1 8.2 %copy-start.23 = (f32[3,768]{1,0:T(4,128)}, f32[3,768]{1,0:T(4,128)S(1)}, u32[]{:S(2)}) copy-start(f32[3,768]{1,0:T(4,128)S(1)} %get-tuple-element.127.second_sums) | copy-start | bytes 27652
  96.1 5.7 %collective-permute-start.11 = (bf16[128,768]{1,0:T(8,128)(2,1)S(1)}, bf16[128,768]{1,0:T(8,128)(2,1)S(1)}, u32[]{:S(2)}, u32[]{:S(2)}) collective-permute-start(bf16[128,768]{1,0:T(8,128)(2,1)S(1)} %get-tuple-element.102.mine), channel_id=1, source_target_pairs={{0,2},{1,3},{2,0},{3,1},{4,6},{5,7},{6,4},{7,5},{8,10},{9,11},{10,... | collective-permute-start | bytes 589832 | tf_op jit(solution)/shard_map/ppermute | solution.py:575
  101.8 3.8 %copy-start.16 = (bf16[128,768]{1,0:T(8,128)(2,1)S(1)}, bf16[128,768]{1,0:T(8,128)(2,1)}, u32[]{:S(2)}) copy-start(bf16[128,768]{1,0:T(8,128)(2,1)} %copy-done.14) | copy-start | bytes 589828
  104.9 5.7 %collective-permute-start.12 = (bf16[128,768]{1,0:T(8,128)(2,1)S(1)}, bf16[128,768]{1,0:T(8,128)(2,1)S(1)}, u32[]{:S(2)}, u32[]{:S(2)}) collective-permute-start(bf16[128,768]{1,0:T(8,128)(2,1)S(1)} %get-tuple-element.108), channel_id=1, source_target_pairs={{0,2},{1,3},{2,0},{3,1},{4,6},{5,7},{6,4},{7,5},{8,10},{9,11},{10,... | collective-permute-start | bytes 589832 | tf_op jit(solution)/shard_map/ppermute | solution.py:575
  105.6 5.0 %copy-start.2 = (bf16[8,96,768]{2,1,0:T(8,128)(2,1)S(1)}, bf16[8,96,768]{2,1,0:T(8,128)(2,1)}, u32[]{:S(2)}) copy-start(bf16[8,96,768]{2,1,0:T(8,128)(2,1)} %copy-done) | copy-start | bytes 3538948
  105.6 5.0 %copy-start.5 = (bf16[8,96,768]{2,1,0:T(8,128)(2,1)S(1)}, bf16[8,96,768]{2,1,0:T(8,128)(2,1)}, u32[]{:S(2)}) copy-start(bf16[8,96,768]{2,1,0:T(8,128)(2,1)} %copy-done.3) | copy-start | bytes 3538948
  105.6 5.0 %copy-start.13 = (bf16[128,192]{1,0:T(8,128)(2,1)S(1)}, bf16[128,192]{1,0:T(8,128)(2,1)}, u32[]{:S(2)}) copy-start(bf16[128,192]{1,0:T(8,128)(2,1)} %get-tuple-element.89.mix0) | copy-start | bytes 147460
  107.4 6.9 %copy-start.6 = (bf16[8,192,768]{2,1,0:T(8,128)(2,1)}, bf16[8,192,768]{2,1,0:T(8,128)(2,1)S(1)}, u32[]{:S(2)}) copy-start(bf16[8,192,768]{2,1,0:T(8,128)(2,1)S(1)} %get-tuple-element.138.feed_keep) | copy-start | bytes 7077892
  110.6 7.6 %collective-permute-start.13 = (bf16[8,192,768]{2,1,0:T(8,128)(2,1)S(1)}, bf16[8,192,768]{2,1,0:T(8,128)(2,1)S(1)}, u32[]{:S(2)}, u32[]{:S(2)}) collective-permute-start(bf16[8,192,768]{2,1,0:T(8,128)(2,1)S(1)} %get-tuple-element.113), channel_id=1, source_target_pairs={{0,8},{8,0},{16,24},{24,16},{32,40},{40,32},{48,56},{56,48},{64,72... | collective-permute-start | bytes 7077896 | tf_op jit(solution)/shard_map/ppermute | solution.py:575
  114.4 0.8 copy-start.11
  117.7 2.1 collective-permute-start.22
  118.2 1.6 copy-start.27
  119.8 0.8 copy-start.28
  125.5 5.8 %copy-start.22 = (bf16[128,192]{1,0:T(8,128)(2,1)S(1)}, bf16[128,192]{1,0:T(8,128)(2,1)}, u32[]{:S(2)}) copy-start(bf16[128,192]{1,0:T(8,128)(2,1)} %copy-done.21) | copy-start | bytes 147460
  125.5 6.3 %copy-start.20 = (bf16[128,192]{1,0:T(8,128)(2,1)S(1)}, bf16[128,192]{1,0:T(8,128)(2,1)}, u32[]{:S(2)}) copy-start(bf16[128,192]{1,0:T(8,128)(2,1)} %copy-done.19) | copy-start | bytes 147460
  125.5 54.3 %all-to-all-start.3 = ((bf16[8,240,768]{2,1,0:T(8,128)(2,1)}), bf16[8,240,768]{2,1,0:T(8,128)(2,1)}, u32[]{:S(2)}, u32[]{:S(2)}) async-start(bf16[8,240,768]{2,1,0:T(8,128)(2,1)} %pair.1), calls=%async_computation.3 | async-start | bytes 5898240 | tf_op jit(solution)/shard_map/all_to_all | solution.py:579
  131.3 6.4 %collective-permute-start.15 = (bf16[128,192]{1,0:T(8,128)(2,1)S(1)}, bf16[128,192]{1,0:T(8,128)(2,1)S(1)}, u32[]{:S(2)}, u32[]{:S(2)}) collective-permute-start(bf16[128,192]{1,0:T(8,128)(2,1)S(1)} %copy-done.22), channel_id=1, source_target_pairs={{0,4},{1,5},{2,6},{3,7},{4,0},{5,1},{6,2},{7,3},{8,12},{9,13},{10,... | collective-permute-start | bytes 147464 | tf_op jit(solution)/shard_map/ppermute | solution.py:575
  131.8 6.4 %collective-permute-start.16 = (bf16[128,192]{1,0:T(8,128)(2,1)S(1)}, bf16[128,192]{1,0:T(8,128)(2,1)S(1)}, u32[]{:S(2)}, u32[]{:S(2)}) collective-permute-start(bf16[128,192]{1,0:T(8,128)(2,1)S(1)} %copy-done.20), channel_id=1, source_target_pairs={{0,6},{1,7},{2,4},{3,5},{4,2},{5,3},{6,0},{7,1},{8,14},{9,15},{10,... | collective-permute-start | bytes 147464 | tf_op jit(solution)/shard_map/ppermute | solution.py:575
  134.7 4.3 %collective-permute-start.14 = (bf16[128,192]{1,0:T(8,128)(2,1)S(1)}, bf16[128,192]{1,0:T(8,128)(2,1)S(1)}, u32[]{:S(2)}, u32[]{:S(2)}) collective-permute-start(bf16[128,192]{1,0:T(8,128)(2,1)S(1)} %get-tuple-element.115), channel_id=1, source_target_pairs={{0,2},{1,3},{2,0},{3,1},{4,6},{5,7},{6,4},{7,5},{8,10},{9,11},{10,... | collective-permute-start | bytes 147464 | tf_op jit(solution)/shard_map/ppermute | solution.py:575
  137.6 1.3 copy-start.40
  150.9 5.4 %copy-start.39 = (bf16[2,128,768]{2,1,0:T(8,128)(2,1)S(1)}, bf16[2,128,768]{2,1,0:T(8,128)(2,1)}, u32[]{:S(2)}) copy-start(bf16[2,128,768]{2,1,0:T(8,128)(2,1)} %get-tuple-element.131) | copy-start | bytes 1179652
  151.0 5.6 %copy-start.38 = (bf16[2,128,768]{2,1,0:T(8,128)(2,1)S(1)}, bf16[2,128,768]{2,1,0:T(8,128)(2,1)}, u32[]{:S(2)}) copy-start(bf16[2,128,768]{2,1,0:T(8,128)(2,1)} %get-tuple-element.132) | copy-start | bytes 1179652
  151.0 8.2 %copy-start.37 = (bf16[2,128,768]{2,1,0:T(8,128)(2,1)S(1)}, bf16[2,128,768]{2,1,0:T(8,128)(2,1)}, u32[]{:S(2)}) copy-start(bf16[2,128,768]{2,1,0:T(8,128)(2,1)} %get-tuple-element.133) | copy-start | bytes 1179652
  156.3 4.9 %collective-permute-start.17 = (bf16[8,48,768]{2,1,0:T(8,128)(2,1)}, bf16[8,48,768]{2,1,0:T(8,128)(2,1)S(1)}, u32[]{:S(2)}, u32[]{:S(2)}) collective-permute-start(bf16[8,48,768]{2,1,0:T(8,128)(2,1)} %get-tuple-element.130), channel_id=1, source_target_pairs={{0,8},{8,0},{16,24},{24,16},{32,40},{40,32},{48,56},{56,48},{64,72... | collective-permute-start | bytes 1769480 | tf_op jit(solution)/shard_map/ppermute | solution.py:575
  156.4 12.0 %collective-permute-start.18 = (bf16[2,128,768]{2,1,0:T(8,128)(2,1)S(1)}, bf16[2,128,768]{2,1,0:T(8,128)(2,1)S(1)}, u32[]{:S(2)}, u32[]{:S(2)}) collective-permute-start(bf16[2,128,768]{2,1,0:T(8,128)(2,1)S(1)} %copy-done.39), channel_id=1, source_target_pairs={{0,2},{1,3},{2,0},{3,1},{4,6},{5,7},{6,4},{7,5},{8,10},{9,11},{10,... | collective-permute-start | bytes 1179656 | tf_op jit(solution)/shard_map/ppermute | solution.py:575
  156.6 20.6 %collective-permute-start.19 = (bf16[2,128,768]{2,1,0:T(8,128)(2,1)S(1)}, bf16[2,128,768]{2,1,0:T(8,128)(2,1)}, u32[]{:S(2)}, u32[]{:S(2)}) collective-permute-start(bf16[2,128,768]{2,1,0:T(8,128)(2,1)S(1)} %copy-done.38), channel_id=1, source_target_pairs={{0,4},{1,5},{2,6},{3,7},{4,0},{5,1},{6,2},{7,3},{8,12},{9,13},{10,... | collective-permute-start | bytes 1179656 | tf_op jit(solution)/shard_map/ppermute | solution.py:575
  159.2 20.6 %collective-permute-start.20 = (bf16[2,128,768]{2,1,0:T(8,128)(2,1)S(1)}, bf16[2,128,768]{2,1,0:T(8,128)(2,1)}, u32[]{:S(2)}, u32[]{:S(2)}) collective-permute-start(bf16[2,128,768]{2,1,0:T(8,128)(2,1)S(1)} %copy-done.37), channel_id=1, source_target_pairs={{0,6},{1,7},{2,4},{3,5},{4,2},{5,3},{6,0},{7,1},{8,14},{9,15},{10,... | collective-permute-start | bytes 1179656 | tf_op jit(solution)/shard_map/ppermute | solution.py:575
  179.8 16.6 %all-to-all-start.2 = ((bf16[8,48,768]{2,1,0:T(8,128)(2,1)}), bf16[8,48,768]{2,1,0:T(8,128)(2,1)S(1)}, u32[]{:S(2)}, u32[]{:S(2)}) async-start(bf16[8,48,768]{2,1,0:T(8,128)(2,1)} %add_convert_fusion), calls=%async_computation.2 | async-start | bytes 1179648 | tf_op jit(solution)/shard_map/all_to_all | solution.py:579
  188.4 8.0 %collective-permute-start.23 = (bf16[64,768]{1,0:T(8,128)(2,1)}, bf16[64,768]{1,0:T(8,128)(2,1)S(1)}, u32[]{:S(2)}, u32[]{:S(2)}) collective-permute-start(bf16[64,768]{1,0:T(8,128)(2,1)} %get-tuple-element.143), channel_id=1, source_target_pairs={{0,1},{1,0},{2,3},{3,2},{4,5},{5,4},{6,7},{7,6},{8,9},{9,8},{10,11... | collective-permute-start | bytes 294920 | tf_op jit(solution)/shard_map/ppermute | solution.py:575
  191.2 7.3 %collective-permute-start.24 = (bf16[64,768]{1,0:T(8,128)(2,1)}, bf16[64,768]{1,0:T(8,128)(2,1)S(1)}, u32[]{:S(2)}, u32[]{:S(2)}) collective-permute-start(bf16[64,768]{1,0:T(8,128)(2,1)} %get-tuple-element.144), channel_id=1, source_target_pairs={{0,4},{1,5},{2,6},{3,7},{4,0},{5,1},{6,2},{7,3},{8,12},{9,13},{10,... | collective-permute-start | bytes 294920 | tf_op jit(solution)/shard_map/ppermute | solution.py:575
  191.2 8.7 %collective-permute-start.25 = (bf16[64,768]{1,0:T(8,128)(2,1)}, bf16[64,768]{1,0:T(8,128)(2,1)S(1)}, u32[]{:S(2)}, u32[]{:S(2)}) collective-permute-start(bf16[64,768]{1,0:T(8,128)(2,1)} %get-tuple-element.145), channel_id=1, source_target_pairs={{0,5},{1,4},{2,7},{3,6},{4,1},{5,0},{6,3},{7,2},{8,13},{9,12},{10,... | collective-permute-start | bytes 294920 | tf_op jit(solution)/shard_map/ppermute | solution.py:575
  196.4 3.5 %copy-start.26 = (bf16[8,48,768]{2,1,0:T(8,128)(2,1)}, bf16[8,48,768]{2,1,0:T(8,128)(2,1)S(1)}, u32[]{:S(2)}) copy-start(bf16[8,48,768]{2,1,0:T(8,128)(2,1)S(1)} %all-to-all-done.2.heads) | copy-start | bytes 1769476
  196.4 3.5 %copy-start.31 = (bf16[64,768]{1,0:T(8,128)(2,1)}, bf16[64,768]{1,0:T(8,128)(2,1)S(1)}, u32[]{:S(2)}) copy-start(bf16[64,768]{1,0:T(8,128)(2,1)S(1)} %collective-permute-done.23.part1) | copy-start | bytes 294916
  198.5 1.5 copy-start.32
  203.1 5.2 %copy-start.29 = (bf16[2,128,768]{2,1,0:T(8,128)(2,1)S(1)}, bf16[2,128,768]{2,1,0:T(8,128)(2,1)}, u32[]{:S(2)}) copy-start(bf16[2,128,768]{2,1,0:T(8,128)(2,1)} %get-tuple-element.122) | copy-start | bytes 1179652
  203.1 26.1 %all-to-all-start.4 = ((bf16[8,112,768]{2,1,0:T(8,128)(2,1)}), bf16[8,112,768]{2,1,0:T(8,128)(2,1)S(1)}, u32[]{:S(2)}, u32[]{:S(2)}) async-start(bf16[8,112,768]{2,1,0:T(8,128)(2,1)} %last_sum.1), calls=%async_computation.4 | async-start | bytes 2752512 | tf_op jit(solution)/shard_map/all_to_all | solution.py:579
  209.6 18.7 %collective-permute-start.21 = (bf16[128,768]{1,0:T(8,128)(2,1)S(1)}, bf16[128,768]{1,0:T(8,128)(2,1)S(1)}, u32[]{:S(2)}, u32[]{:S(2)}) collective-permute-start(bf16[128,768]{1,0:T(8,128)(2,1)S(1)} %slice_bitcast_fusion), channel_id=1, source_target_pairs={{0,1},{1,0},{2,3},{3,2},{4,5},{5,4},{6,7},{7,6},{8,9},{9,8},{10,11... | collective-permute-start | bytes 589832 | tf_op jit(solution)/shard_map/ppermute | solution.py:575
  (10 other events, 6.5 us)

commit v3 on v2

--- a/solution.py
+++ b/solution.py
@@ -164,7 +164,8 @@
             chances[i, h] = share
             outs.append(nn(share, value_h))
         mixture[zed ^ i] = jnp.concatenate(outs, axis=1).astype(bf16)
-    stores += begin(sems, 0, *((mixture.at[k], out) for k, out in enumerate(sends)), (chances, kept_out[0]))
+        stores += begin(sems, 4 + i, (chances.at[i], kept_out[0].at[i]))
+    stores += begin(sems, 0, *((mixture.at[k], out) for k, out in enumerate(sends)))
     finish(stores)
 
 
@@ -339,36 +340,37 @@
     )
 
 
-def pack_kernel(vectors, b_up, w_qkv, w_out, w_up, w_down, heads, feed, heads_own, feed_own, qkv, up, sems):
-    xh, zed, core = places()
-    half = lax.rem(zed, 2)
+def pack_heads_kernel(vectors, b_up, w_qkv, w_out, copies, heads, qkv, sems):
+    zed = places()[1]
+    loads = begin(sems, 0, (w_qkv, qkv), (w_out, heads.at[pl.ds(48, 48)]))
+    bias = b_up[...].astype(f32)
+    small = jnp.concatenate([vectors[...].astype(f32)] + [bias[:, 48 * e : 48 * e + 48] for e in range(4)], axis=0)
+    small = jnp.concatenate([small, jnp.zeros((12, 80), f32)], axis=1)
+    small = jnp.concatenate([small, jnp.zeros((116, 128), f32)], axis=0)
+    heads[0:48, EXTRA:] = jnp.transpose(small)[:48].astype(bf16)
+    heads[0:48, 3 * WIDE : EXTRA] = jnp.zeros((48, EXTRA - 3 * WIDE), bf16)
+    finish(loads)
+    for z in range(4):
+
+        @pl.when(zed == z)
+        def _(z=z):
+            heads[0:48, : 3 * WIDE] = jnp.concatenate(
+                [qkv[:, D * t + WIDE * z : D * t + WIDE * z + WIDE] for t in range(3)], axis=1
+            )
+
+    finish(begin(sems, 2, *((heads, copies.at[k]) for k in range(8))))
+
+
+def pack_feed_kernel(w_up, w_down, feed, feed_own, up, sems):
+    half = lax.rem(places()[1], 2)
     start = pl.multiple_of(96 * half, 32)
     loads = begin(
         sems,
         0,
-        (w_qkv, qkv),
         (w_up, up),
-        (w_out, heads_own.at[pl.ds(48, 48)]),
         (w_down.at[pl.ds(start, 96)], feed_own.at[pl.ds(0, 96)]),
     )
-    bias = b_up[...].astype(f32)
-    small = jnp.concatenate([vectors[...].astype(f32)] + [bias[:, 48 * e : 48 * e + 48] for e in range(4)], axis=0)
-    small = jnp.concatenate([small, jnp.zeros((12, 80), f32)], axis=1)
-    small = jnp.concatenate([small, jnp.zeros((116, 128), f32)], axis=0)
-    heads_own[0:48, EXTRA:] = jnp.transpose(small)[:48].astype(bf16)
-    heads_own[0:48, 3 * WIDE : EXTRA] = jnp.zeros((48, EXTRA - 3 * WIDE), bf16)
     loads[0].wait()
-    for z in range(4):
-
-        @pl.when(zed == z)
-        def _(z=z):
-            heads_own[0:48, : 3 * WIDE] = jnp.concatenate(
-                [qkv[:, D * t + WIDE * z : D * t + WIDE * z + WIDE] for t in range(3)], axis=1
-            )
-
-    loads[2].wait()
-    stores = begin(sems, 4, *((heads_own, heads.at[k]) for k in range(8)))
-    loads[1].wait()
     for h in range(2):
 
         @pl.when(half == h)
@@ -379,9 +381,8 @@
                     [up[:, 192 * f + first : 192 * f + first + 48] for f in range(F)], axis=1
                 )
 
-    loads[3].wait()
-    stores += begin(sems, 12, *((feed_own, feed.at[k]) for k in range(8)))
-    finish(stores)
+    finish(loads[1:])
+    finish(begin(sems, 2, *((feed_own, feed.at[k]) for k in range(8))))
 
 
 def first_kernel(mix0, mix1, mix2, mix3, w_mine, w_other, vectors, tokens, low, norm, hat, *scratch):
@@ -515,49 +516,58 @@
     finish(stores)
 
 
-def pair_kernel(feed_keep, feed_came, out_keep, out_came, pair):
-    pair[:, 0:192, :] = (feed_keep[...].astype(f32) + feed_came[...].astype(f32)).astype(bf16)
-    pair[:, 192:240, :] = (out_keep[...].astype(f32) + out_came[...].astype(f32)).astype(bf16)
+def pair_kernel(head_keep, head_came, out_keep, out_came, pair):
+    pair[:, 0:48, :] = (head_keep[...].astype(f32) + head_came[...].astype(f32)).astype(bf16)
+    pair[:, 48:96, :] = (out_keep[...].astype(f32) + out_came[...].astype(f32)).astype(bf16)
 
 
 def feed_sum_kernel(parts, out0, out1, out2, out3, slots, sems):
-    xh, zed, core = places()
+    xh, zed, _ = places()
     member = 2 * lax.div(zed, 2) + xh
     for m in range(4):
-        rows = 64 if m < 3 else 48
-        total = parts[0, 64 * m : 64 * m + rows, :].astype(f32)
-        for chip in range(1, 8):
-            total += parts[chip, 64 * m : 64 * m + rows, :].astype(f32)
-        slots[member ^ m, 0:rows, :] = total.astype(bf16)
-        if rows < 64:
-            slots[member ^ m, rows:64, :] = jnp.zeros((64 - rows, D), bf16)
+        total = parts[0, 48 * m : 48 * m + 48, :].astype(f32)
+        for k in range(1, 8):
+            total += parts[k, 48 * m : 48 * m + 48, :].astype(f32)
+        slots[member ^ m] = total.astype(bf16)
     finish(begin(sems, 0, *((slots.at[k], out) for k, out in enumerate((out0, out1, out2, out3)))))
 
 
-def last_sum_kernel(heads, part0, part1, part2, part3, copies, total, sems):
+def last_sum_kernel(heads, part0, part1, part2, part3, total):
     quarter = part0[...].astype(f32)
     for part in (part1, part2, part3):
         quarter += part[...].astype(f32)
-    total[0:64, :] = quarter.astype(bf16)
+    total[0:48, :] = quarter.astype(bf16)
     whole = heads[0].astype(f32)
-    for chip in range(1, 8):
-        whole += heads[chip].astype(f32)
-    total[64:112, :] = whole.astype(bf16)
-    finish(begin(sems, 0, *((total, copies.at[k]) for k in range(NBLK))))
-
-
-def unpack_kernel(every, qkv, out, up, down, vectors, bias):
+    for k in range(1, 8):
+        whole += heads[k].astype(f32)
+    total[48:144, :] = whole.astype(bf16)
+
+
+def merge_kernel(own, other, merged):
+    xh = places()[0]
+    merged[pl.ds(pl.multiple_of(48 * xh, 16), 48), :] = own[0:48, :]
+    merged[pl.ds(pl.multiple_of(48 * (1 - xh), 16), 48), :] = other[0:48, :]
+    merged[96:192, :] = (own[48:144, :].astype(f32) + other[48:144, :].astype(f32)).astype(bf16)
+
+
+def unpack_kernel(one0, one1, one2, one3, qkv, out, up, down, vectors, bias, every):
+    zed = places()[1]
+    for k, one in enumerate((one0, one1, one2, one3)):
+        every[zed ^ k] = one[...]
     ups = []
     for h in range(2):
-        quarters = [every[4 * (m // 2) + 2 * h + m % 2, 0:64, :].astype(f32) for m in range(4)]
-        whole = jnp.concatenate(quarters, axis=0)
-        down[96 * h : 96 * h + 96, :] = whole[0:96]
-        ups.append([whole[96:144], whole[144:192]])
-        out[...] = whole[192:240] if h == 0 else out[...] + whole[192:240]
+        quarters = [every[2 * (m // 2) + h, 48 * (m % 2) : 48 * (m % 2) + 48, :].astype(f32) for m in range(4)]
+        down[96 * h : 96 * h + 48, :] = quarters[0]
+        down[96 * h + 48 : 96 * h + 96, :] = quarters[1]
+        ups.append(quarters[2:])
     up[...] = jnp.concatenate(
         [ups[h][e][:, 48 * f : 48 * f + 48] for f in range(F) for h in range(2) for e in range(2)], axis=1
     )
-    heads = [every[2 * z, 64:112, :].astype(f32) + every[2 * z + 1, 64:112, :].astype(f32) for z in range(4)]
+    total = every[0, 144:192, :].astype(f32)
+    for z in range(1, 4):
+        total += every[z, 144:192, :].astype(f32)
+    out[...] = total
+    heads = [every[z, 96:144, :].astype(f32) for z in range(4)]
     for t in range(3):
         qkv[:, D * t : D * t + D] = jnp.concatenate(
             [heads[z][:, WIDE * t : WIDE * t + WIDE] for z in range(4)], axis=1
@@ -583,26 +593,31 @@
     after = lax.optimization_barrier
 
     token_other = swap(tokens, "ctx", NBLK, 1)
-    token_other, vectors = after((token_other, vectors))
+    heads_out = call(
+        pack_heads_kernel,
+        "pack_heads",
+        shape((8, 96, D), bf16),
+        [VM, VM, HB, HB],
+        [pltpu.VMEM((96, D), bf16), pltpu.VMEM((48, 3 * D), bf16), dma(10)],
+        mib=56,
+        flops=10**6,
+        nbytes=2 * 10**6,
+        out_specs=HB,
+    )(vectors, b_up.reshape(1, 192), w_qkv, w_out)
+    w_up, heads_out, token_other = after((w_up, heads_out, token_other))
     pair = jnp.stack([tokens, token_other])
     pairs = [swap(pair, "ctx", NBLK, 2 * k) for k in (1, 2, 3)]
-    heads_out, feed_out = call(
-        pack_kernel,
-        "pack",
-        (shape((8, 96, D), bf16), shape((8, 192, D), bf16)),
-        [VM, VM] + [HB] * 4,
-        [
-            pltpu.VMEM((96, D), bf16),
-            pltpu.VMEM((192, D), bf16),
-            pltpu.VMEM((48, 3 * D), bf16),
-            pltpu.VMEM((48, FF), bf16),
-            dma(20),
-        ],
+    feed_out = call(
+        pack_feed_kernel,
+        "pack_feed",
+        shape((8, 192, D), bf16),
+        [HB] * 2,
+        [pltpu.VMEM((192, D), bf16), pltpu.VMEM((48, FF), bf16), dma(10)],
         mib=56,
         flops=10**6,
-        nbytes=5 * 10**6,
-        out_specs=(HB, HB),
-    )(vectors, b_up.reshape(1, 192), w_qkv, w_out, w_up, w_down)
+        nbytes=4 * 10**6,
+        out_specs=HB,
+    )(w_up, w_down)
     w1_mine = a2a(heads_out, "fsdp", CHIPS)
     w1_mine, feed_out, *pairs = after((w1_mine, feed_out, *pairs))
     w2_mine = a2a(feed_out, "fsdp", CHIPS)
@@ -623,6 +638,7 @@
             pltpu.VMEM((BLK, D + 128), f32),
             dma(6),
         ],
+        mib=56,
         flops=2 * BLK * D * D,
         nbytes=4 * 10**6,
         out_specs=(VM, HB, HB),
@@ -694,62 +710,58 @@
         nbytes=4 * 10**6,
         out_specs=(HB,) * 7 + (VM,),
     )(second_cot, keep, came, rows, first_hat, w1_mine, w1_other, *mixes)
-    feed_came, back1 = after((feed_came, back1))
+    def add(one, two):
+        return (one.astype(f32) + two.astype(f32)).astype(bf16)
+
+    feed_pair, back1, back2, back3 = after((add(feed_keep, feed_came), back1, back2, back3))
+    feed_parts = a2a(feed_pair, "fsdp", CHIPS)
     cots = [back0] + [swap(back, "ctx", NBLK, 2 * (k + 1)) for k, back in enumerate((back1, back2, back3))]
     out_came = swap(out_send, "fsdp", F, 1)
 
-    def add(one, two):
-        return (one.astype(f32) + two.astype(f32)).astype(bf16)
-
-    feed_pair = call(pair_kernel, "pair", shape((8, 240, D), bf16), [VM] * 4, mib=56, flops=10**6, nbytes=9 * 10**6)(
-        feed_keep, feed_came, out_keep, out_came
-    )
-    feed_parts = a2a(feed_pair, "fsdp", CHIPS)
     *head_cots, part0, part1, part2, part3 = attend_back(block_seq, w1_mine, w1_other, cots, kept)
     partials = (part0, part1, part2, part3)
     head_keep, head_send = head_grad(blocks, head_cots, (first_sums, second_sums, up_sums))
     head_came = swap(head_send, "fsdp", F, 1)
     token_parts = [swap(partials[k], "ctx", NBLK, 2 * k) for k in (1, 2, 3)]
-    head_pair, *token_parts = after((add(head_keep, head_came), *token_parts))
-    head_parts = a2a(head_pair, "fsdp", CHIPS)
+    pair = call(pair_kernel, "pair", shape((8, 96, D), bf16), [VM] * 4, flops=10**6, nbytes=4 * 10**6)(
+        head_keep, head_came, out_keep, out_came
+    )
+    head_parts = a2a(pair, "fsdp", CHIPS)
 
     part0, part1, part2, part3 = call(
         feed_sum_kernel,
         "feed_sum",
-        (shape((64, D), bf16),) * 4,
+        (shape((48, D), bf16),) * 4,
         [VM],
-        [pltpu.VMEM((4, 64, D), bf16), dma(4)],
+        [pltpu.VMEM((4, 48, D), bf16), dma(4)],
         mib=56,
         flops=10**6,
         nbytes=3 * 10**6,
         out_specs=(HB,) * 4,
     )(feed_parts)
     parts = [part0] + [swap(part, "ctx", NBLK, bit) for part, bit in ((part1, 1), (part2, 4), (part3, 5))]
-    copies = call(
-        last_sum_kernel,
-        "last_sum",
-        shape((NBLK, 112, D), bf16),
-        [VM] * 5,
-        [pltpu.VMEM((112, D), bf16), dma(NBLK)],
-        mib=56,
-        flops=10**6,
-        nbytes=4 * 10**6,
-        out_specs=HB,
-    )(head_parts, *parts)
+    head_parts, token_parts, parts = after((head_parts, token_parts, parts))
+    total = call(last_sum_kernel, "last_sum", shape((144, D), bf16), [VM] * 5, flops=10**6, nbytes=2 * 10**6)(
+        head_parts, *parts
+    )
+    merged = call(merge_kernel, "merge", shape((192, D), bf16), [VM] * 2, flops=10**6, nbytes=10**6)(
+        total, swap(total, "ctx", NBLK, 1)
+    )
+    every = [merged] + [swap(merged, "ctx", NBLK, 2 * k) for k in (1, 2, 3)]
     by_z = partials[0].astype(f32)
     for part in token_parts:
         by_z += part.astype(f32)
     by_z = by_z.astype(bf16)
     tokens_grad = input_cot + by_z[0].astype(f32) + swap(by_z[1], "ctx", NBLK, 1).astype(f32)
-    every = a2a(copies, "ctx")
     qkv_grad, out_grad_w, up_grad, down_grad, vectors_grad, bias_grad = call(
         unpack_kernel,
         "unpack",
         (shape((48, 3 * D)), shape((48, D)), shape((48, FF)), shape((192, D)), shape((8, 48)), shape((4, 48))),
-        [VM],
+        [VM] * 4,
+        [pltpu.VMEM((4, 192, D), bf16)],
         flops=10**6,
         nbytes=4 * 10**6,
-    )(every)
+    )(*every)
     return (layer_out, tokens_grad, qkv_grad, out_grad_w, up_grad, down_grad, vectors_grad, bias_grad.reshape(192))
 
 

time: 233 us -> 208 us (0.89)
  waiting for transfers between devices: 92.8 us -> 76.2 us
  local copies, waits for them, and re-layouts: 15.5 us -> 11.2 us
    ppermute x26 -> x30, waiting for transfers between devices: 91.3 us -> 75.5 us  [swap(): return lax.ppermute(x, axis, [(i, i ^ bit) for i in range(size)])]
    all_to_all x5 -> x4, starting transfers between devices: 27.6 us -> 21.6 us  [a2a(): return lax.all_to_all(x, axis, 0, 0, tiled=True, axis_index_groups=groups)]
    ppermute x26 -> x30, starting transfers between devices: 33.8 us -> 39.7 us  [swap(): return lax.ppermute(x, axis, [(i, i ^ bit) for i in range(size)])]
    pallas_call x4 -> x6, Pallas kernels: 14.1 us -> 9.77 us  [the longest x1 2.88 us: body(): call(pack_heads_kernel, 'pack_heads', shape((8, 96, D), bf16), [VM, VM, H...]
    unnamed x86 -> x72, local copies, waits for them, and re-layouts: 13.6 us -> 9.29 us
    pallas_call x1, Pallas kernels: 1.55 us -> 4.54 us  [body(): call(first_kernel, 'first', (shape((BLK, D), bf16), shape((BLK, D)), shap...]
  transfers between devices with their start and end apart: 31 -> 34, of which waited for: 21 -> 21; matrix products, arithmetic and copies ran while one was open for 2% -> 1% of each run, Pallas kernels for 16% -> 22%
where the time goes in v3:
time: 208 us
  waiting for transfers between devices  76.2 us (37%)
  starting transfers between devices  61.3 us (29%)
  Pallas kernels  54.9 us (26%)
  local copies, waits for them, and re-layouts  11.2 us (5%)
  other arithmetic  3.04 us (1%)
    ppermute x30, waiting for transfers between devices, swap(): return lax.ppermute(x, axis, [(i, i ^ bit) for i in range(size)])  75.5 us
    ppermute x30, starting transfers between devices, swap(): return lax.ppermute(x, axis, [(i, i ^ bit) for i in range(size)])  39.7 us
    all_to_all x4, starting transfers between devices, a2a(): return lax.all_to_all(x, axis, 0, 0, tiled=True, axis_index_groups=groups)  21.6 us
    pallas_call x1, Pallas kernels, attend_back(): call(attend_back_kernel, 'attend_back', (shape((4 * BLK, WIDE), bf16), sh...  11.3 us
    pallas_call x1, Pallas kernels, attend(): call(attend_kernel, 'attend', (shape((16, D)),) + KEPT + (shape((BLK, WID...  10.5 us
    unnamed x72, local copies, waits for them, and re-layouts  9.29 us
    pallas_call x1, Pallas kernels, head_grad(): call(head_grad_kernel, 'head_grad', (half, half), [HB] * 5 + [VM] * 6, [p...  5.2 us
    pallas_call x1, Pallas kernels, body(): call(first_kernel, 'first', (shape((BLK, D), bf16), shape((BLK, D)), shap...  4.54 us
  transfers between devices with their start and end apart: 34, of which 21 were waited for; matrix products, arithmetic and copies ran while one was open for 1% of the time, Pallas kernels for 22%

profile of v3, /device:TPU:0, one launch (start us, length us, event | category | flops | bytes accessed | tf_op | source)
XLA Modules:
  0.0 207.7 jit_solution(15065547859173586682)
XLA Ops:
  0.6 3.2 %collective-permute-start = (bf16[128,768]{1,0:T(8,128)(2,1)}, bf16[128,768]{1,0:T(8,128)(2,1)S(1)}, u32[]{:S(2)}, u32[]{:S(2)}) collective-permute-start(bf16[128,768]{1,0:T(8,128)(2,1)} %tokens.5), channel_id=1, source_target_pairs={{0,1},{1,0},{2,3},{3,2},{4,5},{5,4},{6,7},{7,6},{8,9},{9,8},{10,11... | collective-permute-start | bytes 589832 | tf_op jit(solution)/shard_map/ppermute | solution.py:585
  3.8 1.2 reshape.24.b_up
  5.1 2.9 %pack_heads.1 = bf16[8,96,768]{2,1,0:T(8,128)(2,1)} custom-call(bf16[8,48]{1,0:T(8,128)(2,1)} %vectors.1, bf16[1,192]{1,0:T(2,128)(2,1)} %reshape.24.b_up, bf16[48,2304]{1,0:T(8,128)(2,1)} %w_qkv.1, bf16[48,768]{1,0:T(8,128)(2,1)} %w_out.1), custom_call_target="tpu_custom_call" | custom-call | flops 1000000 | bytes 2000000 | tf_op jit(solution)/shard_map/pack_heads/pallas_call | solution.py:596
  7.9 1.0 collective-permute-done.other
  8.9 5.6 %all-to-all-start = ((bf16[8,96,768]{2,1,0:T(8,128)(2,1)}), bf16[8,96,768]{2,1,0:T(8,128)(2,1)S(1)}, u32[]{:S(2)}, u32[]{:S(2)}) async-start(bf16[8,96,768]{2,1,0:T(8,128)(2,1)} %pack_heads.1), calls=%async_computation | async-start | bytes 2359296 | tf_op jit(solution)/shard_map/all_to_all | solution.py:589
  14.6 4.1 %collective-permute-start.3 = (bf16[2,128,768]{2,1,0:T(8,128)(2,1)S(1)}, bf16[2,128,768]{2,1,0:T(8,128)(2,1)S(1)}, u32[]{:S(2)}, u32[]{:S(2)}) collective-permute-start(bf16[2,128,768]{2,1,0:T(8,128)(2,1)S(1)} %pad_maximum_fusion), channel_id=1, source_target_pairs={{0,6},{1,7},{2,4},{3,5},{4,2},{5,3},{6,0},{7,1},{8,14},{9,15},{10,... | collective-permute-start | bytes 1179656 | tf_op jit(solution)/shard_map/ppermute | solution.py:585
  18.7 0.9 collective-permute-start.1
  19.7 2.6 %pack_feed.1 = bf16[8,192,768]{2,1,0:T(8,128)(2,1)} custom-call(bf16[48,3072]{1,0:T(8,128)(2,1)} %w_up, bf16[192,768]{1,0:T(8,128)(2,1)} %w_down.1), custom_call_target="tpu_custom_call" | custom-call | flops 1000000 | bytes 4000000 | tf_op jit(solution)/shard_map/pack_feed/pallas_call | solution.py:610
  22.3 12.8 %collective-permute-done.3.pair3 = bf16[2,128,768]{2,1,0:T(8,128)(2,1)S(1)} collective-permute-done((bf16[2,128,768]{2,1,0:T(8,128)(2,1)S(1)}, bf16[2,128,768]{2,1,0:T(8,128)(2,1)S(1)}, u32[]{:S(2)}, u32[]{:S(2)}) %collective-permute-start.3) | collective-permute-done | bytes 393248 | tf_op jit(solution)/shard_map/ppermute | solution.py:585
  35.1 0.7 collective-permute-done.1.pair1
  36.6 5.4 %all-to-all-start.1 = ((bf16[8,192,768]{2,1,0:T(8,128)(2,1)}), bf16[8,192,768]{2,1,0:T(8,128)(2,1)S(1)}, u32[]{:S(2)}, u32[]{:S(2)}) async-start(bf16[8,192,768]{2,1,0:T(8,128)(2,1)} %pack_feed.1), calls=%async_computation.1 | async-start | bytes 4718592 | tf_op jit(solution)/shard_map/all_to_all | solution.py:589
  42.0 2.8 %collective-permute-done.4.w_other = bf16[8,96,768]{2,1,0:T(8,128)(2,1)S(1)} collective-permute-done((bf16[8,96,768]{2,1,0:T(8,128)(2,1)S(1)}, bf16[8,96,768]{2,1,0:T(8,128)(2,1)S(1)}, u32[]{:S(2)}, u32[]{:S(2)}) %collective-permute-start.4) | collective-permute-done | bytes 1179680 | tf_op jit(solution)/shard_map/ppermute | solution.py:585
  44.8 1.1 copy-done.2
  46.0 10.5 %attend.1 = (f32[16,768]{1,0:T(8,128)}, bf16[4,3,128,512]{3,2,1,0:T(8,128)(2,1)}, bf16[3,512,64]{2,1,0:T(8,128)(2,1)}, bf16[3,1024,64]{2,1,0:T(8,128)(2,1)}, bf1...) custom-call(s32[1,3]{1,0:T(1,128)} %lengths.1, ...), custom_call_target="tpu_custom_call" | custom-call | flops 2000000000 | bytes 6000000 | tf_op jit(solution)/shard_map/attend/pallas_call | solution.py:182
  56.5 1.2 collective-permute-start.5
  57.7 3.2 %collective-permute-start.6 = (bf16[128,192]{1,0:T(8,128)(2,1)}, bf16[128,192]{1,0:T(8,128)(2,1)S(1)}, u32[]{:S(2)}, u32[]{:S(2)}) collective-permute-start(bf16[128,192]{1,0:T(8,128)(2,1)} %get-tuple-element.95), channel_id=1, source_target_pairs={{0,4},{1,5},{2,6},{3,7},{4,0},{5,1},{6,2},{7,3},{8,12},{9,13},{10,... | collective-permute-start | bytes 147464 | tf_op jit(solution)/shard_map/ppermute | solution.py:585
  61.3 3.4 %collective-permute-done.6.mix2 = bf16[128,192]{1,0:T(8,128)(2,1)S(1)} collective-permute-done((bf16[128,192]{1,0:T(8,128)(2,1)}, bf16[128,192]{1,0:T(8,128)(2,1)S(1)}, u32[]{:S(2)}, u32[]{:S(2)}) %collective-permute-start.6) | collective-permute-done | bytes 49184 | tf_op jit(solution)/shard_map/ppermute | solution.py:585
  64.6 1.9 collective-permute-done.7.mix3
  67.2 4.5 %first.1 = (bf16[128,768]{1,0:T(8,128)(2,1)}, f32[128,768]{1,0:T(8,128)}, f32[128,896]{1,0:T(8,128)}) custom-call(bf16[128,192]{1,0:T(8,128)(2,1)} %get-tuple-element.93.mix0, bf16[128,192]{1,0:T(8,128)(2,1)} %copy-done.9, bf16[128,192]{1,0:T(8,128)(2,1)} %copy-done.11, bf16[128,192]{1,0:T(8,128)(2,1)} %copy-done.13, bf16[8,96,768]{2,1,0:T(8,128)(2,1)} %copy-done, ...), custom_call_target="tpu_custom_call" | custom-call | flops 150994944 | bytes 4000000 | tf_op jit(solution)/shard_map/first/pallas_call | solution.py:629
  72.0 7.4 %collective-permute-done.8.other.low_other = bf16[128,768]{1,0:T(8,128)(2,1)S(1)} collective-permute-done((bf16[128,768]{1,0:T(8,128)(2,1)}, bf16[128,768]{1,0:T(8,128)(2,1)S(1)}, u32[]{:S(2)}, u32[]{:S(2)}) %collective-permute-start.8) | collective-permute-done | bytes 196640 | tf_op jit(solution)/shard_map/ppermute | solution.py:585
  79.4 0.9 copy-done.15
  80.3 3.0 %feed.1 = (bf16[256,1536]{1,0:T(8,128)(2,1)S(1)}, bf16[256,1536]{1,0:T(8,128)(2,1)S(1)}, f32[128,768]{1,0:T(8,128)S(1)}, bf16[128,768]{1,0:T(8,128)(2,1)S(1)}) custom-call(bf16[128,768]{1,0:T(8,128)(2,1)S(1)} %copy-done.15, bf16[128,768]{1,0:T(8,128)(2,1)S(1)} %collective-permute-done.8.other.low_other, bf16[8,192,768]{2,1,0:T(8,128)(2,1)S(1)} %all-to-all-done.1.w_mine, ...), custom_call_target="tpu_custom_call" | custom-call | flops 1207959552 | bytes 8000000 | tf_op jit(solution)/shard_map/feed/pallas_call | solution.py:650
  83.7 6.2 %collective-permute-done.10.came = bf16[128,768]{1,0:T(8,128)(2,1)S(1)} collective-permute-done((bf16[128,768]{1,0:T(8,128)(2,1)S(1)}, bf16[128,768]{1,0:T(8,128)(2,1)S(1)}, u32[]{:S(2)}, u32[]{:S(2)}) %collective-permute-start.10) | collective-permute-done | bytes 196640 | tf_op jit(solution)/shard_map/ppermute | solution.py:585
  89.8 1.0 second.1
  91.3 5.2 %collective-permute-done.11.other = bf16[128,768]{1,0:T(8,128)(2,1)S(1)} collective-permute-done((bf16[128,768]{1,0:T(8,128)(2,1)S(1)}, bf16[128,768]{1,0:T(8,128)(2,1)S(1)}, u32[]{:S(2)}, u32[]{:S(2)}) %collective-permute-start.11) | collective-permute-done | bytes 196640 | tf_op jit(solution)/shard_map/ppermute | solution.py:585
  96.5 2.5 %feed_back.1 = (bf16[256,1536]{1,0:T(8,128)(2,1)S(1)}, f32[128,768]{1,0:T(8,128)S(1)}, bf16[128,768]{1,0:T(8,128)(2,1)S(1)}, f32[2,768]{1,0:T(2,128)S(1)}) custom-call(bf16[128,768]{1,0:T(8,128)(2,1)S(1)} %get-tuple-element.106.mine, bf16[128,768]{1,0:T(8,128)(2,1)S(1)} %collective-permute-done.11.other, bf16[8,192,768]{2,1,0:T(8,128)(2,1)S(1)} %all-to-all-done.1.w_mine, ...), custom_call_target="tpu_custom_call" | custom-call | flops 1207959552 | bytes 8000000 | tf_op jit(solution)/shard_map/feed_back/pallas_call | solution.py:669
  100.3 1.8 feed_grad.1
  102.1 3.3 %collective-permute-done.12.came = bf16[128,768]{1,0:T(8,128)(2,1)S(1)} collective-permute-done((bf16[128,768]{1,0:T(8,128)(2,1)S(1)}, bf16[128,768]{1,0:T(8,128)(2,1)S(1)}, u32[]{:S(2)}, u32[]{:S(2)}) %collective-permute-start.12) | collective-permute-done | bytes 196640 | tf_op jit(solution)/shard_map/ppermute | solution.py:585
  105.5 3.7 %first_back.1 = (f32[128,768]{1,0:T(8,128)S(1)}, bf16[8,48,768]{2,1,0:T(8,128)(2,1)S(1)}, bf16[8,48,768]{2,1,0:T(8,128)(2,1)S(1)}, bf16[128,192]{1,0:T(8,128)(2,...) custom-call(f32[128,768]{1,0:T(8,128)S(1)} %get-tuple-element.105.co, ...), custom_call_target="tpu_custom_call" | custom-call | flops 301989888 | bytes 4000000 | tf_op jit(solution)/shard_map/first_back/pallas_call | solution.py:695
  109.2 0.8 copy-done.19
  110.7 0.6 copy-done.22
  111.9 2.0 add_convert_fusion
  113.9 5.8 %all-to-all-start.3 = ((bf16[8,192,768]{2,1,0:T(8,128)(2,1)}), bf16[8,192,768]{2,1,0:T(8,128)(2,1)}, u32[]{:S(2)}, u32[]{:S(2)}) async-start(bf16[8,192,768]{2,1,0:T(8,128)(2,1)} %add_convert_fusion), calls=%async_computation.3 | async-start | bytes 4718592 | tf_op jit(solution)/shard_map/all_to_all | solution.py:589
  120.4 1.8 collective-permute-start.15
  122.2 2.3 %collective-permute-start.16 = (bf16[128,192]{1,0:T(8,128)(2,1)S(1)}, bf16[128,192]{1,0:T(8,128)(2,1)S(1)}, u32[]{:S(2)}, u32[]{:S(2)}) collective-permute-start(bf16[128,192]{1,0:T(8,128)(2,1)S(1)} %get-tuple-element.124), channel_id=1, source_target_pairs={{0,6},{1,7},{2,4},{3,5},{4,2},{5,3},{6,0},{7,1},{8,14},{9,15},{10,... | collective-permute-start | bytes 147464 | tf_op jit(solution)/shard_map/ppermute | solution.py:585
  124.7 1.4 collective-permute-done.15.refs_2_
  126.2 1.5 collective-permute-done.16.refs_3_
  128.3 11.3 %attend_back.1 = (bf16[512,192]{1,0:T(8,128)(2,1)}, bf16[1024,192]{1,0:T(8,128)(2,1)}, bf16[1024,192]{1,0:T(8,128)(2,1)}, bf16[2,128,768]{2,1,0:T(8,128)(2,1)}, ...) custom-call(s32[1,8]{1,0:T(1,128)} %block_seq.3, ...), custom_call_target="tpu_custom_call" | custom-call | flops 4000000000 | bytes 8000000 | tf_op jit(solution)/shard_map/attend_back/pallas_call | solution.py:254
  139.6 5.2 %head_grad.1 = (bf16[8,48,768]{2,1,0:T(8,128)(2,1)}, bf16[8,48,768]{2,1,0:T(8,128)(2,1)}) custom-call(bf16[128,768]{1,0:T(8,128)(2,1)} %tokens.5, bf16[128,768]{1,0:T(8,128)(2,1)} %copy-done.29, bf16[2,128,768]{2,1,0:T(8,128)(2,1)} %copy-done.32, bf16[2,128,768]{2,1,0:T(8,128)(2,1)} %copy-done.31, bf16[2,128,768]{2,1,0:T(8,128)(2,1)} %copy-done.30, ...), custom_call_target="tpu_custom_call" | custom-call | flops 2000000000 | bytes 4000000 | tf_op jit(solution)/shard_map/head_grad/pallas_call | solution.py:316
  144.9 2.2 %collective-permute-done.17.head_came = bf16[8,48,768]{2,1,0:T(8,128)(2,1)S(1)} collective-permute-done((bf16[8,48,768]{2,1,0:T(8,128)(2,1)}, bf16[8,48,768]{2,1,0:T(8,128)(2,1)S(1)}, u32[]{:S(2)}, u32[]{:S(2)}) %collective-permute-start.17) | collective-permute-done | bytes 589856 | tf_op jit(solution)/shard_map/ppermute | solution.py:585
  147.1 1.1 copy-done.5
  148.2 1.3 pair.1
  149.5 0.8 all-to-all-done.3.parts
  150.3 4.7 %all-to-all-start.2 = ((bf16[8,96,768]{2,1,0:T(8,128)(2,1)}), bf16[8,96,768]{2,1,0:T(8,128)(2,1)S(1)}, u32[]{:S(2)}, u32[]{:S(2)}) async-start(bf16[8,96,768]{2,1,0:T(8,128)(2,1)} %pair.1), calls=%async_computation.2 | async-start | bytes 2359296 | tf_op jit(solution)/shard_map/all_to_all | solution.py:589
  155.3 3.7 %collective-permute-start.20 = (bf16[2,128,768]{2,1,0:T(8,128)(2,1)}, bf16[2,128,768]{2,1,0:T(8,128)(2,1)S(1)}, u32[]{:S(2)}, u32[]{:S(2)}) collective-permute-start(bf16[2,128,768]{2,1,0:T(8,128)(2,1)} %get-tuple-element.141), channel_id=1, source_target_pairs={{0,4},{1,5},{2,6},{3,7},{4,0},{5,1},{6,2},{7,3},{8,12},{9,13},{10,... | collective-permute-start | bytes 1179656 | tf_op jit(solution)/shard_map/ppermute | solution.py:585
  159.0 0.8 collective-permute-start.21
  159.8 2.7 %feed_sum.1 = (bf16[48,768]{1,0:T(8,128)(2,1)}, bf16[48,768]{1,0:T(8,128)(2,1)}, bf16[48,768]{1,0:T(8,128)(2,1)}, bf16[48,768]{1,0:T(8,128)(2,1)}) custom-call(bf16[8,192,768]{2,1,0:T(8,128)(2,1)} %all-to-all-done.3.parts), custom_call_target="tpu_custom_call" | custom-call | flops 1000000 | bytes 3000000 | tf_op jit(solution)/shard_map/feed_sum/pallas_call | solution.py:731
  162.5 2.8 %collective-permute-start.22 = (bf16[48,768]{1,0:T(8,128)(2,1)}, bf16[48,768]{1,0:T(8,128)(2,1)S(1)}, u32[]{:S(2)}, u32[]{:S(2)}) collective-permute-start(bf16[48,768]{1,0:T(8,128)(2,1)} %get-tuple-element.145), channel_id=1, source_target_pairs={{0,1},{1,0},{2,3},{3,2},{4,5},{5,4},{6,7},{7,6},{8,9},{9,8},{10,11... | collective-permute-start | bytes 221192 | tf_op jit(solution)/shard_map/ppermute | solution.py:585
  165.4 0.7 collective-permute-start.23
  166.1 1.2 collective-permute-done.19
  167.3 4.0 %collective-permute-start.24 = (bf16[48,768]{1,0:T(8,128)(2,1)}, bf16[48,768]{1,0:T(8,128)(2,1)S(1)}, u32[]{:S(2)}, u32[]{:S(2)}) collective-permute-start(bf16[48,768]{1,0:T(8,128)(2,1)} %get-tuple-element.147), channel_id=1, source_target_pairs={{0,5},{1,4},{2,7},{3,6},{4,1},{5,0},{6,3},{7,2},{8,13},{9,12},{10,... | collective-permute-start | bytes 221192 | tf_op jit(solution)/shard_map/ppermute | solution.py:585
  171.3 7.6 %collective-permute-done.20 = bf16[2,128,768]{2,1,0:T(8,128)(2,1)S(1)} collective-permute-done((bf16[2,128,768]{2,1,0:T(8,128)(2,1)}, bf16[2,128,768]{2,1,0:T(8,128)(2,1)S(1)}, u32[]{:S(2)}, u32[]{:S(2)}) %collective-permute-start.20) | collective-permute-done | bytes 393248 | tf_op jit(solution)/shard_map/ppermute | solution.py:585
  179.0 3.4 %collective-permute-done.21 = bf16[2,128,768]{2,1,0:T(8,128)(2,1)S(1)} collective-permute-done((bf16[2,128,768]{2,1,0:T(8,128)(2,1)}, bf16[2,128,768]{2,1,0:T(8,128)(2,1)S(1)}, u32[]{:S(2)}, u32[]{:S(2)}) %collective-permute-start.21) | collective-permute-done | bytes 393248 | tf_op jit(solution)/shard_map/ppermute | solution.py:585
  182.4 0.9 copy-done.18
  183.5 2.8 %collective-permute-start.26 = (bf16[144,768]{1,0:T(8,128)(2,1)S(1)}, bf16[144,768]{1,0:T(8,128)(2,1)S(1)}, u32[]{:S(2)}, u32[]{:S(2)}) collective-permute-start(bf16[144,768]{1,0:T(8,128)(2,1)S(1)} %last_sum.1.own), channel_id=1, source_target_pairs={{0,1},{1,0},{2,3},{3,2},{4,5},{5,4},{6,7},{7,6},{8,9},{9,8},{10,11... | collective-permute-start | bytes 663560 | tf_op jit(solution)/shard_map/ppermute | solution.py:585
  186.5 0.9 collective-permute-start.25
  187.4 5.7 %collective-permute-done.26.other = bf16[144,768]{1,0:T(8,128)(2,1)S(1)} collective-permute-done((bf16[144,768]{1,0:T(8,128)(2,1)S(1)}, bf16[144,768]{1,0:T(8,128)(2,1)S(1)}, u32[]{:S(2)}, u32[]{:S(2)}) %collective-permute-start.26) | collective-permute-done | bytes 221216 | tf_op jit(solution)/shard_map/ppermute | solution.py:585
  193.1 0.9 collective-permute-start.29
  194.0 3.3 %collective-permute-start.27 = (bf16[192,768]{1,0:T(8,128)(2,1)S(1)}, bf16[192,768]{1,0:T(8,128)(2,1)S(1)}, u32[]{:S(2)}, u32[]{:S(2)}) collective-permute-start(bf16[192,768]{1,0:T(8,128)(2,1)S(1)} %merge.1.one0), channel_id=1, source_target_pairs={{0,2},{1,3},{2,0},{3,1},{4,6},{5,7},{6,4},{7,5},{8,10},{9,11},{10,... | collective-permute-start | bytes 884744 | tf_op jit(solution)/shard_map/ppermute | solution.py:585
  197.3 0.8 fusion
  198.1 6.6 %collective-permute-done.29.one3 = bf16[192,768]{1,0:T(8,128)(2,1)S(1)} collective-permute-done((bf16[192,768]{1,0:T(8,128)(2,1)S(1)}, bf16[192,768]{1,0:T(8,128)(2,1)S(1)}, u32[]{:S(2)}, u32[]{:S(2)}) %collective-permute-start.29) | collective-permute-done | bytes 294944 | tf_op jit(solution)/shard_map/ppermute | solution.py:585
  204.8 0.7 collective-permute-done.27.one1
  205.4 1.6 unpack.1
  207.1 0.6 reshape.25
  (99 shorter events, 7.6 us)
Async XLA Ops:
  0.6 13.9 %copy-start.27 = (bf16[128,768]{1,0:T(8,128)(2,1)S(1)}, bf16[128,768]{1,0:T(8,128)(2,1)}, u32[]{:S(2)}) copy-start(bf16[128,768]{1,0:T(8,128)(2,1)} %tokens.5) | copy-start | bytes 589828
  0.6 8.3 %collective-permute-start = (bf16[128,768]{1,0:T(8,128)(2,1)}, bf16[128,768]{1,0:T(8,128)(2,1)S(1)}, u32[]{:S(2)}, u32[]{:S(2)}) collective-permute-start(bf16[128,768]{1,0:T(8,128)(2,1)} %tokens.5), channel_id=1, source_target_pairs={{0,1},{1,0},{2,3},{3,2},{4,5},{5,4},{6,7},{7,6},{8,9},{9,8},{10,11... | collective-permute-start | bytes 589832 | tf_op jit(solution)/shard_map/ppermute | solution.py:585
  8.9 13.4 %copy-start.29 = (bf16[128,768]{1,0:T(8,128)(2,1)}, bf16[128,768]{1,0:T(8,128)(2,1)S(1)}, u32[]{:S(2)}) copy-start(bf16[128,768]{1,0:T(8,128)(2,1)S(1)} %collective-permute-done.other) | copy-start | bytes 589828
  8.9 26.9 %all-to-all-start = ((bf16[8,96,768]{2,1,0:T(8,128)(2,1)}), bf16[8,96,768]{2,1,0:T(8,128)(2,1)S(1)}, u32[]{:S(2)}, u32[]{:S(2)}) async-start(bf16[8,96,768]{2,1,0:T(8,128)(2,1)} %pack_heads.1), calls=%async_computation | async-start | bytes 2359296 | tf_op jit(solution)/shard_map/all_to_all | solution.py:589
  14.6 20.5 %collective-permute-start.3 = (bf16[2,128,768]{2,1,0:T(8,128)(2,1)S(1)}, bf16[2,128,768]{2,1,0:T(8,128)(2,1)S(1)}, u32[]{:S(2)}, u32[]{:S(2)}) collective-permute-start(bf16[2,128,768]{2,1,0:T(8,128)(2,1)S(1)} %pad_maximum_fusion), channel_id=1, source_target_pairs={{0,6},{1,7},{2,4},{3,5},{4,2},{5,3},{6,0},{7,1},{8,14},{9,15},{10,... | collective-permute-start | bytes 1179656 | tf_op jit(solution)/shard_map/ppermute | solution.py:585
  18.7 16.4 %collective-permute-start.2 = (bf16[2,128,768]{2,1,0:T(8,128)(2,1)S(1)}, bf16[2,128,768]{2,1,0:T(8,128)(2,1)S(1)}, u32[]{:S(2)}, u32[]{:S(2)}) collective-permute-start(bf16[2,128,768]{2,1,0:T(8,128)(2,1)S(1)} %pad_maximum_fusion), channel_id=1, source_target_pairs={{0,4},{1,5},{2,6},{3,7},{4,0},{5,1},{6,2},{7,3},{8,12},{9,13},{10,... | collective-permute-start | bytes 1179656 | tf_op jit(solution)/shard_map/ppermute | solution.py:585
  18.7 17.1 %collective-permute-start.1 = (bf16[2,128,768]{2,1,0:T(8,128)(2,1)S(1)}, bf16[2,128,768]{2,1,0:T(8,128)(2,1)S(1)}, u32[]{:S(2)}, u32[]{:S(2)}) collective-permute-start(bf16[2,128,768]{2,1,0:T(8,128)(2,1)S(1)} %pad_maximum_fusion), channel_id=1, source_target_pairs={{0,2},{1,3},{2,0},{3,1},{4,6},{5,7},{6,4},{7,5},{8,10},{9,11},{10,... | collective-permute-start | bytes 1179656 | tf_op jit(solution)/shard_map/ppermute | solution.py:585
  35.1 0.8 copy-start.30
  35.1 0.9 copy-start.31
  35.8 0.7 copy-start.32
  35.8 9.0 %copy-start = (bf16[8,96,768]{2,1,0:T(8,128)(2,1)}, bf16[8,96,768]{2,1,0:T(8,128)(2,1)S(1)}, u32[]{:S(2)}) copy-start(bf16[8,96,768]{2,1,0:T(8,128)(2,1)S(1)} %all-to-all-done.w_mine) | copy-start | bytes 3538948
  36.6 35.2 %all-to-all-start.1 = ((bf16[8,192,768]{2,1,0:T(8,128)(2,1)}), bf16[8,192,768]{2,1,0:T(8,128)(2,1)S(1)}, u32[]{:S(2)}, u32[]{:S(2)}) async-start(bf16[8,192,768]{2,1,0:T(8,128)(2,1)} %pack_feed.1), calls=%async_computation.1 | async-start | bytes 4718592 | tf_op jit(solution)/shard_map/all_to_all | solution.py:589
  42.0 2.8 %collective-permute-start.4 = (bf16[8,96,768]{2,1,0:T(8,128)(2,1)S(1)}, bf16[8,96,768]{2,1,0:T(8,128)(2,1)S(1)}, u32[]{:S(2)}, u32[]{:S(2)}) collective-permute-start(bf16[8,96,768]{2,1,0:T(8,128)(2,1)S(1)} %all-to-all-done.w_mine), channel_id=1, source_target_pairs={{0,8},{8,0},{16,24},{24,16},{32,40},{40,32},{48,56},{56,48},{64,72... | collective-permute-start | bytes 3538952 | tf_op jit(solution)/shard_map/ppermute | solution.py:585
  44.8 1.1 copy-start.2
  56.5 22.9 %copy-start.4 = (f32[16,768]{1,0:T(8,128)S(1)}, f32[16,768]{1,0:T(8,128)}, u32[]{:S(2)}) copy-start(f32[16,768]{1,0:T(8,128)} %get-tuple-element.97.vectors) | copy-start | bytes 147460
  56.5 4.8 %collective-permute-start.5 = (bf16[128,192]{1,0:T(8,128)(2,1)}, bf16[128,192]{1,0:T(8,128)(2,1)S(1)}, u32[]{:S(2)}, u32[]{:S(2)}) collective-permute-start(bf16[128,192]{1,0:T(8,128)(2,1)} %get-tuple-element.94), channel_id=1, source_target_pairs={{0,2},{1,3},{2,0},{3,1},{4,6},{5,7},{6,4},{7,5},{8,10},{9,11},{10,... | collective-permute-start | bytes 147464 | tf_op jit(solution)/shard_map/ppermute | solution.py:585
  57.7 7.0 %collective-permute-start.6 = (bf16[128,192]{1,0:T(8,128)(2,1)}, bf16[128,192]{1,0:T(8,128)(2,1)S(1)}, u32[]{:S(2)}, u32[]{:S(2)}) collective-permute-start(bf16[128,192]{1,0:T(8,128)(2,1)} %get-tuple-element.95), channel_id=1, source_target_pairs={{0,4},{1,5},{2,6},{3,7},{4,0},{5,1},{6,2},{7,3},{8,12},{9,13},{10,... | collective-permute-start | bytes 147464 | tf_op jit(solution)/shard_map/ppermute | solution.py:585
  60.9 5.7 %collective-permute-start.7 = (bf16[128,192]{1,0:T(8,128)(2,1)}, bf16[128,192]{1,0:T(8,128)(2,1)S(1)}, u32[]{:S(2)}, u32[]{:S(2)}) collective-permute-start(bf16[128,192]{1,0:T(8,128)(2,1)} %get-tuple-element.96), channel_id=1, source_target_pairs={{0,6},{1,7},{2,4},{3,5},{4,2},{5,3},{6,0},{7,1},{8,14},{9,15},{10,... | collective-permute-start | bytes 147464 | tf_op jit(solution)/shard_map/ppermute | solution.py:585
  61.3 5.3 %copy-start.9 = (bf16[128,192]{1,0:T(8,128)(2,1)}, bf16[128,192]{1,0:T(8,128)(2,1)S(1)}, u32[]{:S(2)}) copy-start(bf16[128,192]{1,0:T(8,128)(2,1)S(1)} %collective-permute-done.5.mix1) | copy-start | bytes 147460
  64.6 2.0 copy-start.11
  71.8 7.6 %collective-permute-start.9 = (bf16[8,192,768]{2,1,0:T(8,128)(2,1)S(1)}, bf16[8,192,768]{2,1,0:T(8,128)(2,1)S(1)}, u32[]{:S(2)}, u32[]{:S(2)}) collective-permute-start(bf16[8,192,768]{2,1,0:T(8,128)(2,1)S(1)} %all-to-all-done.1.w_mine), channel_id=1, source_target_pairs={{0,8},{8,0},{16,24},{24,16},{32,40},{40,32},{48,56},{56,48},{64,72... | collective-permute-start | bytes 7077896 | tf_op jit(solution)/shard_map/ppermute | solution.py:585
  71.9 18.0 %copy-start.7 = (f32[128,768]{1,0:T(8,128)S(1)}, f32[128,768]{1,0:T(8,128)}, u32[]{:S(2)}) copy-start(f32[128,768]{1,0:T(8,128)} %get-tuple-element.99.norm) | copy-start | bytes 1179652
  71.9 7.5 %collective-permute-start.8 = (bf16[128,768]{1,0:T(8,128)(2,1)}, bf16[128,768]{1,0:T(8,128)(2,1)S(1)}, u32[]{:S(2)}, u32[]{:S(2)}) collective-permute-start(bf16[128,768]{1,0:T(8,128)(2,1)} %get-tuple-element.100.mine.low_mine), channel_id=1, source_target_pairs={{0,2},{1,3},{2,0},{3,1},{4,6},{5,7},{6,4},{7,5},{8,10},{9,11},{10,... | collective-permute-start | bytes 589832 | tf_op jit(solution)/shard_map/ppermute | solution.py:585
  79.4 0.9 copy-start.15
  80.3 9.5 %copy-start.17 = (bf16[128,768]{1,0:T(8,128)(2,1)S(1)}, bf16[128,768]{1,0:T(8,128)(2,1)}, u32[]{:S(2)}) copy-start(bf16[128,768]{1,0:T(8,128)(2,1)} %out_grad.1) | copy-start | bytes 589828
  83.3 6.5 %collective-permute-start.10 = (bf16[128,768]{1,0:T(8,128)(2,1)S(1)}, bf16[128,768]{1,0:T(8,128)(2,1)S(1)}, u32[]{:S(2)}, u32[]{:S(2)}) collective-permute-start(bf16[128,768]{1,0:T(8,128)(2,1)S(1)} %get-tuple-element.103), channel_id=1, source_target_pairs={{0,2},{1,3},{2,0},{3,1},{4,6},{5,7},{6,4},{7,5},{8,10},{9,11},{10,... | collective-permute-start | bytes 589832 | tf_op jit(solution)/shard_map/ppermute | solution.py:585
  90.8 8.2 %copy-start.24 = (f32[3,768]{1,0:T(4,128)}, f32[3,768]{1,0:T(4,128)S(1)}, u32[]{:S(2)}) copy-start(f32[3,768]{1,0:T(4,128)S(1)} %get-tuple-element.134.second_sums) | copy-start | bytes 27652
  90.8 5.7 %collective-permute-start.11 = (bf16[128,768]{1,0:T(8,128)(2,1)S(1)}, bf16[128,768]{1,0:T(8,128)(2,1)S(1)}, u32[]{:S(2)}, u32[]{:S(2)}) collective-permute-start(bf16[128,768]{1,0:T(8,128)(2,1)S(1)} %get-tuple-element.106.mine), channel_id=1, source_target_pairs={{0,2},{1,3},{2,0},{3,1},{4,6},{5,7},{6,4},{7,5},{8,10},{9,11},{10,... | collective-permute-start | bytes 589832 | tf_op jit(solution)/shard_map/ppermute | solution.py:585
  96.5 3.8 %copy-start.16 = (bf16[128,768]{1,0:T(8,128)(2,1)S(1)}, bf16[128,768]{1,0:T(8,128)(2,1)}, u32[]{:S(2)}) copy-start(bf16[128,768]{1,0:T(8,128)(2,1)} %get-tuple-element.100.mine.low_mine) | copy-start | bytes 589828
  99.6 5.8 %copy-start.1 = (bf16[8,96,768]{2,1,0:T(8,128)(2,1)S(1)}, bf16[8,96,768]{2,1,0:T(8,128)(2,1)}, u32[]{:S(2)}) copy-start(bf16[8,96,768]{2,1,0:T(8,128)(2,1)} %copy-done) | copy-start | bytes 3538948
  99.6 5.8 %copy-start.3 = (bf16[8,96,768]{2,1,0:T(8,128)(2,1)S(1)}, bf16[8,96,768]{2,1,0:T(8,128)(2,1)}, u32[]{:S(2)}) copy-start(bf16[8,96,768]{2,1,0:T(8,128)(2,1)} %copy-done.2) | copy-start | bytes 3538948
  99.6 5.8 %copy-start.6 = (f32[128,896]{1,0:T(8,128)S(1)}, f32[128,896]{1,0:T(8,128)}, u32[]{:S(2)}) copy-start(f32[128,896]{1,0:T(8,128)} %get-tuple-element.114.hat) | copy-start | bytes 1376260
  99.7 5.8 %copy-start.8 = (bf16[128,192]{1,0:T(8,128)(2,1)S(1)}, bf16[128,192]{1,0:T(8,128)(2,1)}, u32[]{:S(2)}) copy-start(bf16[128,192]{1,0:T(8,128)(2,1)} %get-tuple-element.93.mix0) | copy-start | bytes 147460
  99.7 5.8 %copy-start.10 = (bf16[128,192]{1,0:T(8,128)(2,1)S(1)}, bf16[128,192]{1,0:T(8,128)(2,1)}, u32[]{:S(2)}) copy-start(bf16[128,192]{1,0:T(8,128)(2,1)} %copy-done.9) | copy-start | bytes 147460
  99.7 5.8 %copy-start.12 = (bf16[128,192]{1,0:T(8,128)(2,1)S(1)}, bf16[128,192]{1,0:T(8,128)(2,1)}, u32[]{:S(2)}) copy-start(bf16[128,192]{1,0:T(8,128)(2,1)} %copy-done.11) | copy-start | bytes 147460
  99.7 5.8 %copy-start.14 = (bf16[128,192]{1,0:T(8,128)(2,1)S(1)}, bf16[128,192]{1,0:T(8,128)(2,1)}, u32[]{:S(2)}) copy-start(bf16[128,192]{1,0:T(8,128)(2,1)} %copy-done.13) | copy-start | bytes 147460
  99.7 5.8 %collective-permute-start.12 = (bf16[128,768]{1,0:T(8,128)(2,1)S(1)}, bf16[128,768]{1,0:T(8,128)(2,1)S(1)}, u32[]{:S(2)}, u32[]{:S(2)}) collective-permute-start(bf16[128,768]{1,0:T(8,128)(2,1)S(1)} %get-tuple-element.112), channel_id=1, source_target_pairs={{0,2},{1,3},{2,0},{3,1},{4,6},{5,7},{6,4},{7,5},{8,10},{9,11},{10,... | collective-permute-start | bytes 589832 | tf_op jit(solution)/shard_map/ppermute | solution.py:585
  105.4 6.5 %collective-permute-start.13 = (bf16[8,192,768]{2,1,0:T(8,128)(2,1)S(1)}, bf16[8,192,768]{2,1,0:T(8,128)(2,1)S(1)}, u32[]{:S(2)}, u32[]{:S(2)}) collective-permute-start(bf16[8,192,768]{2,1,0:T(8,128)(2,1)S(1)} %get-tuple-element.118), channel_id=1, source_target_pairs={{0,8},{8,0},{16,24},{24,16},{32,40},{40,32},{48,56},{56,48},{64,72... | collective-permute-start | bytes 7077896 | tf_op jit(solution)/shard_map/ppermute | solution.py:585
  109.2 0.8 copy-start.19
  113.9 5.8 %copy-start.23 = (bf16[128,192]{1,0:T(8,128)(2,1)S(1)}, bf16[128,192]{1,0:T(8,128)(2,1)}, u32[]{:S(2)}) copy-start(bf16[128,192]{1,0:T(8,128)(2,1)} %copy-done.22) | copy-start | bytes 147460
  113.9 10.6 %copy-start.20 = (bf16[8,48,768]{2,1,0:T(8,128)(2,1)S(1)}, bf16[8,48,768]{2,1,0:T(8,128)(2,1)}, u32[]{:S(2)}) copy-start(bf16[8,48,768]{2,1,0:T(8,128)(2,1)} %copy-done.19) | copy-start | bytes 1769476
  113.9 36.4 %all-to-all-start.3 = ((bf16[8,192,768]{2,1,0:T(8,128)(2,1)}), bf16[8,192,768]{2,1,0:T(8,128)(2,1)}, u32[]{:S(2)}, u32[]{:S(2)}) async-start(bf16[8,192,768]{2,1,0:T(8,128)(2,1)} %add_convert_fusion), calls=%async_computation.3 | async-start | bytes 4718592 | tf_op jit(solution)/shard_map/all_to_all | solution.py:589
  119.8 5.0 %collective-permute-start.14 = (bf16[128,192]{1,0:T(8,128)(2,1)S(1)}, bf16[128,192]{1,0:T(8,128)(2,1)S(1)}, u32[]{:S(2)}, u32[]{:S(2)}) collective-permute-start(bf16[128,192]{1,0:T(8,128)(2,1)S(1)} %copy-done.23), channel_id=1, source_target_pairs={{0,2},{1,3},{2,0},{3,1},{4,6},{5,7},{6,4},{7,5},{8,10},{9,11},{10,... | collective-permute-start | bytes 147464 | tf_op jit(solution)/shard_map/ppermute | solution.py:585
  120.4 5.8 %collective-permute-start.15 = (bf16[128,192]{1,0:T(8,128)(2,1)S(1)}, bf16[128,192]{1,0:T(8,128)(2,1)S(1)}, u32[]{:S(2)}, u32[]{:S(2)}) collective-permute-start(bf16[128,192]{1,0:T(8,128)(2,1)S(1)} %get-tuple-element.123), channel_id=1, source_target_pairs={{0,4},{1,5},{2,6},{3,7},{4,0},{5,1},{6,2},{7,3},{8,12},{9,13},{10,... | collective-permute-start | bytes 147464 | tf_op jit(solution)/shard_map/ppermute | solution.py:585
  122.2 5.5 %collective-permute-start.16 = (bf16[128,192]{1,0:T(8,128)(2,1)S(1)}, bf16[128,192]{1,0:T(8,128)(2,1)S(1)}, u32[]{:S(2)}, u32[]{:S(2)}) collective-permute-start(bf16[128,192]{1,0:T(8,128)(2,1)S(1)} %get-tuple-element.124), channel_id=1, source_target_pairs={{0,6},{1,7},{2,4},{3,5},{4,2},{5,3},{6,0},{7,1},{8,14},{9,15},{10,... | collective-permute-start | bytes 147464 | tf_op jit(solution)/shard_map/ppermute | solution.py:585
  124.5 20.4 %collective-permute-start.18 = (bf16[8,48,768]{2,1,0:T(8,128)(2,1)S(1)}, bf16[8,48,768]{2,1,0:T(8,128)(2,1)S(1)}, u32[]{:S(2)}, u32[]{:S(2)}) collective-permute-start(bf16[8,48,768]{2,1,0:T(8,128)(2,1)S(1)} %copy-done.20), channel_id=1, source_target_pairs={{0,8},{8,0},{16,24},{24,16},{32,40},{40,32},{48,56},{56,48},{64,72... | collective-permute-start | bytes 1769480 | tf_op jit(solution)/shard_map/ppermute | solution.py:585
  124.7 2.9 %copy-start.33 = (bf16[128,192]{1,0:T(8,128)(2,1)}, bf16[128,192]{1,0:T(8,128)(2,1)S(1)}, u32[]{:S(2)}) copy-start(bf16[128,192]{1,0:T(8,128)(2,1)S(1)} %collective-permute-done.14.refs_1_) | copy-start | bytes 147460
  126.2 1.5 copy-start.34
  144.8 2.3 %collective-permute-start.17 = (bf16[8,48,768]{2,1,0:T(8,128)(2,1)}, bf16[8,48,768]{2,1,0:T(8,128)(2,1)S(1)}, u32[]{:S(2)}, u32[]{:S(2)}) collective-permute-start(bf16[8,48,768]{2,1,0:T(8,128)(2,1)} %get-tuple-element.137), channel_id=1, source_target_pairs={{0,8},{8,0},{16,24},{24,16},{32,40},{40,32},{48,56},{56,48},{64,72... | collective-permute-start | bytes 1769480 | tf_op jit(solution)/shard_map/ppermute | solution.py:585
  147.1 1.1 copy-start.5
  150.3 32.1 %all-to-all-start.2 = ((bf16[8,96,768]{2,1,0:T(8,128)(2,1)}), bf16[8,96,768]{2,1,0:T(8,128)(2,1)S(1)}, u32[]{:S(2)}, u32[]{:S(2)}) async-start(bf16[8,96,768]{2,1,0:T(8,128)(2,1)} %pair.1), calls=%async_computation.2 | async-start | bytes 2359296 | tf_op jit(solution)/shard_map/all_to_all | solution.py:589
  155.0 31.2 %copy-start.28 = (bf16[2,128,768]{2,1,0:T(8,128)(2,1)S(1)}, bf16[2,128,768]{2,1,0:T(8,128)(2,1)}, u32[]{:S(2)}) copy-start(bf16[2,128,768]{2,1,0:T(8,128)(2,1)} %get-tuple-element.129) | copy-start | bytes 1179652
  155.1 12.3 %collective-permute-start.19 = (bf16[2,128,768]{2,1,0:T(8,128)(2,1)}, bf16[2,128,768]{2,1,0:T(8,128)(2,1)S(1)}, u32[]{:S(2)}, u32[]{:S(2)}) collective-permute-start(bf16[2,128,768]{2,1,0:T(8,128)(2,1)} %get-tuple-element.140), channel_id=1, source_target_pairs={{0,2},{1,3},{2,0},{3,1},{4,6},{5,7},{6,4},{7,5},{8,10},{9,11},{10,... | collective-permute-start | bytes 1179656 | tf_op jit(solution)/shard_map/ppermute | solution.py:585
  155.3 23.7 %collective-permute-start.20 = (bf16[2,128,768]{2,1,0:T(8,128)(2,1)}, bf16[2,128,768]{2,1,0:T(8,128)(2,1)S(1)}, u32[]{:S(2)}, u32[]{:S(2)}) collective-permute-start(bf16[2,128,768]{2,1,0:T(8,128)(2,1)} %get-tuple-element.141), channel_id=1, source_target_pairs={{0,4},{1,5},{2,6},{3,7},{4,0},{5,1},{6,2},{7,3},{8,12},{9,13},{10,... | collective-permute-start | bytes 1179656 | tf_op jit(solution)/shard_map/ppermute | solution.py:585
  159.0 23.3 %collective-permute-start.21 = (bf16[2,128,768]{2,1,0:T(8,128)(2,1)}, bf16[2,128,768]{2,1,0:T(8,128)(2,1)S(1)}, u32[]{:S(2)}, u32[]{:S(2)}) collective-permute-start(bf16[2,128,768]{2,1,0:T(8,128)(2,1)} %get-tuple-element.142), channel_id=1, source_target_pairs={{0,6},{1,7},{2,4},{3,5},{4,2},{5,3},{6,0},{7,1},{8,14},{9,15},{10,... | collective-permute-start | bytes 1179656 | tf_op jit(solution)/shard_map/ppermute | solution.py:585
  162.5 19.8 %collective-permute-start.22 = (bf16[48,768]{1,0:T(8,128)(2,1)}, bf16[48,768]{1,0:T(8,128)(2,1)S(1)}, u32[]{:S(2)}, u32[]{:S(2)}) collective-permute-start(bf16[48,768]{1,0:T(8,128)(2,1)} %get-tuple-element.145), channel_id=1, source_target_pairs={{0,1},{1,0},{2,3},{3,2},{4,5},{5,4},{6,7},{7,6},{8,9},{9,8},{10,11... | collective-permute-start | bytes 221192 | tf_op jit(solution)/shard_map/ppermute | solution.py:585
  165.4 17.0 %collective-permute-start.23 = (bf16[48,768]{1,0:T(8,128)(2,1)}, bf16[48,768]{1,0:T(8,128)(2,1)S(1)}, u32[]{:S(2)}, u32[]{:S(2)}) collective-permute-start(bf16[48,768]{1,0:T(8,128)(2,1)} %get-tuple-element.146), channel_id=1, source_target_pairs={{0,4},{1,5},{2,6},{3,7},{4,0},{5,1},{6,2},{7,3},{8,12},{9,13},{10,... | collective-permute-start | bytes 221192 | tf_op jit(solution)/shard_map/ppermute | solution.py:585
  167.3 15.0 %collective-permute-start.24 = (bf16[48,768]{1,0:T(8,128)(2,1)}, bf16[48,768]{1,0:T(8,128)(2,1)S(1)}, u32[]{:S(2)}, u32[]{:S(2)}) collective-permute-start(bf16[48,768]{1,0:T(8,128)(2,1)} %get-tuple-element.147), channel_id=1, source_target_pairs={{0,5},{1,4},{2,7},{3,6},{4,1},{5,0},{6,3},{7,2},{8,13},{9,12},{10,... | collective-permute-start | bytes 221192 | tf_op jit(solution)/shard_map/ppermute | solution.py:585
  182.4 0.9 copy-start.18
  183.5 9.6 %collective-permute-start.26 = (bf16[144,768]{1,0:T(8,128)(2,1)S(1)}, bf16[144,768]{1,0:T(8,128)(2,1)S(1)}, u32[]{:S(2)}, u32[]{:S(2)}) collective-permute-start(bf16[144,768]{1,0:T(8,128)(2,1)S(1)} %last_sum.1.own), channel_id=1, source_target_pairs={{0,1},{1,0},{2,3},{3,2},{4,5},{5,4},{6,7},{7,6},{8,9},{9,8},{10,11... | collective-permute-start | bytes 663560 | tf_op jit(solution)/shard_map/ppermute | solution.py:585
  186.5 10.8 %collective-permute-start.25 = (bf16[128,768]{1,0:T(8,128)(2,1)S(1)}, bf16[128,768]{1,0:T(8,128)(2,1)S(1)}, u32[]{:S(2)}, u32[]{:S(2)}) collective-permute-start(bf16[128,768]{1,0:T(8,128)(2,1)S(1)} %slice_bitcast_fusion), channel_id=1, source_target_pairs={{0,1},{1,0},{2,3},{3,2},{4,5},{5,4},{6,7},{7,6},{8,9},{9,8},{10,11... | collective-permute-start | bytes 589832 | tf_op jit(solution)/shard_map/ppermute | solution.py:585
  193.1 11.6 %collective-permute-start.29 = (bf16[192,768]{1,0:T(8,128)(2,1)S(1)}, bf16[192,768]{1,0:T(8,128)(2,1)S(1)}, u32[]{:S(2)}, u32[]{:S(2)}) collective-permute-start(bf16[192,768]{1,0:T(8,128)(2,1)S(1)} %merge.1.one0), channel_id=1, source_target_pairs={{0,6},{1,7},{2,4},{3,5},{4,2},{5,3},{6,0},{7,1},{8,14},{9,15},{10,... | collective-permute-start | bytes 884744 | tf_op jit(solution)/shard_map/ppermute | solution.py:585
  194.0 10.8 %collective-permute-start.28 = (bf16[192,768]{1,0:T(8,128)(2,1)S(1)}, bf16[192,768]{1,0:T(8,128)(2,1)S(1)}, u32[]{:S(2)}, u32[]{:S(2)}) collective-permute-start(bf16[192,768]{1,0:T(8,128)(2,1)S(1)} %merge.1.one0), channel_id=1, source_target_pairs={{0,4},{1,5},{2,6},{3,7},{4,0},{5,1},{6,2},{7,3},{8,12},{9,13},{10,... | collective-permute-start | bytes 884744 | tf_op jit(solution)/shard_map/ppermute | solution.py:585
  194.0 11.4 %collective-permute-start.27 = (bf16[192,768]{1,0:T(8,128)(2,1)S(1)}, bf16[192,768]{1,0:T(8,128)(2,1)S(1)}, u32[]{:S(2)}, u32[]{:S(2)}) collective-permute-start(bf16[192,768]{1,0:T(8,128)(2,1)S(1)} %merge.1.one0), channel_id=1, source_target_pairs={{0,2},{1,3},{2,0},{3,1},{4,6},{5,7},{6,4},{7,5},{8,10},{9,11},{10,... | collective-permute-start | bytes 884744 | tf_op jit(solution)/shard_map/ppermute | solution.py:585
  (6 other events, 3.7 us)

commit v4 on v3

--- a/solution.py
+++ b/solution.py
@@ -521,33 +521,26 @@
     pair[:, 48:96, :] = (out_keep[...].astype(f32) + out_came[...].astype(f32)).astype(bf16)
 
 
-def feed_sum_kernel(parts, out0, out1, out2, out3, slots, sems):
-    xh, zed, _ = places()
-    member = 2 * lax.div(zed, 2) + xh
-    for m in range(4):
-        total = parts[0, 48 * m : 48 * m + 48, :].astype(f32)
+def feed_sum_kernel(parts, keep, send, slots, sems):
+    high = lax.div(places()[1], 2)
+    for m in range(2):
+        total = parts[0, 96 * m : 96 * m + 96, :].astype(f32)
         for k in range(1, 8):
-            total += parts[k, 48 * m : 48 * m + 48, :].astype(f32)
-        slots[member ^ m] = total.astype(bf16)
-    finish(begin(sems, 0, *((slots.at[k], out) for k, out in enumerate((out0, out1, out2, out3)))))
-
-
-def last_sum_kernel(heads, part0, part1, part2, part3, total):
-    quarter = part0[...].astype(f32)
-    for part in (part1, part2, part3):
-        quarter += part[...].astype(f32)
-    total[0:48, :] = quarter.astype(bf16)
+            total += parts[k, 96 * m : 96 * m + 96, :].astype(f32)
+        slots[high ^ m] = total.astype(bf16)
+    finish(begin(sems, 0, (slots.at[0], keep), (slots.at[1], send)))
+
+
+def last_sum_kernel(heads, keep, came, total):
+    total[0:96, :] = (keep[...].astype(f32) + came[...].astype(f32)).astype(bf16)
     whole = heads[0].astype(f32)
     for k in range(1, 8):
         whole += heads[k].astype(f32)
-    total[48:144, :] = whole.astype(bf16)
+    total[96:192, :] = whole.astype(bf16)
 
 
 def merge_kernel(own, other, merged):
-    xh = places()[0]
-    merged[pl.ds(pl.multiple_of(48 * xh, 16), 48), :] = own[0:48, :]
-    merged[pl.ds(pl.multiple_of(48 * (1 - xh), 16), 48), :] = other[0:48, :]
-    merged[96:192, :] = (own[48:144, :].astype(f32) + other[48:144, :].astype(f32)).astype(bf16)
+    merged[...] = (own[...].astype(f32) + other[...].astype(f32)).astype(bf16)
 
 
 def unpack_kernel(one0, one1, one2, one3, qkv, out, up, down, vectors, bias, every):
@@ -556,10 +549,8 @@
         every[zed ^ k] = one[...]
     ups = []
     for h in range(2):
-        quarters = [every[2 * (m // 2) + h, 48 * (m % 2) : 48 * (m % 2) + 48, :].astype(f32) for m in range(4)]
-        down[96 * h : 96 * h + 48, :] = quarters[0]
-        down[96 * h + 48 : 96 * h + 96, :] = quarters[1]
-        ups.append(quarters[2:])
+        down[96 * h : 96 * h + 96, :] = every[h, 0:96, :].astype(f32)
+        ups.append([every[2 + h, 48 * e : 48 * e + 48, :].astype(f32) for e in range(2)])
     up[...] = jnp.concatenate(
         [ups[h][e][:, 48 * f : 48 * f + 48] for f in range(F) for h in range(2) for e in range(2)], axis=1
     )
@@ -728,20 +719,21 @@
     )
     head_parts = a2a(pair, "fsdp", CHIPS)
 
-    part0, part1, part2, part3 = call(
+    ffn = shape((96, D), bf16)
+    feed_rows, feed_sent = call(
         feed_sum_kernel,
         "feed_sum",
-        (shape((48, D), bf16),) * 4,
+        (ffn, ffn),
         [VM],
-        [pltpu.VMEM((4, 48, D), bf16), dma(4)],
+        [pltpu.VMEM((2, 96, D), bf16), dma(2)],
         mib=56,
         flops=10**6,
         nbytes=3 * 10**6,
-        out_specs=(HB,) * 4,
+        out_specs=(HB, HB),
     )(feed_parts)
-    parts = [part0] + [swap(part, "ctx", NBLK, bit) for part, bit in ((part1, 1), (part2, 4), (part3, 5))]
+    parts = [feed_rows, swap(feed_sent, "ctx", NBLK, 4)]
     head_parts, token_parts, parts = after((head_parts, token_parts, parts))
-    total = call(last_sum_kernel, "last_sum", shape((144, D), bf16), [VM] * 5, flops=10**6, nbytes=2 * 10**6)(
+    total = call(last_sum_kernel, "last_sum", shape((192, D), bf16), [VM] * 3, flops=10**6, nbytes=2 * 10**6)(
         head_parts, *parts
     )
     merged = call(merge_kernel, "merge", shape((192, D), bf16), [VM] * 2, flops=10**6, nbytes=10**6)(

time: 208 us -> 210 us (level)
  waiting for transfers between devices: 76.2 us -> 84.5 us
  starting transfers between devices: 61.3 us -> 54.6 us
    ppermute x30 -> x28, waiting for transfers between devices: 75.5 us -> 83.7 us  [swap(): return lax.ppermute(x, axis, [(i, i ^ bit) for i in range(size)])]
    ppermute x30 -> x28, starting transfers between devices: 39.7 us -> 33 us  [swap(): return lax.ppermute(x, axis, [(i, i ^ bit) for i in range(size)])]
  transfers between devices with their start and end apart: 34 -> 32, of which waited for: 21 -> 21; matrix products, arithmetic and copies ran while one was open for 1% -> 1% of each run, Pallas kernels for 22% -> 22%
where the time goes in v4:
time: 210 us; the launch traced here: 209 us
  waiting for transfers between devices  84.5 us (40%)
  Pallas kernels  55 us (26%)
  starting transfers between devices  54.6 us (26%)
  local copies, waits for them, and re-layouts  11.2 us (5%)
  other arithmetic  3.04 us (1%)
    ppermute x28, waiting for transfers between devices, swap(): return lax.ppermute(x, axis, [(i, i ^ bit) for i in range(size)])  83.7 us
    ppermute x28, starting transfers between devices, swap(): return lax.ppermute(x, axis, [(i, i ^ bit) for i in range(size)])  33 us
    all_to_all x4, starting transfers between devices, a2a(): return lax.all_to_all(x, axis, 0, 0, tiled=True, axis_index_groups=groups)  21.6 us
    pallas_call x1, Pallas kernels, attend_back(): call(attend_back_kernel, 'attend_back', (shape((4 * BLK, WIDE), bf16), sh...  11.3 us
    pallas_call x1, Pallas kernels, attend(): call(attend_kernel, 'attend', (shape((16, D)),) + KEPT + (shape((BLK, WID...  10.5 us
    unnamed x72, local copies, waits for them, and re-layouts  9.32 us
    pallas_call x1, Pallas kernels, head_grad(): call(head_grad_kernel, 'head_grad', (half, half), [HB] * 5 + [VM] * 6, [p...  5.2 us
    pallas_call x1, Pallas kernels, body(): call(first_kernel, 'first', (shape((BLK, D), bf16), shape((BLK, D)), shap...  4.53 us
  transfers between devices with their start and end apart: 32, of which 21 were waited for; matrix products, arithmetic and copies ran while one was open for 1% of the time, Pallas kernels for 22%

profile of v4, /device:TPU:0, one launch (start us, length us, event | category | flops | bytes accessed | tf_op | source)
XLA Modules:
  0.0 209.3 jit_solution(3630823090579312273)
XLA Ops:
  0.6 3.2 %collective-permute-start = (bf16[128,768]{1,0:T(8,128)(2,1)}, bf16[128,768]{1,0:T(8,128)(2,1)S(1)}, u32[]{:S(2)}, u32[]{:S(2)}) collective-permute-start(bf16[128,768]{1,0:T(8,128)(2,1)} %tokens.5), channel_id=1, source_target_pairs={{0,1},{1,0},{2,3},{3,2},{4,5},{5,4},{6,7},{7,6},{8,9},{9,8},{10,11... | collective-permute-start | bytes 589832 | tf_op jit(solution)/shard_map/ppermute | solution.py:576
  3.8 1.2 reshape.24.b_up
  5.1 2.9 %pack_heads.1 = bf16[8,96,768]{2,1,0:T(8,128)(2,1)} custom-call(bf16[8,48]{1,0:T(8,128)(2,1)} %vectors.1, bf16[1,192]{1,0:T(2,128)(2,1)} %reshape.24.b_up, bf16[48,2304]{1,0:T(8,128)(2,1)} %w_qkv.1, bf16[48,768]{1,0:T(8,128)(2,1)} %w_out.1), custom_call_target="tpu_custom_call" | custom-call | flops 1000000 | bytes 2000000 | tf_op jit(solution)/shard_map/pack_heads/pallas_call | solution.py:587
  8.0 1.0 collective-permute-done.other
  8.9 5.6 %all-to-all-start = ((bf16[8,96,768]{2,1,0:T(8,128)(2,1)}), bf16[8,96,768]{2,1,0:T(8,128)(2,1)S(1)}, u32[]{:S(2)}, u32[]{:S(2)}) async-start(bf16[8,96,768]{2,1,0:T(8,128)(2,1)} %pack_heads.1), calls=%async_computation | async-start | bytes 2359296 | tf_op jit(solution)/shard_map/all_to_all | solution.py:580
  14.6 4.1 %collective-permute-start.3 = (bf16[2,128,768]{2,1,0:T(8,128)(2,1)S(1)}, bf16[2,128,768]{2,1,0:T(8,128)(2,1)S(1)}, u32[]{:S(2)}, u32[]{:S(2)}) collective-permute-start(bf16[2,128,768]{2,1,0:T(8,128)(2,1)S(1)} %pad_maximum_fusion), channel_id=1, source_target_pairs={{0,6},{1,7},{2,4},{3,5},{4,2},{5,3},{6,0},{7,1},{8,14},{9,15},{10,... | collective-permute-start | bytes 1179656 | tf_op jit(solution)/shard_map/ppermute | solution.py:576
  18.7 0.9 collective-permute-start.1
  19.7 2.6 %pack_feed.1 = bf16[8,192,768]{2,1,0:T(8,128)(2,1)} custom-call(bf16[48,3072]{1,0:T(8,128)(2,1)} %w_up, bf16[192,768]{1,0:T(8,128)(2,1)} %w_down.1), custom_call_target="tpu_custom_call" | custom-call | flops 1000000 | bytes 4000000 | tf_op jit(solution)/shard_map/pack_feed/pallas_call | solution.py:601
  22.3 12.8 %collective-permute-done.3.pair3 = bf16[2,128,768]{2,1,0:T(8,128)(2,1)S(1)} collective-permute-done((bf16[2,128,768]{2,1,0:T(8,128)(2,1)S(1)}, bf16[2,128,768]{2,1,0:T(8,128)(2,1)S(1)}, u32[]{:S(2)}, u32[]{:S(2)}) %collective-permute-start.3) | collective-permute-done | bytes 393248 | tf_op jit(solution)/shard_map/ppermute | solution.py:576
  35.1 0.7 collective-permute-done.1.pair1
  36.6 5.4 %all-to-all-start.1 = ((bf16[8,192,768]{2,1,0:T(8,128)(2,1)}), bf16[8,192,768]{2,1,0:T(8,128)(2,1)S(1)}, u32[]{:S(2)}, u32[]{:S(2)}) async-start(bf16[8,192,768]{2,1,0:T(8,128)(2,1)} %pack_feed.1), calls=%async_computation.1 | async-start | bytes 4718592 | tf_op jit(solution)/shard_map/all_to_all | solution.py:580
  42.0 2.8 %collective-permute-done.4.w_other = bf16[8,96,768]{2,1,0:T(8,128)(2,1)S(1)} collective-permute-done((bf16[8,96,768]{2,1,0:T(8,128)(2,1)S(1)}, bf16[8,96,768]{2,1,0:T(8,128)(2,1)S(1)}, u32[]{:S(2)}, u32[]{:S(2)}) %collective-permute-start.4) | collective-permute-done | bytes 1179680 | tf_op jit(solution)/shard_map/ppermute | solution.py:576
  44.8 1.1 copy-done.2
  46.0 10.5 %attend.1 = (f32[16,768]{1,0:T(8,128)}, bf16[4,3,128,512]{3,2,1,0:T(8,128)(2,1)}, bf16[3,512,64]{2,1,0:T(8,128)(2,1)}, bf16[3,1024,64]{2,1,0:T(8,128)(2,1)}, bf1...) custom-call(s32[1,3]{1,0:T(1,128)} %lengths.1, ...), custom_call_target="tpu_custom_call" | custom-call | flops 2000000000 | bytes 6000000 | tf_op jit(solution)/shard_map/attend/pallas_call | solution.py:182
  56.5 1.2 collective-permute-start.5
  57.7 3.3 %collective-permute-start.6 = (bf16[128,192]{1,0:T(8,128)(2,1)}, bf16[128,192]{1,0:T(8,128)(2,1)S(1)}, u32[]{:S(2)}, u32[]{:S(2)}) collective-permute-start(bf16[128,192]{1,0:T(8,128)(2,1)} %get-tuple-element.91), channel_id=1, source_target_pairs={{0,4},{1,5},{2,6},{3,7},{4,0},{5,1},{6,2},{7,3},{8,12},{9,13},{10,... | collective-permute-start | bytes 147464 | tf_op jit(solution)/shard_map/ppermute | solution.py:576
  61.3 3.4 %collective-permute-done.6.mix2 = bf16[128,192]{1,0:T(8,128)(2,1)S(1)} collective-permute-done((bf16[128,192]{1,0:T(8,128)(2,1)}, bf16[128,192]{1,0:T(8,128)(2,1)S(1)}, u32[]{:S(2)}, u32[]{:S(2)}) %collective-permute-start.6) | collective-permute-done | bytes 49184 | tf_op jit(solution)/shard_map/ppermute | solution.py:576
  64.7 2.0 collective-permute-done.7.mix3
  67.2 4.5 %first.1 = (bf16[128,768]{1,0:T(8,128)(2,1)}, f32[128,768]{1,0:T(8,128)}, f32[128,896]{1,0:T(8,128)}) custom-call(bf16[128,192]{1,0:T(8,128)(2,1)} %get-tuple-element.89.mix0, bf16[128,192]{1,0:T(8,128)(2,1)} %copy-done.9, bf16[128,192]{1,0:T(8,128)(2,1)} %copy-done.11, bf16[128,192]{1,0:T(8,128)(2,1)} %copy-done.13, bf16[8,96,768]{2,1,0:T(8,128)(2,1)} %copy-done, ...), custom_call_target="tpu_custom_call" | custom-call | flops 150994944 | bytes 4000000 | tf_op jit(solution)/shard_map/first/pallas_call | solution.py:620
  72.0 7.4 %collective-permute-done.8.other.low_other = bf16[128,768]{1,0:T(8,128)(2,1)S(1)} collective-permute-done((bf16[128,768]{1,0:T(8,128)(2,1)}, bf16[128,768]{1,0:T(8,128)(2,1)S(1)}, u32[]{:S(2)}, u32[]{:S(2)}) %collective-permute-start.8) | collective-permute-done | bytes 196640 | tf_op jit(solution)/shard_map/ppermute | solution.py:576
  79.4 0.9 copy-done.15
  80.4 3.0 %feed.1 = (bf16[256,1536]{1,0:T(8,128)(2,1)S(1)}, bf16[256,1536]{1,0:T(8,128)(2,1)S(1)}, f32[128,768]{1,0:T(8,128)S(1)}, bf16[128,768]{1,0:T(8,128)(2,1)S(1)}) custom-call(bf16[128,768]{1,0:T(8,128)(2,1)S(1)} %copy-done.15, bf16[128,768]{1,0:T(8,128)(2,1)S(1)} %collective-permute-done.8.other.low_other, bf16[8,192,768]{2,1,0:T(8,128)(2,1)S(1)} %all-to-all-done.1.w_mine, ...), custom_call_target="tpu_custom_call" | custom-call | flops 1207959552 | bytes 8000000 | tf_op jit(solution)/shard_map/feed/pallas_call | solution.py:641
  83.7 6.2 %collective-permute-done.10.came = bf16[128,768]{1,0:T(8,128)(2,1)S(1)} collective-permute-done((bf16[128,768]{1,0:T(8,128)(2,1)S(1)}, bf16[128,768]{1,0:T(8,128)(2,1)S(1)}, u32[]{:S(2)}, u32[]{:S(2)}) %collective-permute-start.10) | collective-permute-done | bytes 196640 | tf_op jit(solution)/shard_map/ppermute | solution.py:576
  89.9 1.0 second.1
  91.3 5.2 %collective-permute-done.11.other = bf16[128,768]{1,0:T(8,128)(2,1)S(1)} collective-permute-done((bf16[128,768]{1,0:T(8,128)(2,1)S(1)}, bf16[128,768]{1,0:T(8,128)(2,1)S(1)}, u32[]{:S(2)}, u32[]{:S(2)}) %collective-permute-start.11) | collective-permute-done | bytes 196640 | tf_op jit(solution)/shard_map/ppermute | solution.py:576
  96.5 2.5 %feed_back.1 = (bf16[256,1536]{1,0:T(8,128)(2,1)S(1)}, f32[128,768]{1,0:T(8,128)S(1)}, bf16[128,768]{1,0:T(8,128)(2,1)S(1)}, f32[2,768]{1,0:T(2,128)S(1)}) custom-call(bf16[128,768]{1,0:T(8,128)(2,1)S(1)} %get-tuple-element.102.mine, bf16[128,768]{1,0:T(8,128)(2,1)S(1)} %collective-permute-done.11.other, bf16[8,192,768]{2,1,0:T(8,128)(2,1)S(1)} %all-to-all-done.1.w_mine, ...), custom_call_target="tpu_custom_call" | custom-call | flops 1207959552 | bytes 8000000 | tf_op jit(solution)/shard_map/feed_back/pallas_call | solution.py:660
  99.7 0.6 collective-permute-start.12
  100.3 1.8 feed_grad.1
  102.1 3.3 %collective-permute-done.12.came = bf16[128,768]{1,0:T(8,128)(2,1)S(1)} collective-permute-done((bf16[128,768]{1,0:T(8,128)(2,1)S(1)}, bf16[128,768]{1,0:T(8,128)(2,1)S(1)}, u32[]{:S(2)}, u32[]{:S(2)}) %collective-permute-start.12) | collective-permute-done | bytes 196640 | tf_op jit(solution)/shard_map/ppermute | solution.py:576
  105.5 3.7 %first_back.1 = (f32[128,768]{1,0:T(8,128)S(1)}, bf16[8,48,768]{2,1,0:T(8,128)(2,1)S(1)}, bf16[8,48,768]{2,1,0:T(8,128)(2,1)S(1)}, bf16[128,192]{1,0:T(8,128)(2,...) custom-call(f32[128,768]{1,0:T(8,128)S(1)} %get-tuple-element.101.co, ...), custom_call_target="tpu_custom_call" | custom-call | flops 301989888 | bytes 4000000 | tf_op jit(solution)/shard_map/first_back/pallas_call | solution.py:686
  109.3 0.8 copy-done.19
  110.1 0.6 copy-done.21
  111.9 2.0 add_convert_fusion
  113.9 5.8 %all-to-all-start.3 = ((bf16[8,192,768]{2,1,0:T(8,128)(2,1)}), bf16[8,192,768]{2,1,0:T(8,128)(2,1)}, u32[]{:S(2)}, u32[]{:S(2)}) async-start(bf16[8,192,768]{2,1,0:T(8,128)(2,1)} %add_convert_fusion), calls=%async_computation.3 | async-start | bytes 4718592 | tf_op jit(solution)/shard_map/all_to_all | solution.py:580
  119.8 0.6 collective-permute-start.14
  120.4 1.8 collective-permute-start.15
  122.2 2.3 %collective-permute-start.16 = (bf16[128,192]{1,0:T(8,128)(2,1)S(1)}, bf16[128,192]{1,0:T(8,128)(2,1)S(1)}, u32[]{:S(2)}, u32[]{:S(2)}) collective-permute-start(bf16[128,192]{1,0:T(8,128)(2,1)S(1)} %get-tuple-element.120), channel_id=1, source_target_pairs={{0,6},{1,7},{2,4},{3,5},{4,2},{5,3},{6,0},{7,1},{8,14},{9,15},{10,... | collective-permute-start | bytes 147464 | tf_op jit(solution)/shard_map/ppermute | solution.py:576
  124.8 1.4 collective-permute-done.15.refs_2_
  126.2 1.5 collective-permute-done.16.refs_3_
  128.3 11.3 %attend_back.1 = (bf16[512,192]{1,0:T(8,128)(2,1)}, bf16[1024,192]{1,0:T(8,128)(2,1)}, bf16[1024,192]{1,0:T(8,128)(2,1)}, bf16[2,128,768]{2,1,0:T(8,128)(2,1)}, ...) custom-call(s32[1,8]{1,0:T(1,128)} %block_seq.3, ...), custom_call_target="tpu_custom_call" | custom-call | flops 4000000000 | bytes 8000000 | tf_op jit(solution)/shard_map/attend_back/pallas_call | solution.py:254
  139.6 5.2 %head_grad.1 = (bf16[8,48,768]{2,1,0:T(8,128)(2,1)}, bf16[8,48,768]{2,1,0:T(8,128)(2,1)}) custom-call(bf16[128,768]{1,0:T(8,128)(2,1)} %tokens.5, bf16[128,768]{1,0:T(8,128)(2,1)} %copy-done.29, bf16[2,128,768]{2,1,0:T(8,128)(2,1)} %copy-done.32, bf16[2,128,768]{2,1,0:T(8,128)(2,1)} %copy-done.31, bf16[2,128,768]{2,1,0:T(8,128)(2,1)} %copy-done.30, ...), custom_call_target="tpu_custom_call" | custom-call | flops 2000000000 | bytes 4000000 | tf_op jit(solution)/shard_map/head_grad/pallas_call | solution.py:316
  144.9 2.2 %collective-permute-done.17.head_came = bf16[8,48,768]{2,1,0:T(8,128)(2,1)S(1)} collective-permute-done((bf16[8,48,768]{2,1,0:T(8,128)(2,1)}, bf16[8,48,768]{2,1,0:T(8,128)(2,1)S(1)}, u32[]{:S(2)}, u32[]{:S(2)}) %collective-permute-start.17) | collective-permute-done | bytes 589856 | tf_op jit(solution)/shard_map/ppermute | solution.py:576
  147.1 1.1 copy-done.5
  148.2 1.3 pair.1
  149.5 0.8 all-to-all-done.3.parts
  150.3 4.7 %all-to-all-start.2 = ((bf16[8,96,768]{2,1,0:T(8,128)(2,1)}), bf16[8,96,768]{2,1,0:T(8,128)(2,1)S(1)}, u32[]{:S(2)}, u32[]{:S(2)}) async-start(bf16[8,96,768]{2,1,0:T(8,128)(2,1)} %pair.1), calls=%async_computation.2 | async-start | bytes 2359296 | tf_op jit(solution)/shard_map/all_to_all | solution.py:580
  155.3 3.7 %collective-permute-start.20 = (bf16[2,128,768]{2,1,0:T(8,128)(2,1)}, bf16[2,128,768]{2,1,0:T(8,128)(2,1)S(1)}, u32[]{:S(2)}, u32[]{:S(2)}) collective-permute-start(bf16[2,128,768]{2,1,0:T(8,128)(2,1)} %get-tuple-element.137), channel_id=1, source_target_pairs={{0,4},{1,5},{2,6},{3,7},{4,0},{5,1},{6,2},{7,3},{8,12},{9,13},{10,... | collective-permute-start | bytes 1179656 | tf_op jit(solution)/shard_map/ppermute | solution.py:576
  159.0 0.8 collective-permute-start.21
  159.8 2.7 %feed_sum.1 = (bf16[96,768]{1,0:T(8,128)(2,1)}, bf16[96,768]{1,0:T(8,128)(2,1)}) custom-call(bf16[8,192,768]{2,1,0:T(8,128)(2,1)} %all-to-all-done.3.parts), custom_call_target="tpu_custom_call" | custom-call | flops 1000000 | bytes 3000000 | tf_op jit(solution)/shard_map/feed_sum/pallas_call | solution.py:723
  162.5 0.8 collective-permute-start.22
  163.4 4.0 %collective-permute-done.19 = bf16[2,128,768]{2,1,0:T(8,128)(2,1)S(1)} collective-permute-done((bf16[2,128,768]{2,1,0:T(8,128)(2,1)}, bf16[2,128,768]{2,1,0:T(8,128)(2,1)S(1)}, u32[]{:S(2)}, u32[]{:S(2)}) %collective-permute-start.19) | collective-permute-done | bytes 393248 | tf_op jit(solution)/shard_map/ppermute | solution.py:576
  167.3 10.4 %collective-permute-done.20 = bf16[2,128,768]{2,1,0:T(8,128)(2,1)S(1)} collective-permute-done((bf16[2,128,768]{2,1,0:T(8,128)(2,1)}, bf16[2,128,768]{2,1,0:T(8,128)(2,1)S(1)}, u32[]{:S(2)}, u32[]{:S(2)}) %collective-permute-start.20) | collective-permute-done | bytes 393248 | tf_op jit(solution)/shard_map/ppermute | solution.py:576
  177.7 4.6 %collective-permute-done.21 = bf16[2,128,768]{2,1,0:T(8,128)(2,1)S(1)} collective-permute-done((bf16[2,128,768]{2,1,0:T(8,128)(2,1)}, bf16[2,128,768]{2,1,0:T(8,128)(2,1)S(1)}, u32[]{:S(2)}, u32[]{:S(2)}) %collective-permute-start.21) | collective-permute-done | bytes 393248 | tf_op jit(solution)/shard_map/ppermute | solution.py:576
  182.4 0.9 copy-done.18
  183.5 2.8 %collective-permute-start.24 = (bf16[192,768]{1,0:T(8,128)(2,1)S(1)}, bf16[192,768]{1,0:T(8,128)(2,1)S(1)}, u32[]{:S(2)}, u32[]{:S(2)}) collective-permute-start(bf16[192,768]{1,0:T(8,128)(2,1)S(1)} %last_sum.1.own), channel_id=1, source_target_pairs={{0,1},{1,0},{2,3},{3,2},{4,5},{5,4},{6,7},{7,6},{8,9},{9,8},{10,11... | collective-permute-start | bytes 884744 | tf_op jit(solution)/shard_map/ppermute | solution.py:576
  186.5 0.9 collective-permute-start.23
  187.4 7.1 %collective-permute-done.24.other = bf16[192,768]{1,0:T(8,128)(2,1)S(1)} collective-permute-done((bf16[192,768]{1,0:T(8,128)(2,1)S(1)}, bf16[192,768]{1,0:T(8,128)(2,1)S(1)}, u32[]{:S(2)}, u32[]{:S(2)}) %collective-permute-start.24) | collective-permute-done | bytes 294944 | tf_op jit(solution)/shard_map/ppermute | solution.py:576
  194.5 0.9 collective-permute-start.27
  195.4 3.3 %collective-permute-start.25 = (bf16[192,768]{1,0:T(8,128)(2,1)S(1)}, bf16[192,768]{1,0:T(8,128)(2,1)S(1)}, u32[]{:S(2)}, u32[]{:S(2)}) collective-permute-start(bf16[192,768]{1,0:T(8,128)(2,1)S(1)} %merge.1.one0), channel_id=1, source_target_pairs={{0,2},{1,3},{2,0},{3,1},{4,6},{5,7},{6,4},{7,5},{8,10},{9,11},{10,... | collective-permute-start | bytes 884744 | tf_op jit(solution)/shard_map/ppermute | solution.py:576
  198.7 0.8 fusion
  199.5 6.9 %collective-permute-done.27.one3 = bf16[192,768]{1,0:T(8,128)(2,1)S(1)} collective-permute-done((bf16[192,768]{1,0:T(8,128)(2,1)S(1)}, bf16[192,768]{1,0:T(8,128)(2,1)S(1)}, u32[]{:S(2)}, u32[]{:S(2)}) %collective-permute-start.27) | collective-permute-done | bytes 294944 | tf_op jit(solution)/shard_map/ppermute | solution.py:576
  206.4 0.7 collective-permute-done.25.one1
  207.0 1.6 unpack.1
  208.7 0.6 reshape.25
  (95 shorter events, 6.3 us)
Async XLA Ops:
  0.6 13.9 %copy-start.27 = (bf16[128,768]{1,0:T(8,128)(2,1)S(1)}, bf16[128,768]{1,0:T(8,128)(2,1)}, u32[]{:S(2)}) copy-start(bf16[128,768]{1,0:T(8,128)(2,1)} %tokens.5) | copy-start | bytes 589828
  0.6 8.3 %collective-permute-start = (bf16[128,768]{1,0:T(8,128)(2,1)}, bf16[128,768]{1,0:T(8,128)(2,1)S(1)}, u32[]{:S(2)}, u32[]{:S(2)}) collective-permute-start(bf16[128,768]{1,0:T(8,128)(2,1)} %tokens.5), channel_id=1, source_target_pairs={{0,1},{1,0},{2,3},{3,2},{4,5},{5,4},{6,7},{7,6},{8,9},{9,8},{10,11... | collective-permute-start | bytes 589832 | tf_op jit(solution)/shard_map/ppermute | solution.py:576
  8.9 13.4 %copy-start.29 = (bf16[128,768]{1,0:T(8,128)(2,1)}, bf16[128,768]{1,0:T(8,128)(2,1)S(1)}, u32[]{:S(2)}) copy-start(bf16[128,768]{1,0:T(8,128)(2,1)S(1)} %collective-permute-done.other) | copy-start | bytes 589828
  8.9 26.9 %all-to-all-start = ((bf16[8,96,768]{2,1,0:T(8,128)(2,1)}), bf16[8,96,768]{2,1,0:T(8,128)(2,1)S(1)}, u32[]{:S(2)}, u32[]{:S(2)}) async-start(bf16[8,96,768]{2,1,0:T(8,128)(2,1)} %pack_heads.1), calls=%async_computation | async-start | bytes 2359296 | tf_op jit(solution)/shard_map/all_to_all | solution.py:580
  14.6 20.5 %collective-permute-start.3 = (bf16[2,128,768]{2,1,0:T(8,128)(2,1)S(1)}, bf16[2,128,768]{2,1,0:T(8,128)(2,1)S(1)}, u32[]{:S(2)}, u32[]{:S(2)}) collective-permute-start(bf16[2,128,768]{2,1,0:T(8,128)(2,1)S(1)} %pad_maximum_fusion), channel_id=1, source_target_pairs={{0,6},{1,7},{2,4},{3,5},{4,2},{5,3},{6,0},{7,1},{8,14},{9,15},{10,... | collective-permute-start | bytes 1179656 | tf_op jit(solution)/shard_map/ppermute | solution.py:576
  18.7 16.4 %collective-permute-start.2 = (bf16[2,128,768]{2,1,0:T(8,128)(2,1)S(1)}, bf16[2,128,768]{2,1,0:T(8,128)(2,1)S(1)}, u32[]{:S(2)}, u32[]{:S(2)}) collective-permute-start(bf16[2,128,768]{2,1,0:T(8,128)(2,1)S(1)} %pad_maximum_fusion), channel_id=1, source_target_pairs={{0,4},{1,5},{2,6},{3,7},{4,0},{5,1},{6,2},{7,3},{8,12},{9,13},{10,... | collective-permute-start | bytes 1179656 | tf_op jit(solution)/shard_map/ppermute | solution.py:576
  18.7 17.1 %collective-permute-start.1 = (bf16[2,128,768]{2,1,0:T(8,128)(2,1)S(1)}, bf16[2,128,768]{2,1,0:T(8,128)(2,1)S(1)}, u32[]{:S(2)}, u32[]{:S(2)}) collective-permute-start(bf16[2,128,768]{2,1,0:T(8,128)(2,1)S(1)} %pad_maximum_fusion), channel_id=1, source_target_pairs={{0,2},{1,3},{2,0},{3,1},{4,6},{5,7},{6,4},{7,5},{8,10},{9,11},{10,... | collective-permute-start | bytes 1179656 | tf_op jit(solution)/shard_map/ppermute | solution.py:576
  35.1 0.8 copy-start.30
  35.1 0.9 copy-start.31
  35.8 0.7 copy-start.32
  35.8 9.0 %copy-start = (bf16[8,96,768]{2,1,0:T(8,128)(2,1)}, bf16[8,96,768]{2,1,0:T(8,128)(2,1)S(1)}, u32[]{:S(2)}) copy-start(bf16[8,96,768]{2,1,0:T(8,128)(2,1)S(1)} %all-to-all-done.w_mine) | copy-start | bytes 3538948
  36.6 35.2 %all-to-all-start.1 = ((bf16[8,192,768]{2,1,0:T(8,128)(2,1)}), bf16[8,192,768]{2,1,0:T(8,128)(2,1)S(1)}, u32[]{:S(2)}, u32[]{:S(2)}) async-start(bf16[8,192,768]{2,1,0:T(8,128)(2,1)} %pack_feed.1), calls=%async_computation.1 | async-start | bytes 4718592 | tf_op jit(solution)/shard_map/all_to_all | solution.py:580
  42.0 2.8 %collective-permute-start.4 = (bf16[8,96,768]{2,1,0:T(8,128)(2,1)S(1)}, bf16[8,96,768]{2,1,0:T(8,128)(2,1)S(1)}, u32[]{:S(2)}, u32[]{:S(2)}) collective-permute-start(bf16[8,96,768]{2,1,0:T(8,128)(2,1)S(1)} %all-to-all-done.w_mine), channel_id=1, source_target_pairs={{0,8},{8,0},{16,24},{24,16},{32,40},{40,32},{48,56},{56,48},{64,72... | collective-permute-start | bytes 3538952 | tf_op jit(solution)/shard_map/ppermute | solution.py:576
  44.8 1.1 copy-start.2
  56.5 22.9 %copy-start.4 = (f32[16,768]{1,0:T(8,128)S(1)}, f32[16,768]{1,0:T(8,128)}, u32[]{:S(2)}) copy-start(f32[16,768]{1,0:T(8,128)} %get-tuple-element.93.vectors) | copy-start | bytes 147460
  56.5 4.8 %collective-permute-start.5 = (bf16[128,192]{1,0:T(8,128)(2,1)}, bf16[128,192]{1,0:T(8,128)(2,1)S(1)}, u32[]{:S(2)}, u32[]{:S(2)}) collective-permute-start(bf16[128,192]{1,0:T(8,128)(2,1)} %get-tuple-element.90), channel_id=1, source_target_pairs={{0,2},{1,3},{2,0},{3,1},{4,6},{5,7},{6,4},{7,5},{8,10},{9,11},{10,... | collective-permute-start | bytes 147464 | tf_op jit(solution)/shard_map/ppermute | solution.py:576
  57.7 7.0 %collective-permute-start.6 = (bf16[128,192]{1,0:T(8,128)(2,1)}, bf16[128,192]{1,0:T(8,128)(2,1)S(1)}, u32[]{:S(2)}, u32[]{:S(2)}) collective-permute-start(bf16[128,192]{1,0:T(8,128)(2,1)} %get-tuple-element.91), channel_id=1, source_target_pairs={{0,4},{1,5},{2,6},{3,7},{4,0},{5,1},{6,2},{7,3},{8,12},{9,13},{10,... | collective-permute-start | bytes 147464 | tf_op jit(solution)/shard_map/ppermute | solution.py:576
  60.9 5.7 %collective-permute-start.7 = (bf16[128,192]{1,0:T(8,128)(2,1)}, bf16[128,192]{1,0:T(8,128)(2,1)S(1)}, u32[]{:S(2)}, u32[]{:S(2)}) collective-permute-start(bf16[128,192]{1,0:T(8,128)(2,1)} %get-tuple-element.92), channel_id=1, source_target_pairs={{0,6},{1,7},{2,4},{3,5},{4,2},{5,3},{6,0},{7,1},{8,14},{9,15},{10,... | collective-permute-start | bytes 147464 | tf_op jit(solution)/shard_map/ppermute | solution.py:576
  61.3 5.3 %copy-start.9 = (bf16[128,192]{1,0:T(8,128)(2,1)}, bf16[128,192]{1,0:T(8,128)(2,1)S(1)}, u32[]{:S(2)}) copy-start(bf16[128,192]{1,0:T(8,128)(2,1)S(1)} %collective-permute-done.5.mix1) | copy-start | bytes 147460
  64.7 2.0 copy-start.11
  71.8 7.6 %collective-permute-start.9 = (bf16[8,192,768]{2,1,0:T(8,128)(2,1)S(1)}, bf16[8,192,768]{2,1,0:T(8,128)(2,1)S(1)}, u32[]{:S(2)}, u32[]{:S(2)}) collective-permute-start(bf16[8,192,768]{2,1,0:T(8,128)(2,1)S(1)} %all-to-all-done.1.w_mine), channel_id=1, source_target_pairs={{0,8},{8,0},{16,24},{24,16},{32,40},{40,32},{48,56},{56,48},{64,72... | collective-permute-start | bytes 7077896 | tf_op jit(solution)/shard_map/ppermute | solution.py:576
  71.9 18.0 %copy-start.7 = (f32[128,768]{1,0:T(8,128)S(1)}, f32[128,768]{1,0:T(8,128)}, u32[]{:S(2)}) copy-start(f32[128,768]{1,0:T(8,128)} %get-tuple-element.95.norm) | copy-start | bytes 1179652
  71.9 7.5 %collective-permute-start.8 = (bf16[128,768]{1,0:T(8,128)(2,1)}, bf16[128,768]{1,0:T(8,128)(2,1)S(1)}, u32[]{:S(2)}, u32[]{:S(2)}) collective-permute-start(bf16[128,768]{1,0:T(8,128)(2,1)} %get-tuple-element.96.mine.low_mine), channel_id=1, source_target_pairs={{0,2},{1,3},{2,0},{3,1},{4,6},{5,7},{6,4},{7,5},{8,10},{9,11},{10,... | collective-permute-start | bytes 589832 | tf_op jit(solution)/shard_map/ppermute | solution.py:576
  79.4 0.9 copy-start.15
  80.4 9.5 %copy-start.17 = (bf16[128,768]{1,0:T(8,128)(2,1)S(1)}, bf16[128,768]{1,0:T(8,128)(2,1)}, u32[]{:S(2)}) copy-start(bf16[128,768]{1,0:T(8,128)(2,1)} %out_grad.1) | copy-start | bytes 589828
  83.3 6.5 %collective-permute-start.10 = (bf16[128,768]{1,0:T(8,128)(2,1)S(1)}, bf16[128,768]{1,0:T(8,128)(2,1)S(1)}, u32[]{:S(2)}, u32[]{:S(2)}) collective-permute-start(bf16[128,768]{1,0:T(8,128)(2,1)S(1)} %get-tuple-element.99), channel_id=1, source_target_pairs={{0,2},{1,3},{2,0},{3,1},{4,6},{5,7},{6,4},{7,5},{8,10},{9,11},{10,... | collective-permute-start | bytes 589832 | tf_op jit(solution)/shard_map/ppermute | solution.py:576
  90.8 8.2 %copy-start.24 = (f32[3,768]{1,0:T(4,128)}, f32[3,768]{1,0:T(4,128)S(1)}, u32[]{:S(2)}) copy-start(f32[3,768]{1,0:T(4,128)S(1)} %get-tuple-element.130.second_sums) | copy-start | bytes 27652
  90.8 5.7 %collective-permute-start.11 = (bf16[128,768]{1,0:T(8,128)(2,1)S(1)}, bf16[128,768]{1,0:T(8,128)(2,1)S(1)}, u32[]{:S(2)}, u32[]{:S(2)}) collective-permute-start(bf16[128,768]{1,0:T(8,128)(2,1)S(1)} %get-tuple-element.102.mine), channel_id=1, source_target_pairs={{0,2},{1,3},{2,0},{3,1},{4,6},{5,7},{6,4},{7,5},{8,10},{9,11},{10,... | collective-permute-start | bytes 589832 | tf_op jit(solution)/shard_map/ppermute | solution.py:576
  96.5 3.8 %copy-start.16 = (bf16[128,768]{1,0:T(8,128)(2,1)S(1)}, bf16[128,768]{1,0:T(8,128)(2,1)}, u32[]{:S(2)}) copy-start(bf16[128,768]{1,0:T(8,128)(2,1)} %get-tuple-element.96.mine.low_mine) | copy-start | bytes 589828
  99.7 5.8 %copy-start.1 = (bf16[8,96,768]{2,1,0:T(8,128)(2,1)S(1)}, bf16[8,96,768]{2,1,0:T(8,128)(2,1)}, u32[]{:S(2)}) copy-start(bf16[8,96,768]{2,1,0:T(8,128)(2,1)} %copy-done) | copy-start | bytes 3538948
  99.7 5.8 %copy-start.3 = (bf16[8,96,768]{2,1,0:T(8,128)(2,1)S(1)}, bf16[8,96,768]{2,1,0:T(8,128)(2,1)}, u32[]{:S(2)}) copy-start(bf16[8,96,768]{2,1,0:T(8,128)(2,1)} %copy-done.2) | copy-start | bytes 3538948
  99.7 5.8 %copy-start.6 = (f32[128,896]{1,0:T(8,128)S(1)}, f32[128,896]{1,0:T(8,128)}, u32[]{:S(2)}) copy-start(f32[128,896]{1,0:T(8,128)} %get-tuple-element.110.hat) | copy-start | bytes 1376260
  99.7 5.8 %copy-start.8 = (bf16[128,192]{1,0:T(8,128)(2,1)S(1)}, bf16[128,192]{1,0:T(8,128)(2,1)}, u32[]{:S(2)}) copy-start(bf16[128,192]{1,0:T(8,128)(2,1)} %get-tuple-element.89.mix0) | copy-start | bytes 147460
  99.7 5.8 %copy-start.10 = (bf16[128,192]{1,0:T(8,128)(2,1)S(1)}, bf16[128,192]{1,0:T(8,128)(2,1)}, u32[]{:S(2)}) copy-start(bf16[128,192]{1,0:T(8,128)(2,1)} %copy-done.9) | copy-start | bytes 147460
  99.7 5.8 %copy-start.12 = (bf16[128,192]{1,0:T(8,128)(2,1)S(1)}, bf16[128,192]{1,0:T(8,128)(2,1)}, u32[]{:S(2)}) copy-start(bf16[128,192]{1,0:T(8,128)(2,1)} %copy-done.11) | copy-start | bytes 147460
  99.7 5.8 %copy-start.14 = (bf16[128,192]{1,0:T(8,128)(2,1)S(1)}, bf16[128,192]{1,0:T(8,128)(2,1)}, u32[]{:S(2)}) copy-start(bf16[128,192]{1,0:T(8,128)(2,1)} %copy-done.13) | copy-start | bytes 147460
  99.7 5.8 %collective-permute-start.12 = (bf16[128,768]{1,0:T(8,128)(2,1)S(1)}, bf16[128,768]{1,0:T(8,128)(2,1)S(1)}, u32[]{:S(2)}, u32[]{:S(2)}) collective-permute-start(bf16[128,768]{1,0:T(8,128)(2,1)S(1)} %get-tuple-element.108), channel_id=1, source_target_pairs={{0,2},{1,3},{2,0},{3,1},{4,6},{5,7},{6,4},{7,5},{8,10},{9,11},{10,... | collective-permute-start | bytes 589832 | tf_op jit(solution)/shard_map/ppermute | solution.py:576
  105.5 6.5 %collective-permute-start.13 = (bf16[8,192,768]{2,1,0:T(8,128)(2,1)S(1)}, bf16[8,192,768]{2,1,0:T(8,128)(2,1)S(1)}, u32[]{:S(2)}, u32[]{:S(2)}) collective-permute-start(bf16[8,192,768]{2,1,0:T(8,128)(2,1)S(1)} %get-tuple-element.114), channel_id=1, source_target_pairs={{0,8},{8,0},{16,24},{24,16},{32,40},{40,32},{48,56},{56,48},{64,72... | collective-permute-start | bytes 7077896 | tf_op jit(solution)/shard_map/ppermute | solution.py:576
  109.3 0.8 copy-start.19
  110.1 0.6 copy-start.21
  113.9 5.8 %copy-start.23 = (bf16[128,192]{1,0:T(8,128)(2,1)S(1)}, bf16[128,192]{1,0:T(8,128)(2,1)}, u32[]{:S(2)}) copy-start(bf16[128,192]{1,0:T(8,128)(2,1)} %copy-done.22) | copy-start | bytes 147460
  113.9 10.6 %copy-start.20 = (bf16[8,48,768]{2,1,0:T(8,128)(2,1)S(1)}, bf16[8,48,768]{2,1,0:T(8,128)(2,1)}, u32[]{:S(2)}) copy-start(bf16[8,48,768]{2,1,0:T(8,128)(2,1)} %copy-done.19) | copy-start | bytes 1769476
  113.9 36.4 %all-to-all-start.3 = ((bf16[8,192,768]{2,1,0:T(8,128)(2,1)}), bf16[8,192,768]{2,1,0:T(8,128)(2,1)}, u32[]{:S(2)}, u32[]{:S(2)}) async-start(bf16[8,192,768]{2,1,0:T(8,128)(2,1)} %add_convert_fusion), calls=%async_computation.3 | async-start | bytes 4718592 | tf_op jit(solution)/shard_map/all_to_all | solution.py:580
  119.8 5.0 %collective-permute-start.14 = (bf16[128,192]{1,0:T(8,128)(2,1)S(1)}, bf16[128,192]{1,0:T(8,128)(2,1)S(1)}, u32[]{:S(2)}, u32[]{:S(2)}) collective-permute-start(bf16[128,192]{1,0:T(8,128)(2,1)S(1)} %copy-done.23), channel_id=1, source_target_pairs={{0,2},{1,3},{2,0},{3,1},{4,6},{5,7},{6,4},{7,5},{8,10},{9,11},{10,... | collective-permute-start | bytes 147464 | tf_op jit(solution)/shard_map/ppermute | solution.py:576
  120.4 5.8 %collective-permute-start.15 = (bf16[128,192]{1,0:T(8,128)(2,1)S(1)}, bf16[128,192]{1,0:T(8,128)(2,1)S(1)}, u32[]{:S(2)}, u32[]{:S(2)}) collective-permute-start(bf16[128,192]{1,0:T(8,128)(2,1)S(1)} %get-tuple-element.119), channel_id=1, source_target_pairs={{0,4},{1,5},{2,6},{3,7},{4,0},{5,1},{6,2},{7,3},{8,12},{9,13},{10,... | collective-permute-start | bytes 147464 | tf_op jit(solution)/shard_map/ppermute | solution.py:576
  122.2 5.5 %collective-permute-start.16 = (bf16[128,192]{1,0:T(8,128)(2,1)S(1)}, bf16[128,192]{1,0:T(8,128)(2,1)S(1)}, u32[]{:S(2)}, u32[]{:S(2)}) collective-permute-start(bf16[128,192]{1,0:T(8,128)(2,1)S(1)} %get-tuple-element.120), channel_id=1, source_target_pairs={{0,6},{1,7},{2,4},{3,5},{4,2},{5,3},{6,0},{7,1},{8,14},{9,15},{10,... | collective-permute-start | bytes 147464 | tf_op jit(solution)/shard_map/ppermute | solution.py:576
  124.5 20.4 %collective-permute-start.18 = (bf16[8,48,768]{2,1,0:T(8,128)(2,1)S(1)}, bf16[8,48,768]{2,1,0:T(8,128)(2,1)S(1)}, u32[]{:S(2)}, u32[]{:S(2)}) collective-permute-start(bf16[8,48,768]{2,1,0:T(8,128)(2,1)S(1)} %copy-done.20), channel_id=1, source_target_pairs={{0,8},{8,0},{16,24},{24,16},{32,40},{40,32},{48,56},{56,48},{64,72... | collective-permute-start | bytes 1769480 | tf_op jit(solution)/shard_map/ppermute | solution.py:576
  124.8 2.9 %copy-start.33 = (bf16[128,192]{1,0:T(8,128)(2,1)}, bf16[128,192]{1,0:T(8,128)(2,1)S(1)}, u32[]{:S(2)}) copy-start(bf16[128,192]{1,0:T(8,128)(2,1)S(1)} %collective-permute-done.14.refs_1_) | copy-start | bytes 147460
  126.2 1.5 copy-start.34
  127.7 0.6 copy-start.35
  144.8 2.3 %collective-permute-start.17 = (bf16[8,48,768]{2,1,0:T(8,128)(2,1)}, bf16[8,48,768]{2,1,0:T(8,128)(2,1)S(1)}, u32[]{:S(2)}, u32[]{:S(2)}) collective-permute-start(bf16[8,48,768]{2,1,0:T(8,128)(2,1)} %get-tuple-element.133), channel_id=1, source_target_pairs={{0,8},{8,0},{16,24},{24,16},{32,40},{40,32},{48,56},{56,48},{64,72... | collective-permute-start | bytes 1769480 | tf_op jit(solution)/shard_map/ppermute | solution.py:576
  147.1 1.1 copy-start.5
  150.3 32.0 %all-to-all-start.2 = ((bf16[8,96,768]{2,1,0:T(8,128)(2,1)}), bf16[8,96,768]{2,1,0:T(8,128)(2,1)S(1)}, u32[]{:S(2)}, u32[]{:S(2)}) async-start(bf16[8,96,768]{2,1,0:T(8,128)(2,1)} %pair.1), calls=%async_computation.2 | async-start | bytes 2359296 | tf_op jit(solution)/shard_map/all_to_all | solution.py:580
  155.0 31.2 %copy-start.28 = (bf16[2,128,768]{2,1,0:T(8,128)(2,1)S(1)}, bf16[2,128,768]{2,1,0:T(8,128)(2,1)}, u32[]{:S(2)}) copy-start(bf16[2,128,768]{2,1,0:T(8,128)(2,1)} %get-tuple-element.125) | copy-start | bytes 1179652
  155.0 12.3 %collective-permute-start.19 = (bf16[2,128,768]{2,1,0:T(8,128)(2,1)}, bf16[2,128,768]{2,1,0:T(8,128)(2,1)S(1)}, u32[]{:S(2)}, u32[]{:S(2)}) collective-permute-start(bf16[2,128,768]{2,1,0:T(8,128)(2,1)} %get-tuple-element.136), channel_id=1, source_target_pairs={{0,2},{1,3},{2,0},{3,1},{4,6},{5,7},{6,4},{7,5},{8,10},{9,11},{10,... | collective-permute-start | bytes 1179656 | tf_op jit(solution)/shard_map/ppermute | solution.py:576
  155.3 22.5 %collective-permute-start.20 = (bf16[2,128,768]{2,1,0:T(8,128)(2,1)}, bf16[2,128,768]{2,1,0:T(8,128)(2,1)S(1)}, u32[]{:S(2)}, u32[]{:S(2)}) collective-permute-start(bf16[2,128,768]{2,1,0:T(8,128)(2,1)} %get-tuple-element.137), channel_id=1, source_target_pairs={{0,4},{1,5},{2,6},{3,7},{4,0},{5,1},{6,2},{7,3},{8,12},{9,13},{10,... | collective-permute-start | bytes 1179656 | tf_op jit(solution)/shard_map/ppermute | solution.py:576
  159.0 23.3 %collective-permute-start.21 = (bf16[2,128,768]{2,1,0:T(8,128)(2,1)}, bf16[2,128,768]{2,1,0:T(8,128)(2,1)S(1)}, u32[]{:S(2)}, u32[]{:S(2)}) collective-permute-start(bf16[2,128,768]{2,1,0:T(8,128)(2,1)} %get-tuple-element.138), channel_id=1, source_target_pairs={{0,6},{1,7},{2,4},{3,5},{4,2},{5,3},{6,0},{7,1},{8,14},{9,15},{10,... | collective-permute-start | bytes 1179656 | tf_op jit(solution)/shard_map/ppermute | solution.py:576
  162.5 19.8 %collective-permute-start.22 = (bf16[96,768]{1,0:T(8,128)(2,1)}, bf16[96,768]{1,0:T(8,128)(2,1)S(1)}, u32[]{:S(2)}, u32[]{:S(2)}) collective-permute-start(bf16[96,768]{1,0:T(8,128)(2,1)} %get-tuple-element.141), channel_id=1, source_target_pairs={{0,4},{1,5},{2,6},{3,7},{4,0},{5,1},{6,2},{7,3},{8,12},{9,13},{10,... | collective-permute-start | bytes 442376 | tf_op jit(solution)/shard_map/ppermute | solution.py:576
  182.4 0.9 copy-start.18
  183.5 11.0 %collective-permute-start.24 = (bf16[192,768]{1,0:T(8,128)(2,1)S(1)}, bf16[192,768]{1,0:T(8,128)(2,1)S(1)}, u32[]{:S(2)}, u32[]{:S(2)}) collective-permute-start(bf16[192,768]{1,0:T(8,128)(2,1)S(1)} %last_sum.1.own), channel_id=1, source_target_pairs={{0,1},{1,0},{2,3},{3,2},{4,5},{5,4},{6,7},{7,6},{8,9},{9,8},{10,11... | collective-permute-start | bytes 884744 | tf_op jit(solution)/shard_map/ppermute | solution.py:576
  186.5 12.2 %collective-permute-start.23 = (bf16[128,768]{1,0:T(8,128)(2,1)S(1)}, bf16[128,768]{1,0:T(8,128)(2,1)S(1)}, u32[]{:S(2)}, u32[]{:S(2)}) collective-permute-start(bf16[128,768]{1,0:T(8,128)(2,1)S(1)} %slice_bitcast_fusion), channel_id=1, source_target_pairs={{0,1},{1,0},{2,3},{3,2},{4,5},{5,4},{6,7},{7,6},{8,9},{9,8},{10,11... | collective-permute-start | bytes 589832 | tf_op jit(solution)/shard_map/ppermute | solution.py:576
  194.5 11.9 %collective-permute-start.27 = (bf16[192,768]{1,0:T(8,128)(2,1)S(1)}, bf16[192,768]{1,0:T(8,128)(2,1)S(1)}, u32[]{:S(2)}, u32[]{:S(2)}) collective-permute-start(bf16[192,768]{1,0:T(8,128)(2,1)S(1)} %merge.1.one0), channel_id=1, source_target_pairs={{0,6},{1,7},{2,4},{3,5},{4,2},{5,3},{6,0},{7,1},{8,14},{9,15},{10,... | collective-permute-start | bytes 884744 | tf_op jit(solution)/shard_map/ppermute | solution.py:576
  195.4 11.0 %collective-permute-start.26 = (bf16[192,768]{1,0:T(8,128)(2,1)S(1)}, bf16[192,768]{1,0:T(8,128)(2,1)S(1)}, u32[]{:S(2)}, u32[]{:S(2)}) collective-permute-start(bf16[192,768]{1,0:T(8,128)(2,1)S(1)} %merge.1.one0), channel_id=1, source_target_pairs={{0,4},{1,5},{2,6},{3,7},{4,0},{5,1},{6,2},{7,3},{8,12},{9,13},{10,... | collective-permute-start | bytes 884744 | tf_op jit(solution)/shard_map/ppermute | solution.py:576
  195.4 11.7 %collective-permute-start.25 = (bf16[192,768]{1,0:T(8,128)(2,1)S(1)}, bf16[192,768]{1,0:T(8,128)(2,1)S(1)}, u32[]{:S(2)}, u32[]{:S(2)}) collective-permute-start(bf16[192,768]{1,0:T(8,128)(2,1)S(1)} %merge.1.one0), channel_id=1, source_target_pairs={{0,2},{1,3},{2,0},{3,1},{4,6},{5,7},{6,4},{7,5},{8,10},{9,11},{10,... | collective-permute-start | bytes 884744 | tf_op jit(solution)/shard_map/ppermute | solution.py:576
  (4 other events, 2.4 us)
